TPU v7x, 32 devices: a whole 2x2x4 slice. The times are simulated.
32 devices in a mesh: lat: 8 (over y, x, core), lon: 4 (over z).
Axes of the slice: x: 2, y: 2, z: 4, core: 2. Of those that a mesh axis runs over, the one named last changes fastest.
Arguments:
- query_field: bfloat16 [64, 64, 512], P('lat', 'lon'), may hold values from -6 to 6
- key_field: bfloat16 [64, 64, 512], P('lat', 'lon'), may hold values from -6 to 6
- value_field: bfloat16 [64, 64, 512], P('lat', 'lon'), may hold values from -6 to 6
- out_grad: bfloat16 [64, 64, 512], P('lat', 'lon'), may hold values from -24 to 24
- pole_reach: int32 [2, 64], replicated, may hold values from 0 to 6
Outputs:
- query_grad: bfloat16 [64, 64, 512], P('lat', 'lon')
- key_grad: bfloat16 [64, 64, 512], P('lat', 'lon')
- value_grad: bfloat16 [64, 64, 512], P('lat', 'lon')
All inputs are finite; a program needn't handle non-finite values.
Results may differ from a plain program's by a relative error of at most 0.012.
The roundings to bfloat16 on the way count: a program that leaves them out, or rounds other values in their place, can miss the bound.
Values may be sent and summed in bfloat16 or wider, within the bound.
No kernel may reach another device: no remote copies, remote signals or barrier semaphores. Data moves between devices by JAX's collectives and lax.ppermute only.
A program may use at most 64 MiB of HBM per device.

v0:
```python
import math

import jax
import jax.numpy as jnp
from jax import lax
from jax.sharding import PartitionSpec as P

HEAD_DIM = 32
RADIUS = 6


def with_halo(block, sides, width):
    for axis, dim in sides:
        count = lax.axis_size(axis)
        forward = [(i, i + 1) for i in range(count - 1)]
        forward.append((count - 1, 0))
        backward = [(target, source) for source, target in forward]
        low = lax.ppermute(
            lax.slice_in_dim(block, block.shape[dim] - width, None, axis=dim), axis, forward
        )
        high = lax.ppermute(lax.slice_in_dim(block, 0, width, axis=dim), axis, backward)
        block = jnp.concatenate([low, block, high], axis=dim)
    return block


def for_sending(array):

    def short(part):
        return part.astype(jnp.bfloat16) if part.dtype == jnp.float32 else part

    return jax.tree.map(short, array)


def swapped(block, axis, apart):
    count = lax.axis_size(axis)
    route = []
    for low in range(count):
        high = low | 1 << apart
        if high != low and high < count:
            route += [(low, high), (high, low)]
    return lax.ppermute(block, axis, route)


def lookup_row(table_row, positions, extent):
    match = positions[:, None] == jnp.arange(extent, dtype=jnp.int32)[None, :]
    return jnp.sum(jnp.where(match, table_row[None, :], 0), axis=1)


def neighbour_mask(
    pole_reach, lat_index, lon_index, block_rows, block_cols, total_rows, total_cols
):
    local_rows = jnp.arange(block_rows, dtype=jnp.int32)
    local_cols = jnp.arange(block_cols, dtype=jnp.int32)
    outer_rows = jnp.arange(block_rows + 2 * RADIUS, dtype=jnp.int32)
    outer_cols = jnp.arange(block_cols + 2 * RADIUS, dtype=jnp.int32)
    global_rows = lat_index * block_rows + local_rows
    global_cols = lon_index * block_cols + local_cols
    padded_rows = lat_index * block_rows + outer_rows
    key_cols = jnp.remainder(
        lon_index * block_cols + outer_cols - RADIUS + total_cols // 2, total_cols
    )
    north_band = padded_rows < RADIUS
    south_band = padded_rows >= total_rows + RADIUS
    north_depth = RADIUS - 1 - padded_rows
    south_depth = padded_rows - total_rows - RADIUS
    north_key = lookup_row(pole_reach[0], key_cols, total_cols)
    south_key = lookup_row(pole_reach[1], key_cols, total_cols)
    key_valid = jnp.where(
        north_band[:, None],
        north_key[None, :] > north_depth[:, None],
        jnp.where(south_band[:, None], south_key[None, :] > south_depth[:, None], True),
    )
    north_query = lookup_row(pole_reach[0], global_cols, total_cols)[None, :] > global_rows[:, None]
    south_query = (
        lookup_row(pole_reach[1], global_cols, total_cols)[None, :]
        > (total_rows - 1 - global_rows)[:, None]
    )
    row_near = (outer_rows[None, :] >= local_rows[:, None]) & (
        outer_rows[None, :] <= local_rows[:, None] + 2 * RADIUS
    )
    col_near = (outer_cols[None, :] >= local_cols[:, None]) & (
        outer_cols[None, :] <= local_cols[:, None] + 2 * RADIUS
    )
    allowed = row_near[:, None, :, None] & col_near[None, :, None, :] & key_valid[None, None, :, :]
    allowed = allowed & (
        jnp.logical_not(north_band)[None, None, :, None] | north_query[:, :, None, None]
    )
    allowed = allowed & (
        jnp.logical_not(south_band)[None, None, :, None] | south_query[:, :, None, None]
    )
    return allowed.reshape(block_rows * block_cols, -1)


def single_slab(padded, block_rows, is_north):
    return jnp.where(
        is_north, padded[RADIUS : 2 * RADIUS], padded[block_rows : block_rows + RADIUS]
    )


def splice(padded, north_part, south_part, block_rows, is_north, is_south):
    northern = jnp.concatenate([jnp.flip(north_part, axis=0), padded[RADIUS:]], axis=0)
    padded = jnp.where(is_north, northern, padded)
    southern = jnp.concatenate(
        [padded[: block_rows + RADIUS], jnp.flip(south_part, axis=0)], axis=0
    )
    return jnp.where(is_south, southern, padded)


def heads_last_cells(field, group_count, group_size):
    cell_count = field.shape[0]
    return field.reshape(cell_count, group_count, group_size, HEAD_DIM).transpose(1, 2, 3, 0)


def cells_first(stacked, cell_count):
    return stacked.reshape(-1, cell_count).T


def query_block(query_rows, key_rows, value_rows, grad_rows, allowed, head_count):
    scale = 1.0 / math.sqrt(HEAD_DIM)
    group_size = math.gcd(head_count, 4)
    group_count = head_count // group_size

    def query_one_group(pieces):
        query_part, key_part, value_part, grad_part = pieces
        scores = (
            jnp.einsum("hdq,hdk->hqk", query_part, key_part, preferred_element_type=jnp.float32)
            * scale
        )
        masked = jnp.where(allowed[None], scores, -1e30)
        row_max = jnp.max(masked, axis=2, keepdims=True)
        row_total = jnp.sum(
            jnp.where(allowed[None], jnp.exp(masked - row_max), 0.0), axis=2, keepdims=True
        )
        log_total = row_max + jnp.log(row_total)
        probs = jnp.where(allowed[None], jnp.exp(scores - log_total), 0.0)
        probs_half = probs.astype(jnp.bfloat16)
        attended = jnp.einsum(
            "hqk,hdk->hdq", probs_half, value_part, preferred_element_type=jnp.float32
        )
        grad_dot = jnp.sum(grad_part.astype(jnp.float32) * attended, axis=1)
        grad_probs = jnp.einsum(
            "hdq,hdk->hqk", grad_part, value_part, preferred_element_type=jnp.float32
        )
        grad_scores = (probs * (grad_probs - grad_dot[:, :, None])).astype(jnp.bfloat16)
        query_grad = (
            jnp.einsum("hqk,hdk->hdq", grad_scores, key_part, preferred_element_type=jnp.float32)
            * scale
        )
        return (log_total[:, :, 0], grad_dot, query_grad.astype(jnp.bfloat16))

    log_groups, dot_groups, grad_groups = lax.map(
        query_one_group,
        (
            heads_last_cells(query_rows, group_count, group_size),
            heads_last_cells(key_rows, group_count, group_size),
            heads_last_cells(value_rows, group_count, group_size),
            heads_last_cells(grad_rows, group_count, group_size),
        ),
    )
    token_count = query_rows.shape[0]
    return (
        cells_first(log_groups, token_count),
        cells_first(dot_groups, token_count),
        cells_first(grad_groups, token_count),
    )


def key_block(
    key_rows, value_rows, query_outer, grad_outer, log_outer, dot_outer, allowed, head_count
):
    scale = 1.0 / math.sqrt(HEAD_DIM)
    group_size = math.gcd(head_count, 4)
    group_count = head_count // group_size
    outer_count = query_outer.shape[0]
    log_groups = log_outer.reshape(outer_count, group_count, group_size).transpose(1, 2, 0)
    dot_groups = dot_outer.reshape(outer_count, group_count, group_size).transpose(1, 2, 0)

    def key_one_group(pieces):
        key_part, value_part, query_part, grad_part, log_part, dot_part = pieces
        scores = (
            jnp.einsum("hdk,hdq->hkq", key_part, query_part, preferred_element_type=jnp.float32)
            * scale
        )
        probs = jnp.where(allowed[None], jnp.exp(scores - log_part[:, None, :]), 0.0)
        probs_half = probs.astype(jnp.bfloat16)
        value_grad = jnp.einsum(
            "hkq,hdq->hdk", probs_half, grad_part, preferred_element_type=jnp.float32
        )
        grad_probs = jnp.einsum(
            "hdk,hdq->hkq", value_part, grad_part, preferred_element_type=jnp.float32
        )
        grad_scores = (probs * (grad_probs - dot_part[:, None, :])).astype(jnp.bfloat16)
        key_grad = (
            jnp.einsum("hkq,hdq->hdk", grad_scores, query_part, preferred_element_type=jnp.float32)
            * scale
        )
        return (key_grad.astype(jnp.bfloat16), value_grad.astype(jnp.bfloat16))

    key_groups, value_groups = lax.map(
        key_one_group,
        (
            heads_last_cells(key_rows, group_count, group_size),
            heads_last_cells(value_rows, group_count, group_size),
            heads_last_cells(query_outer, group_count, group_size),
            heads_last_cells(grad_outer, group_count, group_size),
            log_groups,
            dot_groups,
        ),
    )
    token_count = key_rows.shape[0]
    return (cells_first(key_groups, token_count), cells_first(value_groups, token_count))


def flatten_cells(field):
    return field.reshape(-1, field.shape[-1])


def shards(query_field, key_field, value_field, out_grad, pole_reach):
    block_rows, block_cols, model_width = query_field.shape
    head_count = model_width // HEAD_DIM
    lat_count = lax.axis_size("lat")
    lon_count = lax.axis_size("lon")
    lat_index = lax.axis_index("lat")
    lon_index = lax.axis_index("lon")
    pair_bit = lon_count.bit_length() - 2
    is_north = lat_index == 0
    is_south = lat_index == lat_count - 1
    allowed = neighbour_mask(
        pole_reach,
        lat_index,
        lon_index,
        block_rows,
        block_cols,
        block_rows * lat_count,
        block_cols * lon_count,
    )

    def assemble_single(padded_set, partner_set):
        return tuple(
            (
                splice(padded, partner, partner, block_rows, is_north, is_south)
                for padded, partner in zip(padded_set, partner_set)
            )
        )

    padded_set = (
        with_halo(query_field, (("lat", 0), ("lon", 1)), RADIUS),
        with_halo(key_field, (("lat", 0), ("lon", 1)), RADIUS),
        with_halo(value_field, (("lat", 0), ("lon", 1)), RADIUS),
        with_halo(out_grad, (("lat", 0), ("lon", 1)), RADIUS),
    )
    partner_set = swapped(
        for_sending(tuple((single_slab(padded, block_rows, is_north) for padded in padded_set))),
        "lon",
        pair_bit,
    )
    query_outer, key_outer, value_outer, grad_outer = assemble_single(padded_set, partner_set)
    log_total, grad_dot, query_grad = query_block(
        flatten_cells(query_field),
        flatten_cells(key_outer),
        flatten_cells(value_outer),
        flatten_cells(out_grad),
        allowed,
        head_count,
    )
    stats = (
        log_total.reshape(block_rows, block_cols, head_count),
        grad_dot.reshape(block_rows, block_cols, head_count),
    )
    stat_padded = (
        with_halo(stats[0], (("lat", 0), ("lon", 1)), RADIUS),
        with_halo(stats[1], (("lat", 0), ("lon", 1)), RADIUS),
    )
    stat_partner = swapped(
        tuple((single_slab(padded, block_rows, is_north) for padded in stat_padded)),
        "lon",
        pair_bit,
    )
    log_outer, dot_outer = assemble_single(stat_padded, stat_partner)
    key_grad, value_grad = key_block(
        flatten_cells(key_field),
        flatten_cells(value_field),
        flatten_cells(query_outer),
        flatten_cells(grad_outer),
        flatten_cells(log_outer),
        flatten_cells(dot_outer),
        allowed,
        head_count,
    )
    grid_shape = (block_rows, block_cols, model_width)
    return (
        query_grad.reshape(grid_shape),
        key_grad.reshape(grid_shape),
        value_grad.reshape(grid_shape),
    )


def solution(mesh):
    placed = (
        P("lat", "lon", None),
        P("lat", "lon", None),
        P("lat", "lon", None),
        P("lat", "lon", None),
        P(),
    )
    return jax.shard_map(
        shards,
        mesh=mesh,
        in_specs=placed,
        out_specs=(P("lat", "lon", None), P("lat", "lon", None), P("lat", "lon", None)),
        check_vma=False,
    )
```

profile of v0, /device:TPU:0, one launch (start us, length us, event | category | flops | bytes accessed | tf_op | source)
XLA Modules:
  0.0 192.0 jit_solution(16035493457818279813)
XLA Ops:
  2.2 3.0 %collective-permute-start.6 = (bf16[6,16,512]{2,1,0:T(8,128)(2,1)S(1)}, bf16[6,16,512]{2,1,0:T(8,128)(2,1)S(1)}, u32[]{:S(2)}, u32[]{:S(2)}) collective-permute-start(bf16[6,16,512]{2,1,0:T(8,128)(2,1)S(1)} %get-tuple-element.312), channel_id=1, source_target_pairs={{4,0},{8,4},{12,8},{16,12},{20,16},{24,20},{28,24},{0,28},{5,1},{9... | collective-permute-start | bytes 294920 | tf_op jit(solution)/shard_map/ppermute | solution.py:21
  5.1 1.6 fusion.95
  6.8 2.6 %collective-permute-start.1 = (bf16[6,16,512]{2,1,0:T(8,128)(2,1)}, bf16[6,16,512]{2,1,0:T(8,128)(2,1)S(1)}, u32[]{:S(2)}, u32[]{:S(2)}) collective-permute-start(bf16[6,16,512]{2,1,0:T(8,128)(2,1)} %get-tuple-element.314), channel_id=1, source_target_pairs={{4,0},{8,4},{12,8},{16,12},{20,16},{24,20},{28,24},{0,28},{5,1},{9... | collective-permute-start | bytes 294920 | tf_op jit(solution)/shard_map/ppermute | solution.py:21
  9.4 1.7 fusion.92
  19.1 2.6 %collective-permute-start.21 = (bf16[6,16,512]{2,1,0:T(8,128)(2,1)}, bf16[6,16,512]{2,1,0:T(8,128)(2,1)S(1)}, u32[]{:S(2)}, u32[]{:S(2)}) collective-permute-start(bf16[6,16,512]{2,1,0:T(8,128)(2,1)} %get-tuple-element.308), channel_id=1, source_target_pairs={{4,0},{8,4},{12,8},{16,12},{20,16},{24,20},{28,24},{0,28},{5,1},{9... | collective-permute-start | bytes 294920 | tf_op jit(solution)/shard_map/ppermute | solution.py:21
  21.9 2.7 %collective-permute-start.11 = (bf16[6,16,512]{2,1,0:T(8,128)(2,1)}, bf16[6,16,512]{2,1,0:T(8,128)(2,1)S(1)}, u32[]{:S(2)}, u32[]{:S(2)}) collective-permute-start(bf16[6,16,512]{2,1,0:T(8,128)(2,1)} %get-tuple-element.310), channel_id=1, source_target_pairs={{4,0},{8,4},{12,8},{16,12},{20,16},{24,20},{28,24},{0,28},{5,1},{9... | collective-permute-start | bytes 294920 | tf_op jit(solution)/shard_map/ppermute | solution.py:21
  24.6 2.3 %collective-permute-start.7 = (bf16[20,6,512]{2,1,0:T(8,128)(2,1)S(1)}, bf16[20,6,512]{2,1,0:T(8,128)(2,1)S(1)}, u32[]{:S(2)}, u32[]{:S(2)}) collective-permute-start(bf16[20,6,512]{2,1,0:T(8,128)(2,1)S(1)} %get-tuple-element.300), channel_id=1, source_target_pairs={{0,1},{1,2},{2,3},{3,0},{4,5},{5,6},{6,7},{7,4},{8,9},{9,10},{10,1... | collective-permute-start | bytes 368648 | tf_op jit(solution)/shard_map/ppermute | solution.py:18
  27.0 2.1 %collective-permute-start.8 = (bf16[20,6,512]{2,1,0:T(8,128)(2,1)S(1)}, bf16[20,6,512]{2,1,0:T(8,128)(2,1)S(1)}, u32[]{:S(2)}, u32[]{:S(2)}) collective-permute-start(bf16[20,6,512]{2,1,0:T(8,128)(2,1)S(1)} %get-tuple-element.301), channel_id=1, source_target_pairs={{1,0},{2,1},{3,2},{0,3},{5,4},{6,5},{7,6},{4,7},{9,8},{10,9},{11,1... | collective-permute-start | bytes 368648 | tf_op jit(solution)/shard_map/ppermute | solution.py:21
  29.3 3.8 %collective-permute-start.3 = (bf16[20,6,512]{2,1,0:T(8,128)(2,1)S(1)}, bf16[20,6,512]{2,1,0:T(8,128)(2,1)S(1)}, u32[]{:S(2)}, u32[]{:S(2)}) collective-permute-start(bf16[20,6,512]{2,1,0:T(8,128)(2,1)S(1)} %get-tuple-element.303), channel_id=1, source_target_pairs={{1,0},{2,1},{3,2},{0,3},{5,4},{6,5},{7,6},{4,7},{9,8},{10,9},{11,1... | collective-permute-start | bytes 368648 | tf_op jit(solution)/shard_map/ppermute | solution.py:21
  34.2 5.5 %collective-permute-start.23 = (bf16[20,6,512]{2,1,0:T(8,128)(2,1)S(1)}, bf16[20,6,512]{2,1,0:T(8,128)(2,1)S(1)}, u32[]{:S(2)}, u32[]{:S(2)}) collective-permute-start(bf16[20,6,512]{2,1,0:T(8,128)(2,1)S(1)} %get-tuple-element.297), channel_id=1, source_target_pairs={{1,0},{2,1},{3,2},{0,3},{5,4},{6,5},{7,6},{4,7},{9,8},{10,9},{11,1... | collective-permute-start | bytes 368648 | tf_op jit(solution)/shard_map/ppermute | solution.py:21
  41.3 5.4 %collective-permute-start.13 = (bf16[20,6,512]{2,1,0:T(8,128)(2,1)S(1)}, bf16[20,6,512]{2,1,0:T(8,128)(2,1)S(1)}, u32[]{:S(2)}, u32[]{:S(2)}) collective-permute-start(bf16[20,6,512]{2,1,0:T(8,128)(2,1)S(1)} %get-tuple-element.299), channel_id=1, source_target_pairs={{1,0},{2,1},{3,2},{0,3},{5,4},{6,5},{7,6},{4,7},{9,8},{10,9},{11,1... | collective-permute-start | bytes 368648 | tf_op jit(solution)/shard_map/ppermute | solution.py:21
  48.5 3.0 %collective-permute-start.4 = (bf16[6,28,512]{2,1,0:T(8,128)(2,1)}, bf16[6,28,512]{2,1,0:T(8,128)(2,1)}, u32[]{:S(2)}, u32[]{:S(2)}) collective-permute-start(bf16[6,28,512]{2,1,0:T(8,128)(2,1)} %slice_select_fusion.3), channel_id=1, source_target_pairs={{0,2},{2,0},{1,3},{3,1},{4,6},{6,4},{5,7},{7,5},{8,10},{10,8},{9,1... | collective-permute-start | bytes 516104 | tf_op jit(solution)/shard_map/ppermute | solution.py:41
  54.2 1.2 collective-permute-done.12
  57.3 17.3 %collective-permute-start.14 = (bf16[6,28,512]{2,1,0:T(8,128)(2,1)}, bf16[6,28,512]{2,1,0:T(8,128)(2,1)}, u32[]{:S(2)}, u32[]{:S(2)}) collective-permute-start(bf16[6,28,512]{2,1,0:T(8,128)(2,1)} %slice_select_fusion.1), channel_id=1, source_target_pairs={{0,2},{2,0},{1,3},{3,1},{4,6},{6,4},{5,7},{7,5},{8,10},{10,8},{9,1... | collective-permute-start | bytes 516104 | tf_op jit(solution)/shard_map/ppermute | solution.py:41
  74.5 2.0 %collective-permute-done.9 = bf16[6,28,512]{2,1,0:T(8,128)(2,1)} collective-permute-done((bf16[6,28,512]{2,1,0:T(8,128)(2,1)S(1)}, bf16[6,28,512]{2,1,0:T(8,128)(2,1)}, u32[]{:S(2)}, u32[]{:S(2)}) %collective-permute-start.9) | collective-permute-done | bytes 172064 | tf_op jit(solution)/shard_map/ppermute | solution.py:41
  78.9 3.6 %select_n.199 = bf16[560,4,4,32]{3,2,1,0:T(4,128)(2,1)S(1)} reshape(bf16[20,28,512]{2,1,0:T(8,128)(2,1)} %maximum_select_fusion.3) | data formatting | bytes 1146880 | tf_op jit(solution)/shard_map/jit(_where)/select_n | solution.py:106
  82.5 2.8 %copy.37 = bf16[4,4,32,560]{3,2,1,0:T(8,128)(2,1)} copy(bf16[4,4,32,560]{2,1,0,3:T(4,128)(2,1)S(1)} %bitcast.147) | data formatting | bytes 1146880
  86.3 1.5 maximum_select_fusion
  88.8 3.6 %select_n.195 = bf16[560,4,4,32]{3,2,1,0:T(4,128)(2,1)S(1)} reshape(bf16[20,28,512]{2,1,0:T(8,128)(2,1)} %maximum_select_fusion.1) | data formatting | bytes 1146880 | tf_op jit(solution)/shard_map/jit(_where)/select_n | solution.py:106
  92.5 2.8 %copy.35 = bf16[4,4,32,560]{3,2,1,0:T(8,128)(2,1)} copy(bf16[4,4,32,560]{2,1,0,3:T(4,128)(2,1)S(1)} %bitcast.148) | data formatting | bytes 1146880
  95.4 25.6 %while.28 = (s32[]{:T(128)}, f32[4,4,128]{2,1,0:T(4,128)S(1)}, f32[4,4,128]{2,1,0:T(4,128)S(1)}, bf16[4,4,32,128]{3,2,1,0:T(8,128)(2,1)S(1)}, bf16[4,4,32,128]{3...) while((s32[]{:T(128)}, f32[4,4,128]{2,1,0:T(4,128)S(1)}, ...), condition=%wide.region_8.9_spmd.clone, body=%wide.region_4.8_spmd.clone.sunk | while | flops 78068736 | bytes 6056221 | solution.py:151
  95.4 1.2 and_and_fusion.4
  97.2 1.3 select_reduce_fusion.8
  98.9 1.3 fusion.120
  100.1 1.6 fusion.121
  101.8 1.2 and_and_fusion.4
  103.6 1.3 select_reduce_fusion.8
  105.2 1.3 fusion.120
  106.5 1.6 fusion.121
  108.1 1.2 and_and_fusion.4
  110.0 1.3 select_reduce_fusion.8
  111.6 1.3 fusion.120
  112.9 1.6 fusion.121
  114.5 1.2 and_and_fusion.4
  116.4 1.3 select_reduce_fusion.8
  118.0 1.3 fusion.120
  119.3 1.6 fusion.121
  123.3 2.6 %collective-permute-start.26 = (f32[6,16,16]{1,0,2:T(8,128)}, f32[6,16,16]{1,0,2:T(8,128)}, u32[]{:S(2)}, u32[]{:S(2)}) collective-permute-start(f32[6,16,16]{1,0,2:T(8,128)} %slice.211), channel_id=1, source_target_pairs={{4,0},{8,4},{12,8},{16,12},{20,16},{24,20},{28,24},{0,28},{5,1},{9... | collective-permute-start | bytes 18440 | tf_op jit(solution)/shard_map/ppermute | solution.py:21
  127.3 2.6 %collective-permute-start.16 = (f32[6,16,16]{1,0,2:T(8,128)}, f32[6,16,16]{1,0,2:T(8,128)}, u32[]{:S(2)}, u32[]{:S(2)}) collective-permute-start(f32[6,16,16]{1,0,2:T(8,128)} %slice.193), channel_id=1, source_target_pairs={{4,0},{8,4},{12,8},{16,12},{20,16},{24,20},{28,24},{0,28},{5,1},{9... | collective-permute-start | bytes 18440 | tf_op jit(solution)/shard_map/ppermute | solution.py:21
  131.3 1.2 rev.28
  134.5 1.3 select_n.214
  135.9 2.1 %copy.42 = bf16[4,4,32,560]{3,2,1,0:T(8,128)(2,1)S(1)} copy(bf16[4,4,32,560]{2,1,0,3:T(4,128)(2,1)S(1)} %bitcast.149) | data formatting | bytes 1146880
  137.9 3.6 %select_n.203 = bf16[560,4,4,32]{3,2,1,0:T(4,128)(2,1)S(1)} reshape(bf16[20,28,512]{2,1,0:T(8,128)(2,1)} %maximum_select_fusion.5) | data formatting | bytes 1146880 | tf_op jit(solution)/shard_map/jit(_where)/select_n | solution.py:106
  141.6 2.8 %copy.39 = bf16[4,4,32,560]{3,2,1,0:T(8,128)(2,1)} copy(bf16[4,4,32,560]{2,1,0,3:T(4,128)(2,1)S(1)} %bitcast.150) | data formatting | bytes 1146880
  146.3 3.8 %collective-permute-start.28 = (f32[20,6,16]{1,0,2:T(8,128)S(1)}, f32[20,6,16]{1,0,2:T(8,128)S(1)}, u32[]{:S(2)}, u32[]{:S(2)}) collective-permute-start(f32[20,6,16]{1,0,2:T(8,128)S(1)} %get-tuple-element.305), channel_id=1, source_target_pairs={{1,0},{2,1},{3,2},{0,3},{5,4},{6,5},{7,6},{4,7},{9,8},{10,9},{11,1... | collective-permute-start | bytes 23048 | tf_op jit(solution)/shard_map/ppermute | solution.py:21
  151.2 3.8 %collective-permute-start.18 = (f32[20,6,16]{1,0,2:T(8,128)S(1)}, f32[20,6,16]{1,0,2:T(8,128)S(1)}, u32[]{:S(2)}, u32[]{:S(2)}) collective-permute-start(f32[20,6,16]{1,0,2:T(8,128)S(1)} %get-tuple-element.307), channel_id=1, source_target_pairs={{1,0},{2,1},{3,2},{0,3},{5,4},{6,5},{7,6},{4,7},{9,8},{10,9},{11,1... | collective-permute-start | bytes 23048 | tf_op jit(solution)/shard_map/ppermute | solution.py:21
  156.1 3.2 %collective-permute-done.28 = f32[20,6,16]{1,0,2:T(8,128)S(1)} collective-permute-done((f32[20,6,16]{1,0,2:T(8,128)S(1)}, f32[20,6,16]{1,0,2:T(8,128)S(1)}, u32[]{:S(2)}, u32[]{:S(2)}) %collective-permute-start.28) | collective-permute-done | bytes 7712 | tf_op jit(solution)/shard_map/ppermute | solution.py:21
  160.4 1.5 collective-permute-start.29
  161.9 2.3 %collective-permute-done.17 = f32[20,6,16]{1,0,2:T(8,128)S(1)} collective-permute-done((f32[20,6,16]{1,0,2:T(8,128)S(1)}, f32[20,6,16]{1,0,2:T(8,128)S(1)}, u32[]{:S(2)}, u32[]{:S(2)}) %collective-permute-start.17) | collective-permute-done | bytes 7712 | tf_op jit(solution)/shard_map/ppermute | solution.py:18
  165.3 2.7 %collective-permute-start.19 = (f32[6,28,16]{1,0,2:T(8,128)S(1)}, f32[6,28,16]{1,0,2:T(8,128)S(1)}, u32[]{:S(2)}, u32[]{:S(2)}) collective-permute-start(f32[6,28,16]{1,0,2:T(8,128)S(1)} %slice_select_fusion.5), channel_id=1, source_target_pairs={{0,2},{2,0},{1,3},{3,1},{4,6},{6,4},{5,7},{7,5},{8,10},{10,8},{9,1... | collective-permute-start | bytes 32264 | tf_op jit(solution)/shard_map/ppermute | solution.py:41
  168.8 1.8 collective-permute-done.19
  170.9 19.6 %while.29 = (s32[]{:T(128)}, bf16[4,4,32,128]{3,2,1,0:T(8,128)(2,1)S(1)}, bf16[4,4,32,128]{3,2,1,0:T(8,128)(2,1)S(1)}, bf16[4,4,32,560]{3,2,1,0:T(8,128)(2,1)S(1...) while((s32[]{:T(128)}, ...), condition=%wide.region_10.11_spmd.clone, body=%wide.region_9.10_spmd.clone.sunk | while | flops 75743232 | bytes 4724001 | solution.py:199
  170.9 1.2 and_and_fusion.5
  172.8 1.3 fusion.129
  174.1 1.4 fusion.130
  175.8 1.2 and_and_fusion.5
  177.7 1.3 fusion.129
  179.0 1.4 fusion.130
  180.7 1.2 and_and_fusion.5
  182.6 1.3 fusion.129
  183.9 1.4 fusion.130
  185.6 1.2 and_and_fusion.5
  187.5 1.3 fusion.129
  188.8 1.4 fusion.130
  (236 shorter events, 46.4 us)
Async XLA Ops:
  0.6 13.2 %copy-start.8 = (bf16[8,16,512]{2,1,0:T(8,128)(2,1)S(1)}, bf16[8,16,512]{2,1,0:T(8,128)(2,1)}, u32[]{:S(2)}) copy-start(bf16[8,16,512]{2,1,0:T(8,128)(2,1)} %param.12) | copy-start | bytes 393220
  0.6 11.7 %copy-start.9 = (bf16[8,16,512]{2,1,0:T(8,128)(2,1)S(1)}, bf16[8,16,512]{2,1,0:T(8,128)(2,1)}, u32[]{:S(2)}) copy-start(bf16[8,16,512]{2,1,0:T(8,128)(2,1)} %param.9) | copy-start | bytes 393220
  1.7 17.4 %collective-permute-start.5 = (bf16[6,16,512]{2,1,0:T(8,128)(2,1)S(1)}, bf16[6,16,512]{2,1,0:T(8,128)(2,1)S(1)}, u32[]{:S(2)}, u32[]{:S(2)}) collective-permute-start(bf16[6,16,512]{2,1,0:T(8,128)(2,1)S(1)} %get-tuple-element.313), channel_id=1, source_target_pairs={{0,4},{4,8},{8,12},{12,16},{16,20},{20,24},{24,28},{28,0},{1,5},{5... | collective-permute-start | bytes 294920 | tf_op jit(solution)/shard_map/ppermute | solution.py:18
  2.2 12.0 %copy-start.7 = (bf16[8,16,512]{2,1,0:T(8,128)(2,1)S(1)}, bf16[8,16,512]{2,1,0:T(8,128)(2,1)}, u32[]{:S(2)}) copy-start(bf16[8,16,512]{2,1,0:T(8,128)(2,1)} %param.10) | copy-start | bytes 393220
  2.2 19.6 %collective-permute-start.6 = (bf16[6,16,512]{2,1,0:T(8,128)(2,1)S(1)}, bf16[6,16,512]{2,1,0:T(8,128)(2,1)S(1)}, u32[]{:S(2)}, u32[]{:S(2)}) collective-permute-start(bf16[6,16,512]{2,1,0:T(8,128)(2,1)S(1)} %get-tuple-element.312), channel_id=1, source_target_pairs={{4,0},{8,4},{12,8},{16,12},{20,16},{24,20},{28,24},{0,28},{5,1},{9... | collective-permute-start | bytes 294920 | tf_op jit(solution)/shard_map/ppermute | solution.py:21
  6.7 15.2 %collective-permute-start = (bf16[6,16,512]{2,1,0:T(8,128)(2,1)S(1)}, bf16[6,16,512]{2,1,0:T(8,128)(2,1)S(1)}, u32[]{:S(2)}, u32[]{:S(2)}) collective-permute-start(bf16[6,16,512]{2,1,0:T(8,128)(2,1)S(1)} %get-tuple-element.315), channel_id=1, source_target_pairs={{0,4},{4,8},{8,12},{12,16},{16,20},{20,24},{24,28},{28,0},{1,5},{5... | collective-permute-start | bytes 294920 | tf_op jit(solution)/shard_map/ppermute | solution.py:18
  6.8 17.9 %collective-permute-start.1 = (bf16[6,16,512]{2,1,0:T(8,128)(2,1)}, bf16[6,16,512]{2,1,0:T(8,128)(2,1)S(1)}, u32[]{:S(2)}, u32[]{:S(2)}) collective-permute-start(bf16[6,16,512]{2,1,0:T(8,128)(2,1)} %get-tuple-element.314), channel_id=1, source_target_pairs={{4,0},{8,4},{12,8},{16,12},{20,16},{24,20},{28,24},{0,28},{5,1},{9... | collective-permute-start | bytes 294920 | tf_op jit(solution)/shard_map/ppermute | solution.py:21
  11.1 3.4 %copy-start.6 = (bf16[8,16,512]{2,1,0:T(8,128)(2,1)S(1)}, bf16[8,16,512]{2,1,0:T(8,128)(2,1)}, u32[]{:S(2)}) copy-start(bf16[8,16,512]{2,1,0:T(8,128)(2,1)} %param.11) | copy-start | bytes 393220
  11.1 15.9 %collective-permute-start.20 = (bf16[6,16,512]{2,1,0:T(8,128)(2,1)}, bf16[6,16,512]{2,1,0:T(8,128)(2,1)S(1)}, u32[]{:S(2)}, u32[]{:S(2)}) collective-permute-start(bf16[6,16,512]{2,1,0:T(8,128)(2,1)} %get-tuple-element.309), channel_id=1, source_target_pairs={{0,4},{4,8},{8,12},{12,16},{16,20},{20,24},{24,28},{28,0},{1,5},{5... | collective-permute-start | bytes 294920 | tf_op jit(solution)/shard_map/ppermute | solution.py:18
  19.1 10.0 %collective-permute-start.21 = (bf16[6,16,512]{2,1,0:T(8,128)(2,1)}, bf16[6,16,512]{2,1,0:T(8,128)(2,1)S(1)}, u32[]{:S(2)}, u32[]{:S(2)}) collective-permute-start(bf16[6,16,512]{2,1,0:T(8,128)(2,1)} %get-tuple-element.308), channel_id=1, source_target_pairs={{4,0},{8,4},{12,8},{16,12},{20,16},{24,20},{28,24},{0,28},{5,1},{9... | collective-permute-start | bytes 294920 | tf_op jit(solution)/shard_map/ppermute | solution.py:21
  21.8 7.5 %collective-permute-start.10 = (bf16[6,16,512]{2,1,0:T(8,128)(2,1)}, bf16[6,16,512]{2,1,0:T(8,128)(2,1)S(1)}, u32[]{:S(2)}, u32[]{:S(2)}) collective-permute-start(bf16[6,16,512]{2,1,0:T(8,128)(2,1)} %get-tuple-element.311), channel_id=1, source_target_pairs={{0,4},{4,8},{8,12},{12,16},{16,20},{20,24},{24,28},{28,0},{1,5},{5... | collective-permute-start | bytes 294920 | tf_op jit(solution)/shard_map/ppermute | solution.py:18
  21.9 11.2 %collective-permute-start.11 = (bf16[6,16,512]{2,1,0:T(8,128)(2,1)}, bf16[6,16,512]{2,1,0:T(8,128)(2,1)S(1)}, u32[]{:S(2)}, u32[]{:S(2)}) collective-permute-start(bf16[6,16,512]{2,1,0:T(8,128)(2,1)} %get-tuple-element.310), channel_id=1, source_target_pairs={{4,0},{8,4},{12,8},{16,12},{20,16},{24,20},{28,24},{0,28},{5,1},{9... | collective-permute-start | bytes 294920 | tf_op jit(solution)/shard_map/ppermute | solution.py:21
  24.6 9.6 %collective-permute-start.7 = (bf16[20,6,512]{2,1,0:T(8,128)(2,1)S(1)}, bf16[20,6,512]{2,1,0:T(8,128)(2,1)S(1)}, u32[]{:S(2)}, u32[]{:S(2)}) collective-permute-start(bf16[20,6,512]{2,1,0:T(8,128)(2,1)S(1)} %get-tuple-element.300), channel_id=1, source_target_pairs={{0,1},{1,2},{2,3},{3,0},{4,5},{5,6},{6,7},{7,4},{8,9},{9,10},{10,1... | collective-permute-start | bytes 368648 | tf_op jit(solution)/shard_map/ppermute | solution.py:18
  27.0 12.7 %collective-permute-start.8 = (bf16[20,6,512]{2,1,0:T(8,128)(2,1)S(1)}, bf16[20,6,512]{2,1,0:T(8,128)(2,1)S(1)}, u32[]{:S(2)}, u32[]{:S(2)}) collective-permute-start(bf16[20,6,512]{2,1,0:T(8,128)(2,1)S(1)} %get-tuple-element.301), channel_id=1, source_target_pairs={{1,0},{2,1},{3,2},{0,3},{5,4},{6,5},{7,6},{4,7},{9,8},{10,9},{11,1... | collective-permute-start | bytes 368648 | tf_op jit(solution)/shard_map/ppermute | solution.py:21
  29.1 12.2 %collective-permute-start.2 = (bf16[20,6,512]{2,1,0:T(8,128)(2,1)S(1)}, bf16[20,6,512]{2,1,0:T(8,128)(2,1)S(1)}, u32[]{:S(2)}, u32[]{:S(2)}) collective-permute-start(bf16[20,6,512]{2,1,0:T(8,128)(2,1)S(1)} %get-tuple-element.302), channel_id=1, source_target_pairs={{0,1},{1,2},{2,3},{3,0},{4,5},{5,6},{6,7},{7,4},{8,9},{9,10},{10,1... | collective-permute-start | bytes 368648 | tf_op jit(solution)/shard_map/ppermute | solution.py:18
  29.3 17.4 %collective-permute-start.3 = (bf16[20,6,512]{2,1,0:T(8,128)(2,1)S(1)}, bf16[20,6,512]{2,1,0:T(8,128)(2,1)S(1)}, u32[]{:S(2)}, u32[]{:S(2)}) collective-permute-start(bf16[20,6,512]{2,1,0:T(8,128)(2,1)S(1)} %get-tuple-element.303), channel_id=1, source_target_pairs={{1,0},{2,1},{3,2},{0,3},{5,4},{6,5},{7,6},{4,7},{9,8},{10,9},{11,1... | collective-permute-start | bytes 368648 | tf_op jit(solution)/shard_map/ppermute | solution.py:21
  33.2 15.3 %collective-permute-start.22 = (bf16[20,6,512]{2,1,0:T(8,128)(2,1)S(1)}, bf16[20,6,512]{2,1,0:T(8,128)(2,1)S(1)}, u32[]{:S(2)}, u32[]{:S(2)}) collective-permute-start(bf16[20,6,512]{2,1,0:T(8,128)(2,1)S(1)} %get-tuple-element.296), channel_id=1, source_target_pairs={{0,1},{1,2},{2,3},{3,0},{4,5},{5,6},{6,7},{7,4},{8,9},{9,10},{10,1... | collective-permute-start | bytes 368648 | tf_op jit(solution)/shard_map/ppermute | solution.py:18
  34.2 17.5 %collective-permute-start.23 = (bf16[20,6,512]{2,1,0:T(8,128)(2,1)S(1)}, bf16[20,6,512]{2,1,0:T(8,128)(2,1)S(1)}, u32[]{:S(2)}, u32[]{:S(2)}) collective-permute-start(bf16[20,6,512]{2,1,0:T(8,128)(2,1)S(1)} %get-tuple-element.297), channel_id=1, source_target_pairs={{1,0},{2,1},{3,2},{0,3},{5,4},{6,5},{7,6},{4,7},{9,8},{10,9},{11,1... | collective-permute-start | bytes 368648 | tf_op jit(solution)/shard_map/ppermute | solution.py:21
  39.7 0.7 copy-start.17
  39.7 15.7 %collective-permute-start.12 = (bf16[20,6,512]{2,1,0:T(8,128)(2,1)S(1)}, bf16[20,6,512]{2,1,0:T(8,128)(2,1)S(1)}, u32[]{:S(2)}, u32[]{:S(2)}) collective-permute-start(bf16[20,6,512]{2,1,0:T(8,128)(2,1)S(1)} %get-tuple-element.298), channel_id=1, source_target_pairs={{0,1},{1,2},{2,3},{3,0},{4,5},{5,6},{6,7},{7,4},{8,9},{9,10},{10,1... | collective-permute-start | bytes 368648 | tf_op jit(solution)/shard_map/ppermute | solution.py:18
  40.0 7.0 %copy-start.2 = (bf16[20,28,512]{2,1,0:T(8,128)(2,1)}, bf16[20,28,512]{2,1,0:T(8,128)(2,1)S(1)}, u32[]{:S(2)}) copy-start(bf16[20,28,512]{2,1,0:T(8,128)(2,1)S(1)} %pad_maximum_fusion.1) | copy-start | bytes 1720324
  41.3 7.2 %copy-start.16 = (bf16[20,6,512]{2,1,0:T(8,128)(2,1)}, bf16[20,6,512]{2,1,0:T(8,128)(2,1)S(1)}, u32[]{:S(2)}) copy-start(bf16[20,6,512]{2,1,0:T(8,128)(2,1)S(1)} %collective-permute-done.2) | copy-start | bytes 368644
  41.3 14.9 %collective-permute-start.13 = (bf16[20,6,512]{2,1,0:T(8,128)(2,1)S(1)}, bf16[20,6,512]{2,1,0:T(8,128)(2,1)S(1)}, u32[]{:S(2)}, u32[]{:S(2)}) collective-permute-start(bf16[20,6,512]{2,1,0:T(8,128)(2,1)S(1)} %get-tuple-element.299), channel_id=1, source_target_pairs={{1,0},{2,1},{3,2},{0,3},{5,4},{6,5},{7,6},{4,7},{9,8},{10,9},{11,1... | collective-permute-start | bytes 368648 | tf_op jit(solution)/shard_map/ppermute | solution.py:21
  46.7 1.8 copy-start.19
  46.7 29.9 %collective-permute-start.9 = (bf16[6,28,512]{2,1,0:T(8,128)(2,1)S(1)}, bf16[6,28,512]{2,1,0:T(8,128)(2,1)}, u32[]{:S(2)}, u32[]{:S(2)}) collective-permute-start(bf16[6,28,512]{2,1,0:T(8,128)(2,1)S(1)} %slice_select_fusion.2), channel_id=1, source_target_pairs={{0,2},{2,0},{1,3},{3,1},{4,6},{6,4},{5,7},{7,5},{8,10},{10,8},{9,1... | collective-permute-start | bytes 516104 | tf_op jit(solution)/shard_map/ppermute | solution.py:41
  48.5 36.9 %collective-permute-start.4 = (bf16[6,28,512]{2,1,0:T(8,128)(2,1)}, bf16[6,28,512]{2,1,0:T(8,128)(2,1)}, u32[]{:S(2)}, u32[]{:S(2)}) collective-permute-start(bf16[6,28,512]{2,1,0:T(8,128)(2,1)} %slice_select_fusion.3), channel_id=1, source_target_pairs={{0,2},{2,0},{1,3},{3,1},{4,6},{6,4},{5,7},{7,5},{8,10},{10,8},{9,1... | collective-permute-start | bytes 516104 | tf_op jit(solution)/shard_map/ppermute | solution.py:41
  51.7 1.9 copy-start.12
  52.0 0.9 copy-start.3
  53.6 23.9 %slice-start.1 = ((bf16[20,28,512]{2,1,0:T(8,128)(2,1)}), bf16[14,28,512]{2,1,0:T(8,128)(2,1)S(1)}, s32[]{:S(2)}) async-start(bf16[20,28,512]{2,1,0:T(8,128)(2,1)} %copy-done.2), calls=%async_computation.1 | async-start | bytes 917504 | tf_op jit(solution)/shard_map/slice | solution.py:101
  53.6 23.9 %copy-start.18 = (bf16[20,6,512]{2,1,0:T(8,128)(2,1)S(1)}, bf16[20,6,512]{2,1,0:T(8,128)(2,1)}, u32[]{:S(2)}) copy-start(bf16[20,6,512]{2,1,0:T(8,128)(2,1)} %copy-done.17) | copy-start | bytes 368644
  53.6 73.7 %collective-permute-start.24 = (bf16[6,28,512]{2,1,0:T(8,128)(2,1)}, bf16[6,28,512]{2,1,0:T(8,128)(2,1)}, u32[]{:S(2)}, u32[]{:S(2)}) collective-permute-start(bf16[6,28,512]{2,1,0:T(8,128)(2,1)} %slice_select_fusion), channel_id=1, source_target_pairs={{0,2},{2,0},{1,3},{3,1},{4,6},{6,4},{5,7},{7,5},{8,10},{10,8},{9,1... | collective-permute-start | bytes 516104 | tf_op jit(solution)/shard_map/ppermute | solution.py:41
  55.4 1.9 copy-start.10
  56.2 1.0 copy-start.14
  56.5 21.4 %copy-start.4 = (bf16[20,28,512]{2,1,0:T(8,128)(2,1)}, bf16[20,28,512]{2,1,0:T(8,128)(2,1)S(1)}, u32[]{:S(2)}) copy-start(bf16[20,28,512]{2,1,0:T(8,128)(2,1)S(1)} %pad_maximum_fusion.2) | copy-start | bytes 1720324
  57.3 74.1 %collective-permute-start.14 = (bf16[6,28,512]{2,1,0:T(8,128)(2,1)}, bf16[6,28,512]{2,1,0:T(8,128)(2,1)}, u32[]{:S(2)}, u32[]{:S(2)}) collective-permute-start(bf16[6,28,512]{2,1,0:T(8,128)(2,1)} %slice_select_fusion.1), channel_id=1, source_target_pairs={{0,2},{2,0},{1,3},{3,1},{4,6},{6,4},{5,7},{7,5},{8,10},{10,8},{9,1... | collective-permute-start | bytes 516104 | tf_op jit(solution)/shard_map/ppermute | solution.py:41
  92.4 2.9 %copy-start.23 = (bf16[4,4,32,128]{3,2,1,0:T(8,128)(2,1)S(1)}, bf16[4,4,32,128]{3,2,1,0:T(8,128)(2,1)}, u32[]{:S(2)}) copy-start(bf16[4,4,32,128]{3,2,1,0:T(8,128)(2,1)} %copy.36) | copy-start | bytes 393220
  92.4 2.9 %copy-start.24 = (f32[4,4,128]{2,1,0:T(4,128)S(1)}, f32[4,4,128]{2,1,0:T(4,128)}, u32[]{:S(2)}) copy-start(f32[4,4,128]{2,1,0:T(4,128)} %custom-call.4) | copy-start | bytes 24580
  92.4 2.9 %copy-start.25 = (f32[4,4,128]{2,1,0:T(4,128)S(1)}, f32[4,4,128]{2,1,0:T(4,128)}, u32[]{:S(2)}) copy-start(f32[4,4,128]{2,1,0:T(4,128)} %custom-call.5) | copy-start | bytes 24580
  95.3 35.6 %slice-start.2 = ((bf16[20,28,512]{2,1,0:T(8,128)(2,1)}), bf16[14,28,512]{2,1,0:T(8,128)(2,1)S(1)}, s32[]{:S(2)}) async-start(bf16[20,28,512]{2,1,0:T(8,128)(2,1)} %copy-done.3), calls=%async_computation.2 | async-start | bytes 917504 | tf_op jit(solution)/shard_map/slice | solution.py:101
  95.3 35.6 %copy-start.13 = (bf16[20,6,512]{2,1,0:T(8,128)(2,1)S(1)}, bf16[20,6,512]{2,1,0:T(8,128)(2,1)}, u32[]{:S(2)}) copy-start(bf16[20,6,512]{2,1,0:T(8,128)(2,1)} %copy-done.12) | copy-start | bytes 368644
  120.9 6.4 %copy-start.21 = (bf16[4,4,32,128]{3,2,1,0:T(8,128)(2,1)}, bf16[4,4,32,128]{3,2,1,0:T(8,128)(2,1)S(1)}, u32[]{:S(2)}) copy-start(bf16[4,4,32,128]{3,2,1,0:T(8,128)(2,1)S(1)} %get-tuple-element.105) | copy-start | bytes 393220
  122.6 22.6 %collective-permute-start.25 = (f32[6,16,16]{1,0,2:T(8,128)}, f32[6,16,16]{1,0,2:T(8,128)}, u32[]{:S(2)}, u32[]{:S(2)}) collective-permute-start(f32[6,16,16]{1,0,2:T(8,128)} %slice.209), channel_id=1, source_target_pairs={{0,4},{4,8},{8,12},{12,16},{16,20},{20,24},{24,28},{28,0},{1,5},{5... | collective-permute-start | bytes 18440 | tf_op jit(solution)/shard_map/ppermute | solution.py:18
  123.3 21.9 %collective-permute-start.26 = (f32[6,16,16]{1,0,2:T(8,128)}, f32[6,16,16]{1,0,2:T(8,128)}, u32[]{:S(2)}, u32[]{:S(2)}) collective-permute-start(f32[6,16,16]{1,0,2:T(8,128)} %slice.211), channel_id=1, source_target_pairs={{4,0},{8,4},{12,8},{16,12},{20,16},{24,20},{28,24},{0,28},{5,1},{9... | collective-permute-start | bytes 18440 | tf_op jit(solution)/shard_map/ppermute | solution.py:21
  126.6 23.5 %collective-permute-start.15 = (f32[6,16,16]{1,0,2:T(8,128)}, f32[6,16,16]{1,0,2:T(8,128)}, u32[]{:S(2)}, u32[]{:S(2)}) collective-permute-start(f32[6,16,16]{1,0,2:T(8,128)} %slice.191), channel_id=1, source_target_pairs={{0,4},{4,8},{8,12},{12,16},{16,20},{20,24},{24,28},{28,0},{1,5},{5... | collective-permute-start | bytes 18440 | tf_op jit(solution)/shard_map/ppermute | solution.py:18
  127.3 22.8 %collective-permute-start.16 = (f32[6,16,16]{1,0,2:T(8,128)}, f32[6,16,16]{1,0,2:T(8,128)}, u32[]{:S(2)}, u32[]{:S(2)}) collective-permute-start(f32[6,16,16]{1,0,2:T(8,128)} %slice.193), channel_id=1, source_target_pairs={{4,0},{8,4},{12,8},{16,12},{20,16},{24,20},{28,24},{0,28},{5,1},{9... | collective-permute-start | bytes 18440 | tf_op jit(solution)/shard_map/ppermute | solution.py:21
  130.9 1.6 slice-start.3
  130.9 1.6 copy-start.11
  130.9 1.6 copy-start.15
  131.3 1.6 copy-start
  133.0 1.3 copy-start.1
  133.0 1.4 slice-start
  141.6 2.8 %copy-start.22 = (bf16[4,4,32,128]{3,2,1,0:T(8,128)(2,1)S(1)}, bf16[4,4,32,128]{3,2,1,0:T(8,128)(2,1)}, u32[]{:S(2)}) copy-start(bf16[4,4,32,128]{3,2,1,0:T(8,128)(2,1)} %copy-done.21) | copy-start | bytes 393220
  141.6 3.6 %copy-start.20 = (f32[8,16,16]{1,0,2:T(8,128)S(1)}, f32[8,16,16]{1,0,2:T(8,128)}, u32[]{:S(2)}) copy-start(f32[8,16,16]{1,0,2:T(8,128)} %reshape.391) | copy-start | bytes 24580
  146.2 9.8 %collective-permute-start.27 = (f32[20,6,16]{1,0,2:T(8,128)S(1)}, f32[20,6,16]{1,0,2:T(8,128)S(1)}, u32[]{:S(2)}, u32[]{:S(2)}) collective-permute-start(f32[20,6,16]{1,0,2:T(8,128)S(1)} %get-tuple-element.304), channel_id=1, source_target_pairs={{0,1},{1,2},{2,3},{3,0},{4,5},{5,6},{6,7},{7,4},{8,9},{9,10},{10,1... | collective-permute-start | bytes 23048 | tf_op jit(solution)/shard_map/ppermute | solution.py:18
  146.3 13.0 %collective-permute-start.28 = (f32[20,6,16]{1,0,2:T(8,128)S(1)}, f32[20,6,16]{1,0,2:T(8,128)S(1)}, u32[]{:S(2)}, u32[]{:S(2)}) collective-permute-start(f32[20,6,16]{1,0,2:T(8,128)S(1)} %get-tuple-element.305), channel_id=1, source_target_pairs={{1,0},{2,1},{3,2},{0,3},{5,4},{6,5},{7,6},{4,7},{9,8},{10,9},{11,1... | collective-permute-start | bytes 23048 | tf_op jit(solution)/shard_map/ppermute | solution.py:21
  151.2 13.0 %collective-permute-start.17 = (f32[20,6,16]{1,0,2:T(8,128)S(1)}, f32[20,6,16]{1,0,2:T(8,128)S(1)}, u32[]{:S(2)}, u32[]{:S(2)}) collective-permute-start(f32[20,6,16]{1,0,2:T(8,128)S(1)} %get-tuple-element.306), channel_id=1, source_target_pairs={{0,1},{1,2},{2,3},{3,0},{4,5},{5,6},{6,7},{7,4},{8,9},{9,10},{10,1... | collective-permute-start | bytes 23048 | tf_op jit(solution)/shard_map/ppermute | solution.py:18
  151.2 13.0 %collective-permute-start.18 = (f32[20,6,16]{1,0,2:T(8,128)S(1)}, f32[20,6,16]{1,0,2:T(8,128)S(1)}, u32[]{:S(2)}, u32[]{:S(2)}) collective-permute-start(f32[20,6,16]{1,0,2:T(8,128)S(1)} %get-tuple-element.307), channel_id=1, source_target_pairs={{1,0},{2,1},{3,2},{0,3},{5,4},{6,5},{7,6},{4,7},{9,8},{10,9},{11,1... | collective-permute-start | bytes 23048 | tf_op jit(solution)/shard_map/ppermute | solution.py:21
  160.4 8.1 %collective-permute-start.29 = (f32[6,28,16]{1,0,2:T(8,128)S(1)}, f32[6,28,16]{1,0,2:T(8,128)S(1)}, u32[]{:S(2)}, u32[]{:S(2)}) collective-permute-start(f32[6,28,16]{1,0,2:T(8,128)S(1)} %slice_select_fusion.4), channel_id=1, source_target_pairs={{0,2},{2,0},{1,3},{3,1},{4,6},{6,4},{5,7},{7,5},{8,10},{10,8},{9,1... | collective-permute-start | bytes 32264 | tf_op jit(solution)/shard_map/ppermute | solution.py:41
  165.3 5.2 %collective-permute-start.19 = (f32[6,28,16]{1,0,2:T(8,128)S(1)}, f32[6,28,16]{1,0,2:T(8,128)S(1)}, u32[]{:S(2)}, u32[]{:S(2)}) collective-permute-start(f32[6,28,16]{1,0,2:T(8,128)S(1)} %slice_select_fusion.5), channel_id=1, source_target_pairs={{0,2},{2,0},{1,3},{3,1},{4,6},{6,4},{5,7},{7,5},{8,10},{10,8},{9,1... | collective-permute-start | bytes 32264 | tf_op jit(solution)/shard_map/ppermute | solution.py:41
  168.6 2.3 %copy-start.5 = (bf16[4,4,32,560]{3,2,1,0:T(8,128)(2,1)S(1)}, bf16[4,4,32,560]{3,2,1,0:T(8,128)(2,1)}, u32[]{:S(2)}) copy-start(bf16[4,4,32,560]{3,2,1,0:T(8,128)(2,1)} %copy.39) | copy-start | bytes 1720324
where the time goes:
time: 193 us; the launch traced here: 192 us
  starting transfers between devices  68.8 us (36%)
  local copies, waits for them, and re-layouts  53.2 us (28%)
  matrix products  28.7 us (15%)
  other arithmetic  24.3 us (13%)
  waiting for transfers between devices  15 us (8%)
    ppermute x12, starting transfers between devices, with_halo(): lax.ppermute(lax.slice_in_dim(block, 0, width, axis=dim), axis, backward)  40.6 us
    ppermute x6, starting transfers between devices, swapped(): return lax.ppermute(block, axis, route)  25.1 us
    unnamed x68, local copies, waits for them, and re-layouts  16.5 us
    select_n x6, local copies, waits for them, and re-layouts, splice(): return jnp.where(is_south, southern, padded)  12.4 us
    and x8, other arithmetic, neighbour_mask(): allowed & (jnp.logical_not(south_band)[None, None, :, None] | south_query...  9.31 us
    dot_general x4, matrix products, query_one_group(): jnp.einsum('hqk,hdk->hdq', grad_scores, key_part, preferred_element_type=...  6.43 us
    slice x6, local copies, waits for them, and re-layouts, with_halo(): lax.slice_in_dim(block, 0, width, axis=dim)  6.4 us
    ppermute x12, waiting for transfers between devices, with_halo(): lax.ppermute(lax.slice_in_dim(block, block.shape[dim] - width, None, axis...  6.39 us
  transfers between devices with their start and end apart: 30, of which 11 were waited for; matrix products, arithmetic and copies ran while one was open for 43% of the time, Pallas kernels for 0%

commit v1 on v0

v1 whole, which is shorter than its diff:
```python
import functools
import math

import jax
import jax.numpy as jnp
from jax import lax
from jax.experimental import pallas as pl
from jax.experimental.pallas import tpu as pltpu
from jax.sharding import PartitionSpec as P

HEAD_DIM = 32
RADIUS = 6
STRIP = 8
LANES = 128
NEG = -1e30
LOG2E = 1.4426950408889634


def routes(lat_count, lon_count):
    half = lon_count // 2
    pair, around, across = [], [], []
    for i in range(lat_count):
        for j in range(lon_count):
            me = i * lon_count + j
            pair.append((me, (i ^ 1) * lon_count + j))
            step = 1 if i % 2 == 0 else -1
            around.append((me, i * lon_count + (j + step) % lon_count))
            other = i - 1 if i % 2 == 0 else i + 1
            if 0 <= other < lat_count:
                across.append((me, other * lon_count + j))
            else:
                across.append((me, i * lon_count + (j + half) % lon_count))
    return pair, around, across


def sizes(block_rows, block_cols):
    span = block_rows + RADIUS
    own = block_rows * block_cols
    oth = RADIUS * block_cols
    strip = span * STRIP
    off = RADIUS * (block_cols + 2 * STRIP)
    return own, oth, strip, strip, off


def mask_kernel(rows, cols, lat_count, lon_count, sc_ref, reach_ref, reach_t_ref, out_ref):
    lat, lon = sc_ref[0], sc_ref[1]
    total_rows, total_cols = rows * lat_count, cols * lon_count
    half = total_cols // 2
    odd = lax.rem(lat, 2)
    row0, col0 = lat * rows, lon * cols
    own, oth, strip, _, off = sizes(rows, cols)
    outer = own + 2 * strip + oth + off
    t = lax.broadcasted_iota(jnp.int32, (1, outer), 1)
    is_north, is_south = lat == 0, lat == lat_count - 1
    sender_odd = jnp.where(is_north | is_south, odd, 1 - odd)

    def split(index, width):
        shift = width.bit_length() - 1
        return lax.shift_right_logical(index, shift), index & (width - 1)

    r_own, c_own = split(t, cols)
    u = t - own
    r_oth, c_oth = split(u, cols)
    r_oth = r_oth + jnp.where(odd == 0, rows, -RADIUS)
    first = jnp.where(odd == 0, 0, -RADIUS)
    u = t - (own + oth)
    r_a, c_a = split(u, STRIP)
    r_a, c_a = r_a + first, c_a + jnp.where(odd == 0, -STRIP, cols)
    u = t - (own + oth + strip)
    r_b, c_b = split(u, STRIP)
    r_b, c_b = r_b + first, c_b + jnp.where(odd == 0, cols, -STRIP)
    u = t - (own + oth + 2 * strip)
    width = cols + 2 * STRIP
    r_off, x = split(u, width)
    r_off = jnp.where(
        is_north & (odd == 0),
        -1 - r_off,
        jnp.where(
            is_south & (odd == 1),
            rows + RADIUS - 1 - r_off,
            r_off + jnp.where(odd == 0, -RADIUS, rows),
        ),
    )
    first_at = jnp.where(sender_odd == 0, -STRIP, cols)
    second_at = jnp.where(sender_odd == 0, cols, -STRIP)
    c_off = jnp.where(
        x < cols, x, jnp.where(x < cols + STRIP, x - cols + first_at, x - cols - STRIP + second_at)
    )
    at = [own, own + oth, own + oth + strip, own + oth + 2 * strip]
    r_key = jnp.where(
        t < at[0],
        r_own,
        jnp.where(t < at[1], r_oth, jnp.where(t < at[2], r_a, jnp.where(t < at[3], r_b, r_off))),
    )
    c_key = jnp.where(
        t < at[0],
        c_own,
        jnp.where(t < at[1], c_oth, jnp.where(t < at[2], c_a, jnp.where(t < at[3], c_b, c_off))),
    )
    g_key = r_key + row0
    turned = lax.rem(c_key + (col0 + half + total_cols), total_cols)
    pick = lax.broadcasted_iota(jnp.int32, (total_cols, outer), 0) == turned
    north_key = jnp.sum(jnp.where(pick, reach_t_ref[:, 0:1], 0.0), axis=0, keepdims=True)
    south_key = jnp.sum(jnp.where(pick, reach_t_ref[:, 1:2], 0.0), axis=0, keepdims=True)
    g_f = g_key.astype(jnp.float32)
    behind_n = g_key < 0
    behind_s = g_key >= total_rows
    spare = jnp.where(
        behind_n, north_key + 1.0 + g_f, jnp.where(behind_s, south_key + total_rows - g_f, 1.0)
    )
    valid = jnp.where(spare > 0.5, 1.0, 0.0)
    n = lax.broadcasted_iota(jnp.int32, (own, 1), 0)
    r_n, c_n = split(n, cols)
    pick_n = lax.broadcasted_iota(jnp.int32, (own, total_cols), 1) == (c_n + col0)
    north_n = jnp.sum(jnp.where(pick_n, reach_ref[0:1, :], 0.0), axis=1, keepdims=True)
    south_n = jnp.sum(jnp.where(pick_n, reach_ref[1:2, :], 0.0), axis=1, keepdims=True)
    g_n = (r_n + row0).astype(jnp.float32)
    north_ok = jnp.where(north_n > g_n, 1.0, 0.0)
    south_ok = jnp.where(south_n > total_rows - 1 - g_n, 1.0, 0.0)
    need_n = jnp.where(behind_n, 1.0, 0.0)
    need_s = jnp.where(behind_s, 1.0, 0.0)
    near = (jnp.abs(r_key - r_n) <= RADIUS) & (jnp.abs(c_key - c_n) <= RADIUS)
    ok = jnp.where(near, 1.0, 0.0) * valid
    ok = jnp.where(need_n > north_ok, 0.0, ok)
    ok = jnp.where(need_s > south_ok, 0.0, ok)
    out_ref[...] = jnp.where(ok > 0.5, 0.0, NEG)


def assemble(target, own, oth, first, second, off, odd, rows, cols):
    n_own, n_oth, n_strip, _, n_off = sizes(rows, cols)
    at = 0
    target[0:n_own] = own
    at += n_own
    skip = rows - RADIUS
    start = pl.multiple_of(odd * (skip * cols), skip * cols)
    target[at : at + n_oth] = oth[pl.ds(start, n_oth)]
    at += n_oth
    start = pl.multiple_of(odd * (skip * STRIP), skip * STRIP)
    for piece in (first, second):
        target[at : at + n_strip] = piece[pl.ds(start, n_strip)]
        at += n_strip
    target[at : at + n_off] = off[...]


NT = (((1,), (1,)), ((), ()))


def query_kernel(
    rows, cols, sc_ref, q_ref, k_ref, v_ref, g_ref, oth_ref, lc_ref, s2_ref, off_ref, bias_ref,
    dq_ref, st_ref, kall, vall, stat,
):
    odd = lax.rem(sc_ref[0], 2)
    for i, (target, own) in enumerate(((kall, k_ref), (vall, v_ref))):
        assemble(
            target, own[...], oth_ref.at[i], lc_ref.at[i], s2_ref.at[i], off_ref.at[i], odd, rows, cols
        )
    own_count = rows * cols
    scale = 1.0 / math.sqrt(HEAD_DIM)
    lane = lax.broadcasted_iota(jnp.int32, (own_count, LANES), 1)
    per = LANES // HEAD_DIM
    heads = q_ref.shape[1] // HEAD_DIM
    stat[...] = jnp.zeros_like(stat)

    def group(g, carry):
        at = pl.ds(pl.multiple_of(g * LANES, LANES), LANES)
        kg, vg = kall[:, at], vall[:, at]
        qg, gg = q_ref[:, at], g_ref[:, at]
        total = jnp.zeros((own_count, LANES), jnp.float32)
        stats = stat[...]
        for j in range(per):
            mine = (lane >= j * HEAD_DIM) & (lane < (j + 1) * HEAD_DIM)
            qj = jnp.where(mine, qg, jnp.zeros_like(qg))
            gj = jnp.where(mine, gg, jnp.zeros_like(gg))
            s = lax.dot_general(qj, kg, NT, preferred_element_type=jnp.float32)
            gp = lax.dot_general(gj, vg, NT, preferred_element_type=jnp.float32)
            s = s * (scale * LOG2E) + bias_ref[...]
            top = jnp.max(s, axis=1, keepdims=True)
            e = jnp.exp2(s - top)
            total_e = jnp.sum(e, axis=1, keepdims=True)
            p = e * (1.0 / total_e)
            ph = p.astype(jnp.bfloat16).astype(jnp.float32)
            dot = jnp.sum(ph * gp, axis=1, keepdims=True)
            ds = (p * (gp - dot)).astype(jnp.bfloat16)
            dq = jnp.dot(ds, kg, preferred_element_type=jnp.float32)
            total = jnp.where(mine, dq, total)
            h = g * per + j
            log_total = top + jnp.log2(total_e)
            stats = jnp.where((lane == h) | (lane == h + heads) | (lane == h + 2 * heads), log_total, stats)
            base = h + 3 * heads
            stats = jnp.where(
                (lane == base) | (lane == base + heads) | (lane == base + 2 * heads), dot, stats
            )
        stat[...] = stats
        dq_ref[:, at] = (total * scale).astype(jnp.bfloat16)
        return carry

    lax.fori_loop(0, q_ref.shape[1] // LANES, group, 0)
    x = stat[...]
    high = x.astype(jnp.bfloat16).astype(jnp.float32)
    rest = x - high
    mid = rest.astype(jnp.bfloat16).astype(jnp.float32)
    low = rest - mid
    third = lax.rem(lax.shift_right_logical(lane, heads.bit_length() - 1), 3)
    st_ref[...] = jnp.where(third == 0, high, jnp.where(third == 1, mid, low)).astype(jnp.bfloat16)


def key_kernel(
    rows, cols, sc_ref, q_ref, k_ref, v_ref, g_ref, oth_ref, lc_ref, s2_ref, off_ref,
    st_ref, st_oth_ref, st_lc_ref, st_s2_ref, st_off_ref, bias_ref,
    dk_ref, dv_ref, qall, gall, stall, stat_rows,
):
    odd = lax.rem(sc_ref[0], 2)
    for i, (target, own) in enumerate(((qall, q_ref), (gall, g_ref))):
        assemble(
            target, own[...], oth_ref.at[i], lc_ref.at[i], s2_ref.at[i], off_ref.at[i], odd, rows, cols
        )
    assemble(stall, st_ref[...], st_oth_ref, st_lc_ref, st_s2_ref, st_off_ref, odd, rows, cols)
    own_count = rows * cols
    scale = 1.0 / math.sqrt(HEAD_DIM)
    lane = lax.broadcasted_iota(jnp.int32, (own_count, LANES), 1)
    per = LANES // HEAD_DIM
    heads = q_ref.shape[1] // HEAD_DIM
    row = lax.broadcasted_iota(jnp.int32, (2 * heads, LANES), 0)
    col = lax.broadcasted_iota(jnp.int32, (2 * heads, LANES), 1)
    start = jnp.where(row < heads, row, row + 2 * heads)
    choose = (col == start) | (col == start + heads) | (col == start + 2 * heads)
    choose = jnp.where(choose, 1.0, 0.0).astype(jnp.bfloat16)
    stat_rows[...] = lax.dot_general(choose, stall[...], NT, preferred_element_type=jnp.float32)

    def group(g, carry):
        at = pl.ds(pl.multiple_of(g * LANES, LANES), LANES)
        qg, gg = qall[:, at], gall[:, at]
        kg, vg = k_ref[:, at], v_ref[:, at]
        dk_total = jnp.zeros((own_count, LANES), jnp.float32)
        dv_total = jnp.zeros((own_count, LANES), jnp.float32)
        for j in range(per):
            mine = (lane >= j * HEAD_DIM) & (lane < (j + 1) * HEAD_DIM)
            kj = jnp.where(mine, kg, jnp.zeros_like(kg))
            vj = jnp.where(mine, vg, jnp.zeros_like(vg))
            s = lax.dot_general(kj, qg, NT, preferred_element_type=jnp.float32)
            gp = lax.dot_general(vj, gg, NT, preferred_element_type=jnp.float32)
            h = g * per + j
            log_total = stat_rows[pl.ds(h, 1), :]
            dot = stat_rows[pl.ds(h + heads, 1), :]
            p = jnp.exp2(s * (scale * LOG2E) + (bias_ref[...] - log_total))
            ph = p.astype(jnp.bfloat16)
            dv = jnp.dot(ph, gg, preferred_element_type=jnp.float32)
            ds = (p * (gp - dot)).astype(jnp.bfloat16)
            dk = jnp.dot(ds, qg, preferred_element_type=jnp.float32)
            dk_total = jnp.where(mine, dk, dk_total)
            dv_total = jnp.where(mine, dv, dv_total)
        dk_ref[:, at] = (dk_total * scale).astype(jnp.bfloat16)
        dv_ref[:, at] = dv_total.astype(jnp.bfloat16)
        return carry

    lax.fori_loop(0, q_ref.shape[1] // LANES, group, 0)


def shards(lat_count, lon_count, query, key, value, grad, pole_reach):
    rows, cols, width = query.shape
    lat, lon = lax.axis_index("lat"), lax.axis_index("lon")
    odd = lax.rem(lat, 2)
    even = odd == 0
    pair, around, across = routes(lat_count, lon_count)
    axes = ("lat", "lon")
    n_own, n_oth, n_strip, _, n_off = sizes(rows, cols)
    outer = n_own + n_oth + 2 * n_strip + n_off
    place = jnp.stack([lat, lon]).astype(jnp.int32)

    smem = pl.BlockSpec(memory_space=pltpu.SMEM)
    vmem = pl.BlockSpec(memory_space=pltpu.VMEM)

    def call(body, out_shape, n_in, scratch, flops):
        return pl.pallas_call(
            body,
            out_shape=out_shape,
            in_specs=[smem] + [vmem] * (n_in - 1),
            out_specs=jax.tree.map(lambda _: vmem, out_shape),
            scratch_shapes=scratch,
            compiler_params=pltpu.CompilerParams(vmem_limit_bytes=48 << 20),
            cost_estimate=pl.CostEstimate(flops=flops, bytes_accessed=4 << 20, transcendentals=0),
        )

    reach = pole_reach.astype(jnp.float32)
    bias = call(
        functools.partial(mask_kernel, rows, cols, lat_count, lon_count),
        jax.ShapeDtypeStruct((n_own, outer), jnp.float32), 3, [], 1 << 20,
    )(place, reach, reach.T)

    def strip_of(mine, other):
        axis = mine.ndim - 3
        at = jnp.where(even, cols - STRIP, 0)
        mine = lax.dynamic_slice_in_dim(mine, at, STRIP, axis + 1)
        other = lax.dynamic_slice_in_dim(other, at, STRIP, axis + 1)
        top, low = jnp.where(even, mine, other), jnp.where(even, other, mine)
        both = jnp.concatenate([top, low], axis=axis)
        return both.reshape(both.shape[:axis] + (2 * rows * STRIP, both.shape[-1]))

    def edge_of(mine, first, second):
        axis = mine.ndim - 3
        lead = mine.shape[:axis]
        tail = mine.shape[-1:]
        parts = [lax.dynamic_slice_in_dim(mine, jnp.where(even, 0, rows - RADIUS), RADIUS, axis)]
        for piece in (first, second):
            piece = piece.reshape(lead + (2 * rows, STRIP) + tail)
            parts.append(
                lax.dynamic_slice_in_dim(piece, jnp.where(even, 0, 2 * rows - RADIUS), RADIUS, axis)
            )
        return jnp.concatenate(parts, axis=axis + 1).reshape(lead + (n_off,) + tail)

    def send(block, route):
        return lax.ppermute(block, axes, route)

    def halo(mine, other):
        first = send(strip_of(mine, other), around)
        second = send(first, pair)
        off = send(edge_of(mine, first, second), across)
        return first, second, off

    def flat(field):
        return field.reshape(field.shape[:-3] + (n_own, field.shape[-1]))

    mine = jnp.stack([key, value, query, grad])
    other = send(mine, pair)
    kv = halo(mine[:2], other[:2])
    qg = halo(mine[2:], other[2:])
    fields = tuple(flat(x) for x in (query, key, value, grad))
    vm = lambda shape, dtype=jnp.bfloat16: pltpu.VMEM(shape, dtype)
    local = jax.ShapeDtypeStruct((n_own, width), jnp.bfloat16)
    d_query, stats = call(
        functools.partial(query_kernel, rows, cols),
        (local, jax.ShapeDtypeStruct((n_own, LANES), jnp.bfloat16)),
        10,
        [vm((outer, width)), vm((outer, width)), vm((n_own, LANES), jnp.float32)],
        1 << 29,
    )(place, *fields, flat(other[:2]), *kv, bias)
    stats_grid = stats.reshape(rows, cols, LANES)
    stats_other = send(stats_grid, pair)
    st = halo(stats_grid, stats_other)
    d_key, d_value = call(
        functools.partial(key_kernel, rows, cols),
        (local, local),
        15,
        [
            vm((outer, width)), vm((outer, width)), vm((outer, LANES)),
            vm((2 * (width // HEAD_DIM), outer), jnp.float32),
        ],
        1 << 29,
    )(place, *fields, flat(other[2:]), *qg, stats, flat(stats_other), *st, bias)
    shape = (rows, cols, width)
    return d_query.reshape(shape), d_key.reshape(shape), d_value.reshape(shape)


def solution(mesh):
    field = P("lat", "lon", None)
    return jax.shard_map(
        functools.partial(shards, mesh.shape["lat"], mesh.shape["lon"]),
        mesh=mesh,
        in_specs=(field, field, field, field, P()),
        out_specs=(field, field, field),
        check_vma=False,
    )
```

time: 193 us -> 68 us (0.35)
  starting transfers between devices: 68.8 us -> 14.7 us
  local copies, waits for them, and re-layouts: 53.2 us -> 0.81 us
  matrix products: 28.7 us -> 0 us
  other arithmetic: 24.3 us -> 1.55 us
  waiting for transfers between devices: 15 us -> 33.1 us
  Pallas kernels: 0 us -> 16.9 us
    ppermute x30 -> x11, starting transfers between devices: 68.8 us -> 14.7 us  [send(): return lax.ppermute(block, axes, route)]
    dot_general x24 -> x0, matrix products: 28.7 us -> none  [the longest x4 6.43 us: query_one_group(): jnp.einsum('hqk,hdk->hdq', grad_scores, key_part, preferred_element_type=...]
    ppermute x30 -> x11, waiting for transfers between devices: 15 us -> 33.1 us  [send(): return lax.ppermute(block, axes, route)]
    pallas_call x0 -> x3, Pallas kernels: none -> 16.9 us  [the longest x1 9.91 us: shards(): call(functools.partial(query_kernel, rows, cols), (local, jax.ShapeDtypeS...]
    unnamed x68 -> x10, local copies, waits for them, and re-layouts: 16.5 us -> 0.62 us
    select_n x6 -> x0, local copies, waits for them, and re-layouts: 12.4 us -> none  [splice(): return jnp.where(is_south, southern, padded)]
    and x10 -> x0, other arithmetic: 9.46 us -> none  [the longest x8 9.31 us: neighbour_mask(): allowed & (jnp.logical_not(south_band)[None, None, :, None] | south_query...]
    slice x32 -> x1, local copies, waits for them, and re-layouts: 9.48 us -> 0.03 us  [shards(): other[2:]]
  transfers between devices with their start and end apart: 30 -> 11, of which waited for: 11 -> 8; matrix products, arithmetic and copies ran while one was open for 43% -> 1% of each run, Pallas kernels for 0% -> 1%
where the time goes in v1:
time: 68 us; the launch traced here: 67.8 us
  waiting for transfers between devices  33.1 us (49%)
  Pallas kernels  16.9 us (25%)
  starting transfers between devices  14.7 us (22%)
  other arithmetic  1.55 us (2%)
  local copies, waits for them, and re-layouts  0.81 us (1%)
  between operations  0.79 us (1%)
    ppermute x11, waiting for transfers between devices, send(): return lax.ppermute(block, axes, route)  33.1 us
    ppermute x11, starting transfers between devices, send(): return lax.ppermute(block, axes, route)  14.7 us
    pallas_call x1, Pallas kernels, shards(): call(functools.partial(query_kernel, rows, cols), (local, jax.ShapeDtypeS...  9.91 us
    pallas_call x1, Pallas kernels, shards(): call(functools.partial(key_kernel, rows, cols), (local, local), 15, [vm((...  6.13 us
  transfers between devices with their start and end apart: 11, of which 8 were waited for; matrix products, arithmetic and copies ran while one was open for 1% of the time, Pallas kernels for 1%

profile of v1, /device:TPU:0, one launch (start us, length us, event | category | flops | bytes accessed | tf_op | source)
XLA Modules:
  0.0 67.8 jit_solution(11768552278740407696)
XLA Ops:
  0.6 1.2 %pad_maximum_fusion = bf16[4,8,16,512]{3,2,1,0:T(8,128)(2,1)S(1)} fusion(bf16[1,8,16,512]{3,2,1,0:T(8,128)(2,1)} %bitcast.48, bf16[1,8,16,512]{3,2,1,0:T(8,128)(2,1)} %bitcast.33, bf16[1,8,16,512]{3,2,1,0:T(8,128)(2,1)} %bitcast.43, bf16[1,8,16,512]{3,2,1,0:T(8,128)(2,1)} %bitcast.38), kind=kLoop, calls=%fused_computation | loop fusion | flops 786432 | bytes 1048576 | tf_op jit(solution)/shard_map/stack | solution.py:323
  1.8 0.5 collective-permute-start
  2.3 0.0 copy-start
  2.3 0.0 copy-start.1
  2.3 0.0 copy-start.2
  2.3 0.0 copy-start.3
  2.3 1.5 %collective-permute-done = bf16[4,8,16,512]{3,2,1,0:T(8,128)(2,1)S(1)} collective-permute-done((bf16[4,8,16,512]{3,2,1,0:T(8,128)(2,1)S(1)}, bf16[4,8,16,512]{3,2,1,0:T(8,128)(2,1)S(1)}, u32[]{:S(2)}, u32[]{:S(2)}) %collective-permute-start) | collective-permute-done | bytes 524320 | tf_op jit(solution)/shard_map/ppermute | solution.py:312
  3.9 0.0 copy-done
  3.9 0.0 copy-done.1
  3.9 0.0 copy-done.2
  3.9 0.0 copy-done.3
  3.9 0.1 broadcast_select_fusion.1
  4.1 3.0 %collective-permute-start.1 = (bf16[2,128,512]{2,1,0:T(8,128)(2,1)S(1)}, bf16[2,128,512]{2,1,0:T(8,128)(2,1)S(1)}, u32[]{:S(2)}, u32[]{:S(2)}) collective-permute-start(bf16[2,128,512]{2,1,0:T(8,128)(2,1)S(1)} %maximum_bitcast_fusion), channel_id=1, source_target_pairs={{0,1},{1,2},{2,3},{3,0},{4,7},{5,4},{6,5},{7,6},{8,9},{9,10},{10,1... | collective-permute-start | bytes 786440 | tf_op jit(solution)/shard_map/ppermute | solution.py:312
  7.1 1.6 %collective-permute-start.4 = (bf16[2,128,512]{2,1,0:T(8,128)(2,1)S(1)}, bf16[2,128,512]{2,1,0:T(8,128)(2,1)S(1)}, u32[]{:S(2)}, u32[]{:S(2)}) collective-permute-start(bf16[2,128,512]{2,1,0:T(8,128)(2,1)S(1)} %maximum_bitcast_fusion.1), channel_id=1, source_target_pairs={{0,1},{1,2},{2,3},{3,0},{4,7},{5,4},{6,5},{7,6},{8,9},{9,10},{10,1... | collective-permute-start | bytes 786440 | tf_op jit(solution)/shard_map/ppermute | solution.py:312
  8.8 7.4 %collective-permute-done.1.lc_ref = bf16[2,128,512]{2,1,0:T(8,128)(2,1)S(1)} collective-permute-done((bf16[2,128,512]{2,1,0:T(8,128)(2,1)S(1)}, bf16[2,128,512]{2,1,0:T(8,128)(2,1)S(1)}, u32[]{:S(2)}, u32[]{:S(2)}) %collective-permute-start.1) | collective-permute-done | bytes 262176 | tf_op jit(solution)/shard_map/ppermute | solution.py:312
  16.2 0.0 collective-permute-start.2
  16.2 5.3 %collective-permute-done.4.lc_ref = bf16[2,128,512]{2,1,0:T(8,128)(2,1)S(1)} collective-permute-done((bf16[2,128,512]{2,1,0:T(8,128)(2,1)S(1)}, bf16[2,128,512]{2,1,0:T(8,128)(2,1)S(1)}, u32[]{:S(2)}, u32[]{:S(2)}) %collective-permute-start.4) | collective-permute-done | bytes 262176 | tf_op jit(solution)/shard_map/ppermute | solution.py:312
  21.5 0.0 collective-permute-start.5
  21.5 0.0 collective-permute-done.2.s2_ref
  21.6 1.5 %collective-permute-start.3 = (bf16[2,192,512]{2,1,0:T(8,128)(2,1)S(1)}, bf16[2,192,512]{2,1,0:T(8,128)(2,1)S(1)}, u32[]{:S(2)}, u32[]{:S(2)}) collective-permute-start(bf16[2,192,512]{2,1,0:T(8,128)(2,1)S(1)} %bitcast.67), channel_id=1, source_target_pairs={{0,2},{1,3},{2,0},{3,1},{4,8},{5,9},{6,10},{7,11},{8,4},{9,5},{10,... | collective-permute-start | bytes 1179656 | tf_op jit(solution)/shard_map/ppermute | solution.py:312
  23.1 0.0 copy-start.4
  23.1 0.1 pad_add_fusion.sc_ref
  23.1 0.6 copy-done.4
  23.7 0.1 copy.10
  23.8 0.8 %shard_map.76.bias_ref = f32[128,640]{1,0:T(8,128)S(1)} custom-call(s32[2]{0:T(128)S(1)} %pad_add_fusion.sc_ref, f32[2,64]{1,0:T(2,128)S(1)} %convert_element_type.3.reach_ref, f32[64,2]{1,0:T(8,128)S(1)} %bitcast.62), custom_call_target="tpu_custom_call" | custom-call | flops 1048576 | bytes 4194304 | tf_op jit(solution)/shard_map/pallas_call | solution.py:285
  24.7 0.0 collective-permute-done.5.s2_ref
  24.8 9.3 %collective-permute-done.3.off_ref = bf16[2,192,512]{2,1,0:T(8,128)(2,1)S(1)} collective-permute-done((bf16[2,192,512]{2,1,0:T(8,128)(2,1)S(1)}, bf16[2,192,512]{2,1,0:T(8,128)(2,1)S(1)}, u32[]{:S(2)}, u32[]{:S(2)}) %collective-permute-start.3) | collective-permute-done | bytes 393248 | tf_op jit(solution)/shard_map/ppermute | solution.py:312
  34.0 9.9 %shard_map.77 = (bf16[128,512]{1,0:T(8,128)(2,1)}, bf16[128,128]{1,0:T(8,128)(2,1)S(1)}) custom-call(s32[2]{0:T(128)S(1)} %pad_add_fusion.sc_ref, bf16[128,512]{1,0:T(8,128)(2,1)S(1)} %bitcast.36, bf16[128,512]{1,0:T(8,128)(2,1)S(1)} %bitcast.41, bf16[128,512]{1,0:T(8,128)(2,1)S(1)} %bitcast.46, bf16[128,512]{1,0:T(8,128)(2,1)S(1)} %bitcast.51, ...), custom_call_target="tpu_custom_call" | custom-call | flops 536870912 | bytes 4194304 | tf_op jit(solution)/shard_map/pallas_call | solution.py:330
  44.0 0.0 collective-permute-start.7
  44.0 0.7 %collective-permute-start.6 = (bf16[2,192,512]{2,1,0:T(8,128)(2,1)S(1)}, bf16[2,192,512]{2,1,0:T(8,128)(2,1)S(1)}, u32[]{:S(2)}, u32[]{:S(2)}) collective-permute-start(bf16[2,192,512]{2,1,0:T(8,128)(2,1)S(1)} %bitcast.66), channel_id=1, source_target_pairs={{0,2},{1,3},{2,0},{3,1},{4,8},{5,9},{6,10},{7,11},{8,4},{9,5},{10,... | collective-permute-start | bytes 1179656 | tf_op jit(solution)/shard_map/ppermute | solution.py:312
  44.7 0.5 collective-permute-done.7
  45.2 2.3 %collective-permute-start.8 = (bf16[128,128]{1,0:T(8,128)(2,1)S(1)}, bf16[128,128]{1,0:T(8,128)(2,1)S(1)}, u32[]{:S(2)}, u32[]{:S(2)}) collective-permute-start(bf16[128,128]{1,0:T(8,128)(2,1)S(1)} %maximum_bitcast_fusion.2), channel_id=1, source_target_pairs={{0,1},{1,2},{2,3},{3,0},{4,7},{5,4},{6,5},{7,6},{8,9},{9,10},{10,1... | collective-permute-start | bytes 98312 | tf_op jit(solution)/shard_map/ppermute | solution.py:312
  47.5 5.8 %collective-permute-done.8.st_lc_ref = bf16[128,128]{1,0:T(8,128)(2,1)S(1)} collective-permute-done((bf16[128,128]{1,0:T(8,128)(2,1)S(1)}, bf16[128,128]{1,0:T(8,128)(2,1)S(1)}, u32[]{:S(2)}, u32[]{:S(2)}) %collective-permute-start.8) | collective-permute-done | bytes 32800 | tf_op jit(solution)/shard_map/ppermute | solution.py:312
  53.3 0.0 collective-permute-start.9
  53.3 1.2 %collective-permute-done.9.st_s2_ref = bf16[128,128]{1,0:T(8,128)(2,1)S(1)} collective-permute-done((bf16[128,128]{1,0:T(8,128)(2,1)S(1)}, bf16[128,128]{1,0:T(8,128)(2,1)S(1)}, u32[]{:S(2)}, u32[]{:S(2)}) %collective-permute-start.9) | collective-permute-done | bytes 32800 | tf_op jit(solution)/shard_map/ppermute | solution.py:312
  54.5 5.0 %collective-permute-start.10 = (bf16[192,128]{1,0:T(8,128)(2,1)S(1)}, bf16[192,128]{1,0:T(8,128)(2,1)S(1)}, u32[]{:S(2)}, u32[]{:S(2)}) collective-permute-start(bf16[192,128]{1,0:T(8,128)(2,1)S(1)} %bitcast.68), channel_id=1, source_target_pairs={{0,2},{1,3},{2,0},{3,1},{4,8},{5,9},{6,10},{7,11},{8,4},{9,5},{10,... | collective-permute-start | bytes 147464 | tf_op jit(solution)/shard_map/ppermute | solution.py:312
  59.6 0.0 collective-permute-done.6.off_ref
  59.6 2.1 %collective-permute-done.10.st_off_ref = bf16[192,128]{1,0:T(8,128)(2,1)S(1)} collective-permute-done((bf16[192,128]{1,0:T(8,128)(2,1)S(1)}, bf16[192,128]{1,0:T(8,128)(2,1)S(1)}, u32[]{:S(2)}, u32[]{:S(2)}) %collective-permute-start.10) | collective-permute-done | bytes 49184 | tf_op jit(solution)/shard_map/ppermute | solution.py:312
  61.7 6.1 %shard_map.78 = (bf16[128,512]{1,0:T(8,128)(2,1)}, bf16[128,512]{1,0:T(8,128)(2,1)}) custom-call(s32[2]{0:T(128)S(1)} %pad_add_fusion.sc_ref, bf16[128,512]{1,0:T(8,128)(2,1)S(1)} %bitcast.37, bf16[128,512]{1,0:T(8,128)(2,1)S(1)} %bitcast.42, bf16[128,512]{1,0:T(8,128)(2,1)S(1)} %bitcast.47, bf16[128,512]{1,0:T(8,128)(2,1)S(1)} %bitcast.52, ...), custom_call_target="tpu_custom_call" | custom-call | flops 536870912 | bytes 4194304 | tf_op jit(solution)/shard_map/pallas_call | solution.py:340
  (18 shorter events, 0.3 us)
Async XLA Ops:
  1.8 2.1 %collective-permute-start = (bf16[4,8,16,512]{3,2,1,0:T(8,128)(2,1)S(1)}, bf16[4,8,16,512]{3,2,1,0:T(8,128)(2,1)S(1)}, u32[]{:S(2)}, u32[]{:S(2)}) collective-permute-start(bf16[4,8,16,512]{3,2,1,0:T(8,128)(2,1)S(1)} %pad_maximum_fusion), channel_id=1, source_target_pairs={{0,4},{1,5},{2,6},{3,7},{4,0},{5,1},{6,2},{7,3},{8,12},{9,13},{10,... | collective-permute-start | bytes 1572872 | tf_op jit(solution)/shard_map/ppermute | solution.py:312
  2.3 1.6 %copy-start = (bf16[8,16,512]{2,1,0:T(8,128)(2,1)S(1)}, bf16[8,16,512]{2,1,0:T(8,128)(2,1)}, u32[]{:S(2)}) copy-start(bf16[8,16,512]{2,1,0:T(8,128)(2,1)} %param.5) | copy-start | bytes 393220
  2.3 1.6 %copy-start.1 = (bf16[8,16,512]{2,1,0:T(8,128)(2,1)S(1)}, bf16[8,16,512]{2,1,0:T(8,128)(2,1)}, u32[]{:S(2)}) copy-start(bf16[8,16,512]{2,1,0:T(8,128)(2,1)} %param.6) | copy-start | bytes 393220
  2.3 1.6 %copy-start.2 = (bf16[8,16,512]{2,1,0:T(8,128)(2,1)S(1)}, bf16[8,16,512]{2,1,0:T(8,128)(2,1)}, u32[]{:S(2)}) copy-start(bf16[8,16,512]{2,1,0:T(8,128)(2,1)} %param.7) | copy-start | bytes 393220
  2.3 1.6 %copy-start.3 = (bf16[8,16,512]{2,1,0:T(8,128)(2,1)S(1)}, bf16[8,16,512]{2,1,0:T(8,128)(2,1)}, u32[]{:S(2)}) copy-start(bf16[8,16,512]{2,1,0:T(8,128)(2,1)} %param.8) | copy-start | bytes 393220
  4.1 12.1 %collective-permute-start.1 = (bf16[2,128,512]{2,1,0:T(8,128)(2,1)S(1)}, bf16[2,128,512]{2,1,0:T(8,128)(2,1)S(1)}, u32[]{:S(2)}, u32[]{:S(2)}) collective-permute-start(bf16[2,128,512]{2,1,0:T(8,128)(2,1)S(1)} %maximum_bitcast_fusion), channel_id=1, source_target_pairs={{0,1},{1,2},{2,3},{3,0},{4,7},{5,4},{6,5},{7,6},{8,9},{9,10},{10,1... | collective-permute-start | bytes 786440 | tf_op jit(solution)/shard_map/ppermute | solution.py:312
  7.1 14.4 %collective-permute-start.4 = (bf16[2,128,512]{2,1,0:T(8,128)(2,1)S(1)}, bf16[2,128,512]{2,1,0:T(8,128)(2,1)S(1)}, u32[]{:S(2)}, u32[]{:S(2)}) collective-permute-start(bf16[2,128,512]{2,1,0:T(8,128)(2,1)S(1)} %maximum_bitcast_fusion.1), channel_id=1, source_target_pairs={{0,1},{1,2},{2,3},{3,0},{4,7},{5,4},{6,5},{7,6},{8,9},{9,10},{10,1... | collective-permute-start | bytes 786440 | tf_op jit(solution)/shard_map/ppermute | solution.py:312
  16.2 5.3 %collective-permute-start.2 = (bf16[2,128,512]{2,1,0:T(8,128)(2,1)S(1)}, bf16[2,128,512]{2,1,0:T(8,128)(2,1)S(1)}, u32[]{:S(2)}, u32[]{:S(2)}) collective-permute-start(bf16[2,128,512]{2,1,0:T(8,128)(2,1)S(1)} %collective-permute-done.1.lc_ref), channel_id=1, source_target_pairs={{0,4},{1,5},{2,6},{3,7},{4,0},{5,1},{6,2},{7,3},{8,12},{9,13},{10,... | collective-permute-start | bytes 786440 | tf_op jit(solution)/shard_map/ppermute | solution.py:312
  21.5 3.2 %collective-permute-start.5 = (bf16[2,128,512]{2,1,0:T(8,128)(2,1)S(1)}, bf16[2,128,512]{2,1,0:T(8,128)(2,1)S(1)}, u32[]{:S(2)}, u32[]{:S(2)}) collective-permute-start(bf16[2,128,512]{2,1,0:T(8,128)(2,1)S(1)} %collective-permute-done.4.lc_ref), channel_id=1, source_target_pairs={{0,4},{1,5},{2,6},{3,7},{4,0},{5,1},{6,2},{7,3},{8,12},{9,13},{10,... | collective-permute-start | bytes 786440 | tf_op jit(solution)/shard_map/ppermute | solution.py:312
  21.6 12.4 %collective-permute-start.3 = (bf16[2,192,512]{2,1,0:T(8,128)(2,1)S(1)}, bf16[2,192,512]{2,1,0:T(8,128)(2,1)S(1)}, u32[]{:S(2)}, u32[]{:S(2)}) collective-permute-start(bf16[2,192,512]{2,1,0:T(8,128)(2,1)S(1)} %bitcast.67), channel_id=1, source_target_pairs={{0,2},{1,3},{2,0},{3,1},{4,8},{5,9},{6,10},{7,11},{8,4},{9,5},{10,... | collective-permute-start | bytes 1179656 | tf_op jit(solution)/shard_map/ppermute | solution.py:312
  23.1 0.7 %copy-start.4 = (s32[2,64]{1,0:T(2,128)S(1)}, s32[2,64]{1,0:T(2,128)}, u32[]{:S(2)}) copy-start(s32[2,64]{1,0:T(2,128)} %param.9) | copy-start | bytes 1540
  44.0 1.2 %collective-permute-start.7 = (bf16[8,16,128]{2,1,0:T(8,128)(2,1)S(1)}, bf16[8,16,128]{2,1,0:T(8,128)(2,1)S(1)}, u32[]{:S(2)}, u32[]{:S(2)}) collective-permute-start(bf16[8,16,128]{2,1,0:T(8,128)(2,1)S(1)} %bitcast.59), channel_id=1, source_target_pairs={{0,4},{1,5},{2,6},{3,7},{4,0},{5,1},{6,2},{7,3},{8,12},{9,13},{10,... | collective-permute-start | bytes 98312 | tf_op jit(solution)/shard_map/ppermute | solution.py:312
  44.0 15.6 %collective-permute-start.6 = (bf16[2,192,512]{2,1,0:T(8,128)(2,1)S(1)}, bf16[2,192,512]{2,1,0:T(8,128)(2,1)S(1)}, u32[]{:S(2)}, u32[]{:S(2)}) collective-permute-start(bf16[2,192,512]{2,1,0:T(8,128)(2,1)S(1)} %bitcast.66), channel_id=1, source_target_pairs={{0,2},{1,3},{2,0},{3,1},{4,8},{5,9},{6,10},{7,11},{8,4},{9,5},{10,... | collective-permute-start | bytes 1179656 | tf_op jit(solution)/shard_map/ppermute | solution.py:312
  45.2 8.1 %collective-permute-start.8 = (bf16[128,128]{1,0:T(8,128)(2,1)S(1)}, bf16[128,128]{1,0:T(8,128)(2,1)S(1)}, u32[]{:S(2)}, u32[]{:S(2)}) collective-permute-start(bf16[128,128]{1,0:T(8,128)(2,1)S(1)} %maximum_bitcast_fusion.2), channel_id=1, source_target_pairs={{0,1},{1,2},{2,3},{3,0},{4,7},{5,4},{6,5},{7,6},{8,9},{9,10},{10,1... | collective-permute-start | bytes 98312 | tf_op jit(solution)/shard_map/ppermute | solution.py:312
  53.3 1.2 %collective-permute-start.9 = (bf16[128,128]{1,0:T(8,128)(2,1)S(1)}, bf16[128,128]{1,0:T(8,128)(2,1)S(1)}, u32[]{:S(2)}, u32[]{:S(2)}) collective-permute-start(bf16[128,128]{1,0:T(8,128)(2,1)S(1)} %collective-permute-done.8.st_lc_ref), channel_id=1, source_target_pairs={{0,4},{1,5},{2,6},{3,7},{4,0},{5,1},{6,2},{7,3},{8,12},{9,13},{10,... | collective-permute-start | bytes 98312 | tf_op jit(solution)/shard_map/ppermute | solution.py:312
  54.5 7.1 %collective-permute-start.10 = (bf16[192,128]{1,0:T(8,128)(2,1)S(1)}, bf16[192,128]{1,0:T(8,128)(2,1)S(1)}, u32[]{:S(2)}, u32[]{:S(2)}) collective-permute-start(bf16[192,128]{1,0:T(8,128)(2,1)S(1)} %bitcast.68), channel_id=1, source_target_pairs={{0,2},{1,3},{2,0},{3,1},{4,8},{5,9},{6,10},{7,11},{8,4},{9,5},{10,... | collective-permute-start | bytes 147464 | tf_op jit(solution)/shard_map/ppermute | solution.py:312

commit v2 on v1

v2 whole, which is shorter than its diff:
```python
import functools
import math

import jax
import jax.numpy as jnp
from jax import lax
from jax.experimental import pallas as pl
from jax.experimental.pallas import tpu as pltpu
from jax.sharding import PartitionSpec as P

HEAD_DIM = 32
RADIUS = 6
STRIP = 8
LANES = 128
NEG = -1e30
LOG2E = 1.4426950408889634


def routes(lat_count, lon_count):
    half = lon_count // 2
    pair, around, across = [], [], []
    for i in range(lat_count):
        for j in range(lon_count):
            me = i * lon_count + j
            pair.append((me, (i ^ 1) * lon_count + j))
            step = 1 if i % 2 == 0 else -1
            around.append((me, i * lon_count + (j + step) % lon_count))
            other = i - 1 if i % 2 == 0 else i + 1
            if 0 <= other < lat_count:
                across.append((me, other * lon_count + j))
            else:
                across.append((me, i * lon_count + (j + half) % lon_count))
    return pair, around, across


def sizes(rows, cols):
    own, strip, off = rows * cols, 2 * rows * STRIP, RADIUS * (cols + 2 * STRIP)
    return own, own, strip, strip, off


def mask_kernel(rows, cols, lat_count, lon_count, sc_ref, reach_ref, reach_t_ref, out_ref, out_t_ref):
    lat, lon = sc_ref[0], sc_ref[1]
    total_rows, total_cols = rows * lat_count, cols * lon_count
    half = total_cols // 2
    odd = lax.rem(lat, 2)
    row0, col0 = lat * rows, lon * cols
    own, oth, strip, _, off = sizes(rows, cols)
    outer = own + 2 * strip + oth + off
    t = lax.broadcasted_iota(jnp.int32, (1, outer), 1)
    is_north, is_south = lat == 0, lat == lat_count - 1
    sender_odd = jnp.where(is_north | is_south, odd, 1 - odd)

    def split(index, width):
        shift = width.bit_length() - 1
        return lax.shift_right_logical(index, shift), index & (width - 1)

    r_own, c_own = split(t, cols)
    u = t - own
    r_oth, c_oth = split(u, cols)
    r_oth = r_oth + jnp.where(odd == 0, rows, -rows)
    first = jnp.where(odd == 0, 0, -rows)
    u = t - (own + oth)
    r_a, c_a = split(u, STRIP)
    r_a, c_a = r_a + first, c_a + jnp.where(odd == 0, -STRIP, cols)
    u = t - (own + oth + strip)
    r_b, c_b = split(u, STRIP)
    r_b, c_b = r_b + first, c_b + jnp.where(odd == 0, cols, -STRIP)
    u = t - (own + oth + 2 * strip)
    width = cols + 2 * STRIP
    r_off, x = split(u, width)
    r_off = jnp.where(
        is_north & (odd == 0),
        -1 - r_off,
        jnp.where(
            is_south & (odd == 1),
            rows + RADIUS - 1 - r_off,
            r_off + jnp.where(odd == 0, -RADIUS, rows),
        ),
    )
    first_at = jnp.where(sender_odd == 0, -STRIP, cols)
    second_at = jnp.where(sender_odd == 0, cols, -STRIP)
    c_off = jnp.where(
        x < cols, x, jnp.where(x < cols + STRIP, x - cols + first_at, x - cols - STRIP + second_at)
    )
    at = [own, own + oth, own + oth + strip, own + oth + 2 * strip]
    r_key = jnp.where(
        t < at[0],
        r_own,
        jnp.where(t < at[1], r_oth, jnp.where(t < at[2], r_a, jnp.where(t < at[3], r_b, r_off))),
    )
    c_key = jnp.where(
        t < at[0],
        c_own,
        jnp.where(t < at[1], c_oth, jnp.where(t < at[2], c_a, jnp.where(t < at[3], c_b, c_off))),
    )
    g_key = r_key + row0
    turned = lax.rem(c_key + (col0 + half + total_cols), total_cols)
    pick = lax.broadcasted_iota(jnp.int32, (total_cols, outer), 0) == turned
    north_key = jnp.sum(jnp.where(pick, reach_t_ref[:, 0:1], 0.0), axis=0, keepdims=True)
    south_key = jnp.sum(jnp.where(pick, reach_t_ref[:, 1:2], 0.0), axis=0, keepdims=True)
    g_f = g_key.astype(jnp.float32)
    behind_n = g_key < 0
    behind_s = g_key >= total_rows
    spare = jnp.where(
        behind_n, north_key + 1.0 + g_f, jnp.where(behind_s, south_key + total_rows - g_f, 1.0)
    )
    valid = jnp.where(spare > 0.5, 1.0, 0.0)
    n = lax.broadcasted_iota(jnp.int32, (own, 1), 0)
    r_n, c_n = split(n, cols)
    pick_n = lax.broadcasted_iota(jnp.int32, (own, total_cols), 1) == (c_n + col0)
    north_n = jnp.sum(jnp.where(pick_n, reach_ref[0:1, :], 0.0), axis=1, keepdims=True)
    south_n = jnp.sum(jnp.where(pick_n, reach_ref[1:2, :], 0.0), axis=1, keepdims=True)
    g_n = (r_n + row0).astype(jnp.float32)
    north_ok = jnp.where(north_n > g_n, 1.0, 0.0)
    south_ok = jnp.where(south_n > total_rows - 1 - g_n, 1.0, 0.0)
    need_n = jnp.where(behind_n, 1.0, 0.0)
    need_s = jnp.where(behind_s, 1.0, 0.0)
    near = (jnp.abs(r_key - r_n) <= RADIUS) & (jnp.abs(c_key - c_n) <= RADIUS)
    ok = jnp.where(near, 1.0, 0.0) * valid
    ok = jnp.where(need_n > north_ok, 0.0, ok)
    ok = jnp.where(need_s > south_ok, 0.0, ok)
    bias = jnp.where(ok > 0.5, 0.0, NEG)
    out_ref[...] = bias
    out_t_ref[...] = bias.T


def assemble(target, *pieces):
    at = 0
    for piece in pieces:
        target[at : at + piece.shape[0]] = piece[...]
        at += piece.shape[0]


NT = (((1,), (1,)), ((), ()))
SCALE = 1.0 / math.sqrt(HEAD_DIM)


def lanes_of(shape, j):
    lane = lax.broadcasted_iota(jnp.int32, shape, 1)
    return (lane >= j * HEAD_DIM) & (lane < (j + 1) * HEAD_DIM)


def spread(x):
    per = LANES // HEAD_DIM
    return jnp.concatenate(
        [jnp.where(lanes_of(x.shape, j), x, jnp.zeros_like(x)) for j in range(per)], axis=0
    )


def gather(x):
    per = LANES // HEAD_DIM
    count = x.shape[0] // per
    total = x[0:count]
    for j in range(1, per):
        total = jnp.where(lanes_of((count, LANES), j), x[j * count : (j + 1) * count], total)
    return total


def part(x, j, axis):
    count = x.shape[axis] // (LANES // HEAD_DIM)
    return lax.slice_in_dim(x, j * count, (j + 1) * count, axis=axis)


def groups(width):
    for g in range(width // LANES):
        yield slice(g * LANES, (g + 1) * LANES), g * (LANES // HEAD_DIM)


def dot_nt(a, b):
    return lax.dot_general(a, b, NT, preferred_element_type=jnp.float32)


def partial_stats(q_ref, g_ref, keys, values, bias, top_ref, sum_ref, dot_ref):
    for at, first in groups(q_ref.shape[1]):
        s_all = dot_nt(keys[:, at], spread(q_ref[:, at]))
        gp_all = dot_nt(values[:, at], spread(g_ref[:, at]))
        for j in range(LANES // HEAD_DIM):
            s, gp = part(s_all, j, 1) * (SCALE * LOG2E) + bias, part(gp_all, j, 1)
            top = jnp.max(s, axis=0, keepdims=True)
            e = jnp.exp2(s - top)
            h = first + j
            top_ref[h : h + 1, :] = top
            sum_ref[h : h + 1, :] = jnp.sum(e, axis=0, keepdims=True)
            dot_ref[h : h + 1, :] = jnp.sum(e * gp, axis=0, keepdims=True)


def near_stats_kernel(
    q_ref, g_ref, k_ref, v_ref, k_oth, v_oth, lc_ref, s2_ref, bias_ref,
    kall_ref, vall_ref, top_ref, sum_ref, dot_ref,
):
    assemble(kall_ref, k_ref, k_oth, lc_ref.at[0], s2_ref.at[0])
    assemble(vall_ref, v_ref, v_oth, lc_ref.at[1], s2_ref.at[1])
    near = kall_ref.shape[0]
    partial_stats(
        q_ref, g_ref, kall_ref, vall_ref, bias_ref[0:near, :], top_ref, sum_ref, dot_ref
    )


def far_stats_kernel(
    q_ref, g_ref, off_ref, bias_ref, top_ref, sum_ref, dot_ref, st_ref, top2, sum2, dot2
):
    near = bias_ref.shape[0] - off_ref.shape[1]
    partial_stats(
        q_ref, g_ref, off_ref.at[0], off_ref.at[1], bias_ref[near:, :], top2, sum2, dot2
    )
    top = jnp.maximum(top_ref[...], top2[...])
    a, b = jnp.exp2(top_ref[...] - top), jnp.exp2(top2[...] - top)
    total = sum_ref[...] * a + sum2[...] * b
    log_total = top + jnp.log2(total)
    dot = (dot_ref[...] * a + dot2[...] * b) / total
    terms = []
    for x in (log_total, dot):
        high = x.astype(jnp.bfloat16).astype(jnp.float32)
        mid = (x - high).astype(jnp.bfloat16).astype(jnp.float32)
        terms += [high, mid, x - high - mid]
    count = sum(x.shape[0] for x in terms)
    terms.append(jnp.zeros((LANES - count, top.shape[1]), jnp.float32))
    st_ref[...] = jnp.concatenate(terms, axis=0).T.astype(jnp.bfloat16)


def query_kernel(q_ref, g_ref, kall_ref, vall_ref, off_ref, bias_ref, st_ref, dq_ref):
    heads = q_ref.shape[1] // HEAD_DIM
    near = kall_ref.shape[0]
    row = lax.broadcasted_iota(jnp.int32, (LANES, LANES), 0)

    def stat_of(h):
        choose = (row == h) | (row == h + heads) | (row == h + 2 * heads)
        choose = jnp.where(choose, 1.0, 0.0).astype(jnp.bfloat16)
        return jnp.dot(st_ref[...], choose, preferred_element_type=jnp.float32)

    def wide(x, count):
        return jnp.concatenate([x] * -(-count // LANES), axis=1)[:, :count]

    per = LANES // HEAD_DIM
    for at, first in groups(q_ref.shape[1]):
        sides = (
            (kall_ref[:, at], vall_ref[:, at], bias_ref[:, 0:near]),
            (off_ref[0, :, at], off_ref[1, :, at], bias_ref[:, near:]),
        )
        qs, gs = spread(q_ref[:, at]), spread(g_ref[:, at])
        logs = [stat_of(first + j) for j in range(per)]
        dots = [stat_of(first + j + 3 * heads) for j in range(per)]
        total = jnp.zeros((q_ref.shape[0], LANES), jnp.float32)
        for kg, vg, bias in sides:
            count = kg.shape[0]
            s, gp = dot_nt(qs, kg), dot_nt(gs, vg)
            ds = []
            for j in range(per):
                p = jnp.exp2(part(s, j, 0) * (SCALE * LOG2E) + (bias - wide(logs[j], count)))
                ds.append((p * (part(gp, j, 0) - wide(dots[j], count))).astype(jnp.bfloat16))
            ds = jnp.concatenate(ds, axis=0)
            total += gather(jnp.dot(ds, kg, preferred_element_type=jnp.float32))
        dq_ref[:, at] = (total * SCALE).astype(jnp.bfloat16)


def key_sums(k_ref, v_ref, queries, grads, stats, bias, stat_rows, finish):
    heads = k_ref.shape[1] // HEAD_DIM
    row = lax.broadcasted_iota(jnp.int32, (2 * heads, LANES), 0)
    col = lax.broadcasted_iota(jnp.int32, (2 * heads, LANES), 1)
    base = jnp.where(row < heads, row, row + 2 * heads)
    choose = (col == base) | (col == base + heads) | (col == base + 2 * heads)
    choose = jnp.where(choose, 1.0, 0.0).astype(jnp.bfloat16)
    stat_rows[...] = dot_nt(choose, stats[...])
    for at, first in groups(k_ref.shape[1]):
        qg, gg = queries[:, at], grads[:, at]
        s, gp = dot_nt(spread(k_ref[:, at]), qg), dot_nt(spread(v_ref[:, at]), gg)
        p_half, ds = [], []
        for j in range(LANES // HEAD_DIM):
            h = first + j
            log_total, dot = stat_rows[h : h + 1, :], stat_rows[h + heads : h + heads + 1, :]
            p = jnp.exp2(part(s, j, 0) * (SCALE * LOG2E) + (bias - log_total))
            p_half.append(p.astype(jnp.bfloat16))
            ds.append((p * (part(gp, j, 0) - dot)).astype(jnp.bfloat16))
        dv = jnp.dot(jnp.concatenate(p_half, axis=0), gg, preferred_element_type=jnp.float32)
        dk = jnp.dot(jnp.concatenate(ds, axis=0), qg, preferred_element_type=jnp.float32)
        finish(at, gather(dk), gather(dv))


def near_key_kernel(
    k_ref, v_ref, q_ref, g_ref, q_oth, g_oth, lc_ref, s2_ref,
    st_ref, st_oth, st_lc, st_s2, bias_ref, dk_ref, dv_ref, qall, gall, stall, stat_rows,
):
    assemble(qall, q_ref, q_oth, lc_ref.at[0], s2_ref.at[0])
    assemble(gall, g_ref, g_oth, lc_ref.at[1], s2_ref.at[1])
    assemble(stall, st_ref, st_oth, st_lc, st_s2)
    near = qall.shape[0]

    def finish(at, dk, dv):
        dk_ref[:, at], dv_ref[:, at] = dk, dv

    key_sums(k_ref, v_ref, qall, gall, stall, bias_ref[:, 0:near], stat_rows, finish)


def far_key_kernel(
    k_ref, v_ref, off_ref, st_off, bias_ref, dk_in, dv_in, dk_ref, dv_ref, stat_rows
):
    near = bias_ref.shape[1] - off_ref.shape[1]

    def finish(at, dk, dv):
        dk_ref[:, at] = ((dk_in[:, at] + dk) * SCALE).astype(jnp.bfloat16)
        dv_ref[:, at] = (dv_in[:, at] + dv).astype(jnp.bfloat16)

    key_sums(
        k_ref, v_ref, off_ref.at[0], off_ref.at[1], st_off, bias_ref[:, near:], stat_rows, finish
    )


def shards(lat_count, lon_count, query, key, value, grad, pole_reach):
    rows, cols, width = query.shape
    lat, lon = lax.axis_index("lat"), lax.axis_index("lon")
    odd = lax.rem(lat, 2)
    even = odd == 0
    pair, around, across = routes(lat_count, lon_count)
    axes = ("lat", "lon")
    n_own, n_oth, n_strip, _, n_off = sizes(rows, cols)
    near = n_own + n_oth + 2 * n_strip
    outer = near + n_off
    place = jnp.stack([lat, lon]).astype(jnp.int32)

    smem = pl.BlockSpec(memory_space=pltpu.SMEM)
    vmem = pl.BlockSpec(memory_space=pltpu.VMEM)

    def call(body, outs, operands, scratch=(), flops=1 << 28, scalars=False):
        return pl.pallas_call(
            body,
            out_shape=outs,
            in_specs=[smem] * scalars + [vmem] * (len(operands) - scalars),
            out_specs=jax.tree.map(lambda _: vmem, outs),
            scratch_shapes=scratch,
            compiler_params=pltpu.CompilerParams(vmem_limit_bytes=32 << 20),
            cost_estimate=pl.CostEstimate(flops=flops, bytes_accessed=4 << 20, transcendentals=0),
        )(*operands)

    def array(*shape, dtype=jnp.bfloat16):
        return jax.ShapeDtypeStruct(shape, dtype)

    f32 = jnp.float32
    heads = width // HEAD_DIM
    reach = pole_reach.astype(f32)
    bias, bias_t = call(
        functools.partial(mask_kernel, rows, cols, lat_count, lon_count),
        (array(n_own, outer, dtype=f32), array(outer, n_own, dtype=f32)),
        (place, reach, reach.T),
        scalars=True,
    )

    def strip_of(mine, other):
        at = jnp.where(even, cols - STRIP, 0)
        mine = lax.dynamic_slice_in_dim(mine, at, STRIP, 1)
        other = lax.dynamic_slice_in_dim(other, at, STRIP, 1)
        top, low = jnp.where(even, mine, other), jnp.where(even, other, mine)
        return jnp.concatenate([top, low], axis=0).reshape(2 * rows * STRIP, -1)

    def edge_of(mine, first, second):
        parts = [lax.dynamic_slice_in_dim(mine, jnp.where(even, 0, rows - RADIUS), RADIUS, 0)]
        for piece in (first, second):
            piece = piece.reshape(2 * rows, STRIP, -1)
            parts.append(
                lax.dynamic_slice_in_dim(piece, jnp.where(even, 0, 2 * rows - RADIUS), RADIUS, 0)
            )
        return jnp.concatenate(parts, axis=1).reshape(n_off, -1)

    def send(block, route):
        return lax.ppermute(block, axes, route)

    def stacked(parts):
        return jnp.stack(parts) if len(parts) > 1 else parts[0]

    def strips(mine, other):
        return stacked([strip_of(a, b) for a, b in zip(mine, other)])

    def edges(mine, first, second):
        if len(mine) == 1:
            return edge_of(mine[0], first, second)
        return jnp.stack([edge_of(a, first[i], second[i]) for i, a in enumerate(mine)])

    def flat(field):
        return field.reshape(n_own, field.shape[-1])

    key_o, value_o = send(key, pair), send(value, pair)
    kv, kv_o = (key, value), (key_o, value_o)
    kv_1 = send(strips(kv, kv_o), around)
    kv_2 = send(kv_1, pair)
    kv_off = send(edges(kv, kv_1, kv_2), across)

    query_s, grad_s, _ = lax.optimization_barrier((query, grad, key_o))
    query_o, grad_o = send(query_s, pair), send(grad_s, pair)
    qg, qg_o = (query, grad), (query_o, grad_o)
    qg_1 = send(strips(qg, qg_o), around)

    q, k, v, g = (flat(x) for x in (query, key, value, grad))
    stat = array(heads, n_own, dtype=f32)
    kall, vall, *near_stats = call(
        near_stats_kernel,
        (array(near, width), array(near, width), stat, stat, stat),
        (q, g, k, v, flat(key_o), flat(value_o), kv_1, kv_2, bias_t),
    )
    stats = call(
        far_stats_kernel,
        array(n_own, LANES),
        (q, g, kv_off, bias_t, *near_stats),
        [pltpu.VMEM((heads, n_own), f32)] * 3,
    )
    stats_grid = stats.reshape(rows, cols, LANES)
    stats_o = send(stats_grid, pair)
    st_1 = send(strip_of(stats_grid, stats_o), around)
    d_query = call(query_kernel, array(n_own, width), (q, g, kall, vall, kv_off, bias, stats))
    st_1, d_query = lax.optimization_barrier((st_1, d_query))
    st_2 = send(st_1, pair)
    st_off = send(edge_of(stats_grid, st_1, st_2), across)

    qg_1, _ = lax.optimization_barrier((qg_1, stats_o))
    qg_2 = send(qg_1, pair)
    qg_off = send(edges(qg, qg_1, qg_2), across)

    sums = array(n_own, width, dtype=f32)
    d_key, d_value = call(
        near_key_kernel,
        (sums, sums),
        (
            k, v, q, g, flat(query_o), flat(grad_o), qg_1, qg_2,
            stats, flat(stats_o), st_1, st_2, bias,
        ),
        [
            pltpu.VMEM((near, width), jnp.bfloat16),
            pltpu.VMEM((near, width), jnp.bfloat16),
            pltpu.VMEM((near, LANES), jnp.bfloat16),
            pltpu.VMEM((2 * heads, near), f32),
        ],
    )
    d_key, d_value = call(
        far_key_kernel,
        (array(n_own, width), array(n_own, width)),
        (k, v, qg_off, st_off, bias, d_key, d_value),
        [pltpu.VMEM((2 * heads, n_off), f32)],
    )
    shape = (rows, cols, width)
    return d_query.reshape(shape), d_key.reshape(shape), d_value.reshape(shape)


def solution(mesh):
    field = P("lat", "lon", None)
    return jax.shard_map(
        functools.partial(shards, mesh.shape["lat"], mesh.shape["lon"]),
        mesh=mesh,
        in_specs=(field, field, field, field, P()),
        out_specs=(field, field, field),
        check_vma=False,
    )
```

time: 68 us -> 55 us (0.81)
  waiting for transfers between devices: 33.1 us -> 26.4 us
  Pallas kernels: 16.9 us -> 12 us
  starting transfers between devices: 14.7 us -> 11.4 us
  local copies, waits for them, and re-layouts: 0.81 us -> 2.71 us
    ppermute x11 -> x14, waiting for transfers between devices: 33.1 us -> 26.4 us  [send(): return lax.ppermute(block, axes, route)]
    pallas_call x3 -> x6, Pallas kernels: 16.9 us -> 12 us  [call(): pl.pallas_call(body, out_shape=outs, in_specs=[smem] * scalars + [vmem] *...]
    ppermute x11 -> x14, starting transfers between devices: 14.7 us -> 11.4 us  [send(): return lax.ppermute(block, axes, route)]
    another operation x3 -> x7, other arithmetic: 1.21 us -> 0.19 us  [the longest x5 0.11 us: stacked(): return jnp.stack(parts) if len(parts) > 1 else parts[0]]
    dynamic_slice x1 -> x4, local copies, waits for them, and re-layouts: 0.01 us -> 0.95 us  [edge_of(): lax.dynamic_slice_in_dim(mine, jnp.where(even, 0, rows - RADIUS), RADIUS, 0)]
    unnamed x10, local copies, waits for them, and re-layouts: 0.62 us -> 1.49 us
    select_n x2 -> x4, other arithmetic: 0.14 us -> 0.97 us  [strip_of(): top, low = (jnp.where(even, mine, other), jnp.where(even, other, mine))]
  transfers between devices with their start and end apart: 11 -> 14, of which waited for: 8 -> 10; matrix products, arithmetic and copies ran while one was open for 1% -> 3% of each run, Pallas kernels for 1% -> 18%
where the time goes in v2:
time: 55 us; the launch traced here: 54.7 us
  waiting for transfers between devices  26.4 us (48%)
  Pallas kernels  12 us (22%)
  starting transfers between devices  11.4 us (21%)
  local copies, waits for them, and re-layouts  2.71 us (5%)
  other arithmetic  1.31 us (2%)
  between operations  0.94 us (2%)
    ppermute x14, waiting for transfers between devices, send(): return lax.ppermute(block, axes, route)  26.4 us
    pallas_call x6, Pallas kernels, call(): pl.pallas_call(body, out_shape=outs, in_specs=[smem] * scalars + [vmem] *...  12 us
    ppermute x14, starting transfers between devices, send(): return lax.ppermute(block, axes, route)  11.4 us
    unnamed x10, local copies, waits for them, and re-layouts  1.49 us
  transfers between devices with their start and end apart: 14, of which 10 were waited for; matrix products, arithmetic and copies ran while one was open for 3% of the time, Pallas kernels for 18%

profile of v2, /device:TPU:0, one launch (start us, length us, event | category | flops | bytes accessed | tf_op | source)
XLA Modules:
  0.0 54.7 jit_solution(11857431811396150387)
XLA Ops:
  0.6 0.0 copy-start.2
  0.6 0.5 collective-permute-start
  1.2 0.1 collective-permute-start.1
  1.2 0.9 %constant_dynamic-slice_fusion.14 = bf16[6,16,512]{2,1,0:T(8,128)(2,1)S(1)} fusion(bf16[8,16,512]{2,1,0:T(8,128)(2,1)} %param.6, s32[]{:T(128)S(6)} %select_n.101), kind=kLoop, calls=%fused_computation.46 | loop fusion | bytes 196612 | tf_op jit(solution)/shard_map/dynamic_slice | solution.py:355
  2.1 0.2 collective-permute-done
  2.4 0.4 collective-permute-done.1
  2.7 0.0 copy-done.2
  2.7 0.9 %broadcast_select_fusion.5 = (bf16[8,8,512]{2,1,0:T(8,128)(2,1)S(1)}, bf16[8,8,512]{2,1,0:T(8,128)(2,1)S(1)}, bf16[8,8,512]{2,1,0:T(8,128)(2,1)S(1)}, bf16[8,8,512]{2,1,0:T(8,128)(2,1)S(1)}) fusion(pred[]{:T(512)S(6)} %eq.3, bf16[8,16,512]{2,1,0:T(8,128)(2,1)S(1)} %collective-permute-done.1, s32[]{:T(128)S(6)} %select_n.103, bf16[8,16,512]{2,1,0:T(8,128)(2,1)} %param.7, ...), kind=kLoop, calls=%fused_computation.25 | loop fusion | flops 131072 | bytes 524293 | tf_op jit(solution)/shard_map/jit(_where)/select_n | solution.py:351
  3.7 0.0 copy-start
  3.7 2.8 %collective-permute-start.2 = (bf16[2,128,512]{2,1,0:T(8,128)(2,1)S(1)}, bf16[2,128,512]{2,1,0:T(8,128)(2,1)S(1)}, u32[]{:S(2)}, u32[]{:S(2)}) collective-permute-start(bf16[2,128,512]{2,1,0:T(8,128)(2,1)S(1)} %pad_maximum_fusion.2), channel_id=1, source_target_pairs={{0,1},{1,2},{2,3},{3,0},{4,7},{5,4},{6,5},{7,6},{8,9},{9,10},{10,1... | collective-permute-start | bytes 786440 | tf_op jit(solution)/shard_map/ppermute | solution.py:364
  6.5 0.0 copy-start.4
  6.5 0.1 pad_add_fusion.sc_ref
  6.6 0.6 %copy-done.4 = s32[2,64]{1,0:T(2,128)S(1)} copy-done((s32[2,64]{1,0:T(2,128)S(1)}, s32[2,64]{1,0:T(2,128)}, u32[]{:S(2)}) %copy-start.4) | copy-done | bytes 536
  7.2 0.1 copy.10
  7.3 0.0 copy-done
  7.3 2.1 %collective-permute-start.7 = (bf16[8,16,512]{2,1,0:T(8,128)(2,1)S(1)}, bf16[8,16,512]{2,1,0:T(8,128)(2,1)S(1)}, u32[]{:S(2)}, u32[]{:S(2)}) collective-permute-start(bf16[8,16,512]{2,1,0:T(8,128)(2,1)S(1)} %copy-done), channel_id=1, source_target_pairs={{0,4},{1,5},{2,6},{3,7},{4,0},{5,1},{6,2},{7,3},{8,12},{9,13},{10,... | collective-permute-start | bytes 393224 | tf_op jit(solution)/shard_map/ppermute | solution.py:364
  9.4 0.0 copy-start.3
  9.4 0.9 %shard_map.76 = (f32[128,704]{1,0:T(8,128)S(1)}, f32[704,128]{1,0:T(8,128)S(1)}) custom-call(s32[2]{0:T(128)S(1)} %pad_add_fusion.sc_ref, f32[2,64]{1,0:T(2,128)S(1)} %convert_element_type.3.reach_ref, f32[64,2]{1,0:T(8,128)S(1)} %bitcast.73), custom_call_target="tpu_custom_call" | custom-call | flops 268435456 | bytes 4194304 | tf_op jit(solution)/shard_map/pallas_call | solution.py:324
  10.4 0.0 copy-done.3
  10.4 0.0 copy-start.1
  10.4 0.9 %copy-done.1 = bf16[8,16,512]{2,1,0:T(8,128)(2,1)S(1)} copy-done((bf16[8,16,512]{2,1,0:T(8,128)(2,1)S(1)}, bf16[8,16,512]{2,1,0:T(8,128)(2,1)}, u32[]{:S(2)}) %copy-start.1) | copy-done | bytes 131096
  11.3 0.0 collective-permute-start.8
  11.3 0.0 collective-permute-done.7
  11.3 4.2 %collective-permute-done.2.lc_ref = bf16[2,128,512]{2,1,0:T(8,128)(2,1)S(1)} collective-permute-done((bf16[2,128,512]{2,1,0:T(8,128)(2,1)S(1)}, bf16[2,128,512]{2,1,0:T(8,128)(2,1)S(1)}, u32[]{:S(2)}, u32[]{:S(2)}) %collective-permute-start.2) | collective-permute-done | bytes 262176 | tf_op jit(solution)/shard_map/ppermute | solution.py:364
  15.5 0.0 collective-permute-start.3
  15.6 1.5 %collective-permute-done.3.s2_ref = bf16[2,128,512]{2,1,0:T(8,128)(2,1)S(1)} collective-permute-done((bf16[2,128,512]{2,1,0:T(8,128)(2,1)S(1)}, bf16[2,128,512]{2,1,0:T(8,128)(2,1)S(1)}, u32[]{:S(2)}, u32[]{:S(2)}) %collective-permute-start.3) | collective-permute-done | bytes 262176 | tf_op jit(solution)/shard_map/ppermute | solution.py:364
  17.2 1.3 %collective-permute-start.4 = (bf16[2,192,512]{2,1,0:T(8,128)(2,1)S(1)}, bf16[2,192,512]{2,1,0:T(8,128)(2,1)S(1)}, u32[]{:S(2)}, u32[]{:S(2)}) collective-permute-start(bf16[2,192,512]{2,1,0:T(8,128)(2,1)S(1)} %pad_maximum_fusion), channel_id=1, source_target_pairs={{0,2},{1,3},{2,0},{3,1},{4,8},{5,9},{6,10},{7,11},{8,4},{9,5},{10,... | collective-permute-start | bytes 1179656 | tf_op jit(solution)/shard_map/ppermute | solution.py:364
  18.5 0.0 collective-permute-done.8
  18.6 1.6 %collective-permute-start.9 = (bf16[2,128,512]{2,1,0:T(8,128)(2,1)S(1)}, bf16[2,128,512]{2,1,0:T(8,128)(2,1)S(1)}, u32[]{:S(2)}, u32[]{:S(2)}) collective-permute-start(bf16[2,128,512]{2,1,0:T(8,128)(2,1)S(1)} %pad_maximum_fusion.3), channel_id=1, source_target_pairs={{0,1},{1,2},{2,3},{3,0},{4,7},{5,4},{6,5},{7,6},{8,9},{9,10},{10,1... | collective-permute-start | bytes 786440 | tf_op jit(solution)/shard_map/ppermute | solution.py:364
  20.2 1.6 %shard_map.77 = (bf16[512,512]{1,0:T(8,128)(2,1)S(1)}, bf16[512,512]{1,0:T(8,128)(2,1)S(1)}, f32[16,128]{1,0:T(8,128)S(1)}, f32[16,128]{1,0:T(8,128)S(1)}, f32[16,128]{1,0:T(8,128)S(1)}) custom-call(bf16[128,512]{1,0:T(8,128)(2,1)S(1)} %bitcast.49, bf16[128,512]{1,0:T(8,128)(2,1)S(1)} %bitcast.53, bf16[128,512]{1,0:T(8,128)(2,1)S(1)} %bitcast.57, ...), custom_call_target="tpu_custom_call" | custom-call | flops 268435456 | bytes 4194304 | tf_op jit(solution)/shard_map/pallas_call | solution.py:324
  21.8 13.2 %collective-permute-done.4.off_ref = bf16[2,192,512]{2,1,0:T(8,128)(2,1)S(1)} collective-permute-done((bf16[2,192,512]{2,1,0:T(8,128)(2,1)S(1)}, bf16[2,192,512]{2,1,0:T(8,128)(2,1)S(1)}, u32[]{:S(2)}, u32[]{:S(2)}) %collective-permute-start.4) | collective-permute-done | bytes 393248 | tf_op jit(solution)/shard_map/ppermute | solution.py:364
  35.1 0.9 %shard_map.78.st_ref = bf16[128,128]{1,0:T(8,128)(2,1)S(1)} custom-call(bf16[128,512]{1,0:T(8,128)(2,1)S(1)} %bitcast.50, bf16[128,512]{1,0:T(8,128)(2,1)S(1)} %bitcast.54, bf16[2,192,512]{2,1,0:T(8,128)(2,1)S(1)} %collective-permute-done.4.off_ref, f32[704,128]{1,0:T(8,128)S(1)} %get-tuple-element.19.bias_ref, f32[16,128]{1,0:T(8,128)S(1)} %get-tuple-element.20.top_ref, ...), custom_call_target="tpu_custom_call" | custom-call | flops 268435456 | bytes 4194304 | tf_op jit(solution)/shard_map/pallas_call | solution.py:324
  36.0 0.1 collective-permute-start.5
  36.1 0.0 collective-permute-done.9.lc_ref
  36.1 1.2 %collective-permute-done.5 = bf16[8,16,128]{2,1,0:T(8,128)(2,1)S(1)} collective-permute-done((bf16[8,16,128]{2,1,0:T(8,128)(2,1)S(1)}, bf16[8,16,128]{2,1,0:T(8,128)(2,1)S(1)}, u32[]{:S(2)}, u32[]{:S(2)}) %collective-permute-start.5) | collective-permute-done | bytes 32800 | tf_op jit(solution)/shard_map/ppermute | solution.py:364
  37.3 0.2 collective-permute-start.10
  37.5 0.1 collective-permute-start.6
  37.6 1.2 %collective-permute-done.10.s2_ref = bf16[2,128,512]{2,1,0:T(8,128)(2,1)S(1)} collective-permute-done((bf16[2,128,512]{2,1,0:T(8,128)(2,1)S(1)}, bf16[2,128,512]{2,1,0:T(8,128)(2,1)S(1)}, u32[]{:S(2)}, u32[]{:S(2)}) %collective-permute-start.10) | collective-permute-done | bytes 262176 | tf_op jit(solution)/shard_map/ppermute | solution.py:364
  38.9 0.1 collective-permute-start.11
  39.0 3.8 %shard_map.79 = bf16[128,512]{1,0:T(8,128)(2,1)} custom-call(bf16[128,512]{1,0:T(8,128)(2,1)S(1)} %bitcast.51, bf16[128,512]{1,0:T(8,128)(2,1)S(1)} %bitcast.55, bf16[512,512]{1,0:T(8,128)(2,1)S(1)} %get-tuple-element.23.kall_ref, bf16[512,512]{1,0:T(8,128)(2,1)S(1)} %get-tuple-element.24.vall_ref, bf16[2,192,512]{2,1,0:T(8,128)(2,1)S(1)} %collective-permute-done.4.off_ref, ...), custom_call_target="tpu_custom_call" | custom-call | flops 268435456 | bytes 4194304 | tf_op jit(solution)/shard_map/pallas_call | solution.py:324
  42.8 0.4 collective-permute-done.6.st_lc
  43.2 0.0 collective-permute-start.12
  43.3 1.2 %collective-permute-done.12.st_s2 = bf16[128,128]{1,0:T(8,128)(2,1)S(1)} collective-permute-done((bf16[128,128]{1,0:T(8,128)(2,1)S(1)}, bf16[128,128]{1,0:T(8,128)(2,1)S(1)}, u32[]{:S(2)}, u32[]{:S(2)}) %collective-permute-start.12) | collective-permute-done | bytes 32800 | tf_op jit(solution)/shard_map/ppermute | solution.py:364
  44.5 2.6 %collective-permute-start.13 = (bf16[192,128]{1,0:T(8,128)(2,1)S(1)}, bf16[192,128]{1,0:T(8,128)(2,1)S(1)}, u32[]{:S(2)}, u32[]{:S(2)}) collective-permute-start(bf16[192,128]{1,0:T(8,128)(2,1)S(1)} %bitcast.79), channel_id=1, source_target_pairs={{0,2},{1,3},{2,0},{3,1},{4,8},{5,9},{6,10},{7,11},{8,4},{9,5},{10,... | collective-permute-start | bytes 147464 | tf_op jit(solution)/shard_map/ppermute | solution.py:364
  47.0 2.7 %shard_map.80 = (f32[128,512]{1,0:T(8,128)S(1)}, f32[128,512]{1,0:T(8,128)S(1)}) custom-call(bf16[128,512]{1,0:T(8,128)(2,1)S(1)} %bitcast.58, bf16[128,512]{1,0:T(8,128)(2,1)S(1)} %bitcast.61, bf16[128,512]{1,0:T(8,128)(2,1)S(1)} %bitcast.52, bf16[128,512]{1,0:T(8,128)(2,1)S(1)} %bitcast.56, bf16[128,512]{1,0:T(8,128)(2,1)S(1)} %bitcast.66, ...), custom_call_target="tpu_custom_call" | custom-call | flops 268435456 | bytes 4194304 | tf_op jit(solution)/shard_map/pallas_call | solution.py:324
  49.8 2.9 %collective-permute-done.13.st_off = bf16[192,128]{1,0:T(8,128)(2,1)S(1)} collective-permute-done((bf16[192,128]{1,0:T(8,128)(2,1)S(1)}, bf16[192,128]{1,0:T(8,128)(2,1)S(1)}, u32[]{:S(2)}, u32[]{:S(2)}) %collective-permute-start.13) | collective-permute-done | bytes 49184 | tf_op jit(solution)/shard_map/ppermute | solution.py:364
  52.7 0.0 collective-permute-done.11.off_ref
  52.7 2.0 %shard_map.81 = (bf16[128,512]{1,0:T(8,128)(2,1)}, bf16[128,512]{1,0:T(8,128)(2,1)}) custom-call(bf16[128,512]{1,0:T(8,128)(2,1)S(1)} %bitcast.59, bf16[128,512]{1,0:T(8,128)(2,1)S(1)} %bitcast.62, bf16[2,192,512]{2,1,0:T(8,128)(2,1)S(1)} %collective-permute-done.11.off_ref, bf16[192,128]{1,0:T(8,128)(2,1)S(1)} %collective-permute-done.13.st_off, ...), custom_call_target="tpu_custom_call" | custom-call | flops 268435456 | bytes 4194304 | tf_op jit(solution)/shard_map/pallas_call | solution.py:324
  (34 shorter events, 0.6 us)
Async XLA Ops:
  0.6 2.1 %copy-start.2 = (bf16[8,16,512]{2,1,0:T(8,128)(2,1)S(1)}, bf16[8,16,512]{2,1,0:T(8,128)(2,1)}, u32[]{:S(2)}) copy-start(bf16[8,16,512]{2,1,0:T(8,128)(2,1)} %param.6) | copy-start | bytes 393220
  0.6 1.7 %collective-permute-start = (bf16[8,16,512]{2,1,0:T(8,128)(2,1)}, bf16[8,16,512]{2,1,0:T(8,128)(2,1)S(1)}, u32[]{:S(2)}, u32[]{:S(2)}) collective-permute-start(bf16[8,16,512]{2,1,0:T(8,128)(2,1)} %param.6), channel_id=1, source_target_pairs={{0,4},{1,5},{2,6},{3,7},{4,0},{5,1},{6,2},{7,3},{8,12},{9,13},{10,... | collective-permute-start | bytes 393224 | tf_op jit(solution)/shard_map/ppermute | solution.py:364
  1.2 1.6 %collective-permute-start.1 = (bf16[8,16,512]{2,1,0:T(8,128)(2,1)}, bf16[8,16,512]{2,1,0:T(8,128)(2,1)S(1)}, u32[]{:S(2)}, u32[]{:S(2)}) collective-permute-start(bf16[8,16,512]{2,1,0:T(8,128)(2,1)} %param.7), channel_id=1, source_target_pairs={{0,4},{1,5},{2,6},{3,7},{4,0},{5,1},{6,2},{7,3},{8,12},{9,13},{10,... | collective-permute-start | bytes 393224 | tf_op jit(solution)/shard_map/ppermute | solution.py:364
  3.7 3.6 %copy-start = (bf16[8,16,512]{2,1,0:T(8,128)(2,1)S(1)}, bf16[8,16,512]{2,1,0:T(8,128)(2,1)}, u32[]{:S(2)}) copy-start(bf16[8,16,512]{2,1,0:T(8,128)(2,1)} %param.5) | copy-start | bytes 393220
  3.7 11.8 %collective-permute-start.2 = (bf16[2,128,512]{2,1,0:T(8,128)(2,1)S(1)}, bf16[2,128,512]{2,1,0:T(8,128)(2,1)S(1)}, u32[]{:S(2)}, u32[]{:S(2)}) collective-permute-start(bf16[2,128,512]{2,1,0:T(8,128)(2,1)S(1)} %pad_maximum_fusion.2), channel_id=1, source_target_pairs={{0,1},{1,2},{2,3},{3,0},{4,7},{5,4},{6,5},{7,6},{8,9},{9,10},{10,1... | collective-permute-start | bytes 786440 | tf_op jit(solution)/shard_map/ppermute | solution.py:364
  6.5 0.7 %copy-start.4 = (s32[2,64]{1,0:T(2,128)S(1)}, s32[2,64]{1,0:T(2,128)}, u32[]{:S(2)}) copy-start(s32[2,64]{1,0:T(2,128)} %param.9) | copy-start | bytes 1540
  7.3 4.0 %collective-permute-start.7 = (bf16[8,16,512]{2,1,0:T(8,128)(2,1)S(1)}, bf16[8,16,512]{2,1,0:T(8,128)(2,1)S(1)}, u32[]{:S(2)}, u32[]{:S(2)}) collective-permute-start(bf16[8,16,512]{2,1,0:T(8,128)(2,1)S(1)} %copy-done), channel_id=1, source_target_pairs={{0,4},{1,5},{2,6},{3,7},{4,0},{5,1},{6,2},{7,3},{8,12},{9,13},{10,... | collective-permute-start | bytes 393224 | tf_op jit(solution)/shard_map/ppermute | solution.py:364
  9.4 0.9 %copy-start.3 = (bf16[8,16,512]{2,1,0:T(8,128)(2,1)S(1)}, bf16[8,16,512]{2,1,0:T(8,128)(2,1)}, u32[]{:S(2)}) copy-start(bf16[8,16,512]{2,1,0:T(8,128)(2,1)} %param.7) | copy-start | bytes 393220
  10.4 0.9 %copy-start.1 = (bf16[8,16,512]{2,1,0:T(8,128)(2,1)S(1)}, bf16[8,16,512]{2,1,0:T(8,128)(2,1)}, u32[]{:S(2)}) copy-start(bf16[8,16,512]{2,1,0:T(8,128)(2,1)} %param.8) | copy-start | bytes 393220
  11.3 7.2 %collective-permute-start.8 = (bf16[8,16,512]{2,1,0:T(8,128)(2,1)S(1)}, bf16[8,16,512]{2,1,0:T(8,128)(2,1)S(1)}, u32[]{:S(2)}, u32[]{:S(2)}) collective-permute-start(bf16[8,16,512]{2,1,0:T(8,128)(2,1)S(1)} %copy-done.1), channel_id=1, source_target_pairs={{0,4},{1,5},{2,6},{3,7},{4,0},{5,1},{6,2},{7,3},{8,12},{9,13},{10,... | collective-permute-start | bytes 393224 | tf_op jit(solution)/shard_map/ppermute | solution.py:364
  15.5 1.5 %collective-permute-start.3 = (bf16[2,128,512]{2,1,0:T(8,128)(2,1)S(1)}, bf16[2,128,512]{2,1,0:T(8,128)(2,1)S(1)}, u32[]{:S(2)}, u32[]{:S(2)}) collective-permute-start(bf16[2,128,512]{2,1,0:T(8,128)(2,1)S(1)} %collective-permute-done.2.lc_ref), channel_id=1, source_target_pairs={{0,4},{1,5},{2,6},{3,7},{4,0},{5,1},{6,2},{7,3},{8,12},{9,13},{10,... | collective-permute-start | bytes 786440 | tf_op jit(solution)/shard_map/ppermute | solution.py:364
  17.2 17.9 %collective-permute-start.4 = (bf16[2,192,512]{2,1,0:T(8,128)(2,1)S(1)}, bf16[2,192,512]{2,1,0:T(8,128)(2,1)S(1)}, u32[]{:S(2)}, u32[]{:S(2)}) collective-permute-start(bf16[2,192,512]{2,1,0:T(8,128)(2,1)S(1)} %pad_maximum_fusion), channel_id=1, source_target_pairs={{0,2},{1,3},{2,0},{3,1},{4,8},{5,9},{6,10},{7,11},{8,4},{9,5},{10,... | collective-permute-start | bytes 1179656 | tf_op jit(solution)/shard_map/ppermute | solution.py:364
  18.6 17.5 %collective-permute-start.9 = (bf16[2,128,512]{2,1,0:T(8,128)(2,1)S(1)}, bf16[2,128,512]{2,1,0:T(8,128)(2,1)S(1)}, u32[]{:S(2)}, u32[]{:S(2)}) collective-permute-start(bf16[2,128,512]{2,1,0:T(8,128)(2,1)S(1)} %pad_maximum_fusion.3), channel_id=1, source_target_pairs={{0,1},{1,2},{2,3},{3,0},{4,7},{5,4},{6,5},{7,6},{8,9},{9,10},{10,1... | collective-permute-start | bytes 786440 | tf_op jit(solution)/shard_map/ppermute | solution.py:364
  36.0 1.3 %collective-permute-start.5 = (bf16[8,16,128]{2,1,0:T(8,128)(2,1)S(1)}, bf16[8,16,128]{2,1,0:T(8,128)(2,1)S(1)}, u32[]{:S(2)}, u32[]{:S(2)}) collective-permute-start(bf16[8,16,128]{2,1,0:T(8,128)(2,1)S(1)} %bitcast.63), channel_id=1, source_target_pairs={{0,4},{1,5},{2,6},{3,7},{4,0},{5,1},{6,2},{7,3},{8,12},{9,13},{10,... | collective-permute-start | bytes 98312 | tf_op jit(solution)/shard_map/ppermute | solution.py:364
  37.3 1.5 %collective-permute-start.10 = (bf16[2,128,512]{2,1,0:T(8,128)(2,1)S(1)}, bf16[2,128,512]{2,1,0:T(8,128)(2,1)S(1)}, u32[]{:S(2)}, u32[]{:S(2)}) collective-permute-start(bf16[2,128,512]{2,1,0:T(8,128)(2,1)S(1)} %collective-permute-done.9.lc_ref), channel_id=1, source_target_pairs={{0,4},{1,5},{2,6},{3,7},{4,0},{5,1},{6,2},{7,3},{8,12},{9,13},{10,... | collective-permute-start | bytes 786440 | tf_op jit(solution)/shard_map/ppermute | solution.py:364
  37.5 5.8 %collective-permute-start.6 = (bf16[128,128]{1,0:T(8,128)(2,1)S(1)}, bf16[128,128]{1,0:T(8,128)(2,1)S(1)}, u32[]{:S(2)}, u32[]{:S(2)}) collective-permute-start(bf16[128,128]{1,0:T(8,128)(2,1)S(1)} %maximum_bitcast_fusion.4), channel_id=1, source_target_pairs={{0,1},{1,2},{2,3},{3,0},{4,7},{5,4},{6,5},{7,6},{8,9},{9,10},{10,1... | collective-permute-start | bytes 98312 | tf_op jit(solution)/shard_map/ppermute | solution.py:364
  38.9 13.8 %collective-permute-start.11 = (bf16[2,192,512]{2,1,0:T(8,128)(2,1)S(1)}, bf16[2,192,512]{2,1,0:T(8,128)(2,1)S(1)}, u32[]{:S(2)}, u32[]{:S(2)}) collective-permute-start(bf16[2,192,512]{2,1,0:T(8,128)(2,1)S(1)} %pad_maximum_fusion.1), channel_id=1, source_target_pairs={{0,2},{1,3},{2,0},{3,1},{4,8},{5,9},{6,10},{7,11},{8,4},{9,5},{10,... | collective-permute-start | bytes 1179656 | tf_op jit(solution)/shard_map/ppermute | solution.py:364
  43.2 1.2 %collective-permute-start.12 = (bf16[128,128]{1,0:T(8,128)(2,1)S(1)}, bf16[128,128]{1,0:T(8,128)(2,1)S(1)}, u32[]{:S(2)}, u32[]{:S(2)}) collective-permute-start(bf16[128,128]{1,0:T(8,128)(2,1)S(1)} %collective-permute-done.6.st_lc), channel_id=1, source_target_pairs={{0,4},{1,5},{2,6},{3,7},{4,0},{5,1},{6,2},{7,3},{8,12},{9,13},{10,... | collective-permute-start | bytes 98312 | tf_op jit(solution)/shard_map/ppermute | solution.py:364
  44.5 8.3 %collective-permute-start.13 = (bf16[192,128]{1,0:T(8,128)(2,1)S(1)}, bf16[192,128]{1,0:T(8,128)(2,1)S(1)}, u32[]{:S(2)}, u32[]{:S(2)}) collective-permute-start(bf16[192,128]{1,0:T(8,128)(2,1)S(1)} %bitcast.79), channel_id=1, source_target_pairs={{0,2},{1,3},{2,0},{3,1},{4,8},{5,9},{6,10},{7,11},{8,4},{9,5},{10,... | collective-permute-start | bytes 147464 | tf_op jit(solution)/shard_map/ppermute | solution.py:364

commit v3 on v2

--- a/solution.py
+++ b/solution.py
@@ -3,6 +3,7 @@
 
 import jax
 import jax.numpy as jnp
+import numpy as np
 from jax import lax
 from jax.experimental import pallas as pl
 from jax.experimental.pallas import tpu as pltpu
@@ -10,7 +11,6 @@
 
 HEAD_DIM = 32
 RADIUS = 6
-STRIP = 8
 LANES = 128
 NEG = -1e30
 LOG2E = 1.4426950408889634
@@ -33,68 +33,48 @@
     return pair, around, across
 
 
-def sizes(rows, cols):
-    own, strip, off = rows * cols, 2 * rows * STRIP, RADIUS * (cols + 2 * STRIP)
-    return own, own, strip, strip, off
-
-
-def mask_kernel(rows, cols, lat_count, lon_count, sc_ref, reach_ref, reach_t_ref, out_ref, out_t_ref):
+def pieces(rows, cols):
+    corners = 2 * RADIUS * RADIUS
+    pad = -corners % 16
+    strip = 2 * rows * RADIUS
+    return rows * cols, rows * cols, strip, strip, RADIUS * cols, corners + pad
+
+
+def layout(rows, cols, odd, pole):
+    west, east = range(-RADIUS, 0), range(cols, cols + RADIUS)
+    mine, other = range(0, rows), range(-rows, 0) if odd else range(rows, 2 * rows)
+    beyond = range(rows, rows + RADIUS) if odd else range(-RADIUS, 0)
+    if pole:
+        beyond = beyond[::-1]
+    sender_odd = odd if pole else not odd
+    places = [(r, c) for r in range(rows) for c in range(cols)]
+    places += [(r + (-rows if odd else rows), c) for r, c in places]
+    first, second = (east, west) if odd else (west, east)
+    for side, bands in ((first, (mine, other)), (second, (other, mine))):
+        places += [(r, c) for band in bands for r in band for c in side]
+    places += [(r, c) for r in beyond for c in range(cols)]
+    for side in (east, west) if sender_odd else (west, east):
+        places += [(r, c) for r in beyond for c in side]
+    nowhere = (1 << 20, 0)
+    places += [nowhere] * (sum(pieces(rows, cols)) - len(places))
+    return np.array(places, np.int32).T
+
+
+def mask_kernel(
+    rows, cols, lat_count, lon_count, sc_ref, reach_ref, reach_t_ref, table_ref,
+    near_ref, far_ref, out_t_ref,
+):
     lat, lon = sc_ref[0], sc_ref[1]
     total_rows, total_cols = rows * lat_count, cols * lon_count
-    half = total_cols // 2
     odd = lax.rem(lat, 2)
+    pole = jnp.where(jnp.where(odd == 0, lat, lat_count - 1 - lat) == 0, 1, 0)
     row0, col0 = lat * rows, lon * cols
-    own, oth, strip, _, off = sizes(rows, cols)
-    outer = own + 2 * strip + oth + off
-    t = lax.broadcasted_iota(jnp.int32, (1, outer), 1)
-    is_north, is_south = lat == 0, lat == lat_count - 1
-    sender_odd = jnp.where(is_north | is_south, odd, 1 - odd)
-
-    def split(index, width):
-        shift = width.bit_length() - 1
-        return lax.shift_right_logical(index, shift), index & (width - 1)
-
-    r_own, c_own = split(t, cols)
-    u = t - own
-    r_oth, c_oth = split(u, cols)
-    r_oth = r_oth + jnp.where(odd == 0, rows, -rows)
-    first = jnp.where(odd == 0, 0, -rows)
-    u = t - (own + oth)
-    r_a, c_a = split(u, STRIP)
-    r_a, c_a = r_a + first, c_a + jnp.where(odd == 0, -STRIP, cols)
-    u = t - (own + oth + strip)
-    r_b, c_b = split(u, STRIP)
-    r_b, c_b = r_b + first, c_b + jnp.where(odd == 0, cols, -STRIP)
-    u = t - (own + oth + 2 * strip)
-    width = cols + 2 * STRIP
-    r_off, x = split(u, width)
-    r_off = jnp.where(
-        is_north & (odd == 0),
-        -1 - r_off,
-        jnp.where(
-            is_south & (odd == 1),
-            rows + RADIUS - 1 - r_off,
-            r_off + jnp.where(odd == 0, -RADIUS, rows),
-        ),
-    )
-    first_at = jnp.where(sender_odd == 0, -STRIP, cols)
-    second_at = jnp.where(sender_odd == 0, cols, -STRIP)
-    c_off = jnp.where(
-        x < cols, x, jnp.where(x < cols + STRIP, x - cols + first_at, x - cols - STRIP + second_at)
-    )
-    at = [own, own + oth, own + oth + strip, own + oth + 2 * strip]
-    r_key = jnp.where(
-        t < at[0],
-        r_own,
-        jnp.where(t < at[1], r_oth, jnp.where(t < at[2], r_a, jnp.where(t < at[3], r_b, r_off))),
-    )
-    c_key = jnp.where(
-        t < at[0],
-        c_own,
-        jnp.where(t < at[1], c_oth, jnp.where(t < at[2], c_a, jnp.where(t < at[3], c_b, c_off))),
-    )
+    which = 2 * (2 * odd + pole)
+    r_key = table_ref[pl.ds(which, 1), :]
+    c_key = table_ref[pl.ds(which + 1, 1), :]
+    outer = r_key.shape[1]
     g_key = r_key + row0
-    turned = lax.rem(c_key + (col0 + half + total_cols), total_cols)
+    turned = lax.rem(c_key + (col0 + total_cols // 2 + total_cols), total_cols)
     pick = lax.broadcasted_iota(jnp.int32, (total_cols, outer), 0) == turned
     north_key = jnp.sum(jnp.where(pick, reach_t_ref[:, 0:1], 0.0), axis=0, keepdims=True)
     south_key = jnp.sum(jnp.where(pick, reach_t_ref[:, 1:2], 0.0), axis=0, keepdims=True)
@@ -105,9 +85,10 @@
         behind_n, north_key + 1.0 + g_f, jnp.where(behind_s, south_key + total_rows - g_f, 1.0)
     )
     valid = jnp.where(spare > 0.5, 1.0, 0.0)
-    n = lax.broadcasted_iota(jnp.int32, (own, 1), 0)
-    r_n, c_n = split(n, cols)
-    pick_n = lax.broadcasted_iota(jnp.int32, (own, total_cols), 1) == (c_n + col0)
+    n = lax.broadcasted_iota(jnp.int32, (rows * cols, 1), 0)
+    shift = cols.bit_length() - 1
+    r_n, c_n = lax.shift_right_logical(n, shift), n & (cols - 1)
+    pick_n = lax.broadcasted_iota(jnp.int32, (rows * cols, total_cols), 1) == (c_n + col0)
     north_n = jnp.sum(jnp.where(pick_n, reach_ref[0:1, :], 0.0), axis=1, keepdims=True)
     south_n = jnp.sum(jnp.where(pick_n, reach_ref[1:2, :], 0.0), axis=1, keepdims=True)
     g_n = (r_n + row0).astype(jnp.float32)
@@ -120,7 +101,9 @@
     ok = jnp.where(need_n > north_ok, 0.0, ok)
     ok = jnp.where(need_s > south_ok, 0.0, ok)
     bias = jnp.where(ok > 0.5, 0.0, NEG)
-    out_ref[...] = bias
+    count = near_ref.shape[1]
+    near_ref[...] = bias[:, 0:count]
+    far_ref[...] = bias[:, count:]
     out_t_ref[...] = bias.T
 
 
@@ -185,11 +168,11 @@
 
 
 def near_stats_kernel(
-    q_ref, g_ref, k_ref, v_ref, k_oth, v_oth, lc_ref, s2_ref, bias_ref,
+    q_ref, g_ref, k_ref, v_ref, k_oth, v_oth, lc_ref, s2_ref, off_ref, bias_ref,
     kall_ref, vall_ref, top_ref, sum_ref, dot_ref,
 ):
-    assemble(kall_ref, k_ref, k_oth, lc_ref.at[0], s2_ref.at[0])
-    assemble(vall_ref, v_ref, v_oth, lc_ref.at[1], s2_ref.at[1])
+    assemble(kall_ref, k_ref, k_oth, lc_ref.at[0], s2_ref.at[0], off_ref.at[0])
+    assemble(vall_ref, v_ref, v_oth, lc_ref.at[1], s2_ref.at[1], off_ref.at[1])
     near = kall_ref.shape[0]
     partial_stats(
         q_ref, g_ref, kall_ref, vall_ref, bias_ref[0:near, :], top_ref, sum_ref, dot_ref
@@ -218,9 +201,11 @@
     st_ref[...] = jnp.concatenate(terms, axis=0).T.astype(jnp.bfloat16)
 
 
-def query_kernel(q_ref, g_ref, kall_ref, vall_ref, off_ref, bias_ref, st_ref, dq_ref):
+def query_kernel(
+    q_ref, g_ref, kall_ref, vall_ref, corner_ref, near_ref, far_ref, st_ref, dq_ref
+):
     heads = q_ref.shape[1] // HEAD_DIM
-    near = kall_ref.shape[0]
+    near = near_ref.shape[1]
     row = lax.broadcasted_iota(jnp.int32, (LANES, LANES), 0)
 
     def stat_of(h):
@@ -233,9 +218,11 @@
 
     per = LANES // HEAD_DIM
     for at, first in groups(q_ref.shape[1]):
+        k_far = jnp.concatenate([kall_ref[near:, at], corner_ref[0, :, at]], axis=0)
+        v_far = jnp.concatenate([vall_ref[near:, at], corner_ref[1, :, at]], axis=0)
         sides = (
-            (kall_ref[:, at], vall_ref[:, at], bias_ref[:, 0:near]),
-            (off_ref[0, :, at], off_ref[1, :, at], bias_ref[:, near:]),
+            (kall_ref[0:near, at], vall_ref[0:near, at], near_ref[...]),
+            (k_far, v_far, far_ref[...]),
         )
         qs, gs = spread(q_ref[:, at]), spread(g_ref[:, at])
         logs = [stat_of(first + j) for j in range(per)]
@@ -283,26 +270,22 @@
     assemble(qall, q_ref, q_oth, lc_ref.at[0], s2_ref.at[0])
     assemble(gall, g_ref, g_oth, lc_ref.at[1], s2_ref.at[1])
     assemble(stall, st_ref, st_oth, st_lc, st_s2)
-    near = qall.shape[0]
 
     def finish(at, dk, dv):
         dk_ref[:, at], dv_ref[:, at] = dk, dv
 
-    key_sums(k_ref, v_ref, qall, gall, stall, bias_ref[:, 0:near], stat_rows, finish)
+    key_sums(k_ref, v_ref, qall, gall, stall, bias_ref[...], stat_rows, finish)
 
 
 def far_key_kernel(
     k_ref, v_ref, off_ref, st_off, bias_ref, dk_in, dv_in, dk_ref, dv_ref, stat_rows
 ):
-    near = bias_ref.shape[1] - off_ref.shape[1]
 
     def finish(at, dk, dv):
         dk_ref[:, at] = ((dk_in[:, at] + dk) * SCALE).astype(jnp.bfloat16)
         dv_ref[:, at] = (dv_in[:, at] + dv).astype(jnp.bfloat16)
 
-    key_sums(
-        k_ref, v_ref, off_ref.at[0], off_ref.at[1], st_off, bias_ref[:, near:], stat_rows, finish
-    )
+    key_sums(k_ref, v_ref, off_ref.at[0], off_ref.at[1], st_off, bias_ref[...], stat_rows, finish)
 
 
 def shards(lat_count, lon_count, query, key, value, grad, pole_reach):
@@ -312,23 +295,23 @@
     even = odd == 0
     pair, around, across = routes(lat_count, lon_count)
     axes = ("lat", "lon")
-    n_own, n_oth, n_strip, _, n_off = sizes(rows, cols)
+    n_own, n_oth, n_strip, _, n_off, n_corner = pieces(rows, cols)
     near = n_own + n_oth + 2 * n_strip
-    outer = near + n_off
+    far = n_off + n_corner
     place = jnp.stack([lat, lon]).astype(jnp.int32)
 
     smem = pl.BlockSpec(memory_space=pltpu.SMEM)
     vmem = pl.BlockSpec(memory_space=pltpu.VMEM)
 
-    def call(body, outs, operands, scratch=(), flops=1 << 28, scalars=False):
+    def call(body, outs, operands, scratch=(), flops=1 << 10, scalars=False):
         return pl.pallas_call(
             body,
             out_shape=outs,
             in_specs=[smem] * scalars + [vmem] * (len(operands) - scalars),
             out_specs=jax.tree.map(lambda _: vmem, outs),
             scratch_shapes=scratch,
-            compiler_params=pltpu.CompilerParams(vmem_limit_bytes=32 << 20),
-            cost_estimate=pl.CostEstimate(flops=flops, bytes_accessed=4 << 20, transcendentals=0),
+            compiler_params=pltpu.CompilerParams(vmem_limit_bytes=16 << 20),
+            cost_estimate=pl.CostEstimate(flops=flops, bytes_accessed=1 << 10, transcendentals=0),
         )(*operands)
 
     def array(*shape, dtype=jnp.bfloat16):
@@ -336,54 +319,61 @@
 
     f32 = jnp.float32
     heads = width // HEAD_DIM
-    reach = pole_reach.astype(f32)
-    bias, bias_t = call(
-        functools.partial(mask_kernel, rows, cols, lat_count, lon_count),
-        (array(n_own, outer, dtype=f32), array(outer, n_own, dtype=f32)),
-        (place, reach, reach.T),
-        scalars=True,
-    )
-
     def strip_of(mine, other):
-        at = jnp.where(even, cols - STRIP, 0)
-        mine = lax.dynamic_slice_in_dim(mine, at, STRIP, 1)
-        other = lax.dynamic_slice_in_dim(other, at, STRIP, 1)
-        top, low = jnp.where(even, mine, other), jnp.where(even, other, mine)
-        return jnp.concatenate([top, low], axis=0).reshape(2 * rows * STRIP, -1)
-
-    def edge_of(mine, first, second):
-        parts = [lax.dynamic_slice_in_dim(mine, jnp.where(even, 0, rows - RADIUS), RADIUS, 0)]
-        for piece in (first, second):
-            piece = piece.reshape(2 * rows, STRIP, -1)
-            parts.append(
-                lax.dynamic_slice_in_dim(piece, jnp.where(even, 0, 2 * rows - RADIUS), RADIUS, 0)
-            )
-        return jnp.concatenate(parts, axis=1).reshape(n_off, -1)
+        side = [jnp.where(even, x[:, cols - RADIUS :], x[:, :RADIUS]) for x in (mine, other)]
+        return jnp.concatenate([x.reshape(rows * RADIUS, -1) for x in side], axis=0)
+
+    def edge_of(mine, even=even):
+        return jnp.where(even, mine[:RADIUS], mine[rows - RADIUS :]).reshape(n_off, -1)
+
+    def corner_of(first, second):
+        count, half = RADIUS * RADIUS, n_strip // 2
+        parts = [
+            jnp.where(even, x[at : at + count], x[at + half - count : at + half])
+            for x, at in ((first, 0), (second, half))
+        ]
+        parts.append(jnp.zeros((n_corner - 2 * count, first.shape[1]), first.dtype))
+        return jnp.concatenate(parts, axis=0)
 
     def send(block, route):
         return lax.ppermute(block, axes, route)
 
-    def stacked(parts):
-        return jnp.stack(parts) if len(parts) > 1 else parts[0]
-
-    def strips(mine, other):
-        return stacked([strip_of(a, b) for a, b in zip(mine, other)])
-
-    def edges(mine, first, second):
-        if len(mine) == 1:
-            return edge_of(mine[0], first, second)
-        return jnp.stack([edge_of(a, first[i], second[i]) for i, a in enumerate(mine)])
-
     def flat(field):
         return field.reshape(n_own, field.shape[-1])
 
+    def strips(mine, other):
+        return jnp.stack([strip_of(a, b) for a, b in zip(mine, other)])
+
+    def edges(mine, even=even):
+        return jnp.stack([edge_of(a, even) for a in mine])
+
+    def corners(first, second):
+        return jnp.stack([corner_of(a, b) for a, b in zip(first, second)])
+
     key_o, value_o = send(key, pair), send(value, pair)
     kv, kv_o = (key, value), (key_o, value_o)
-    kv_1 = send(strips(kv, kv_o), around)
+    kv_strip, place = lax.optimization_barrier((strips(kv, kv_o), place))
+    kv_1 = send(kv_strip, around)
+
+    reach = pole_reach.astype(f32)
+    table = np.concatenate(
+        [layout(rows, cols, odd, pole) for odd in (False, True) for pole in (False, True)]
+    )
+    bias_near, bias_far, bias_t = call(
+        functools.partial(mask_kernel, rows, cols, lat_count, lon_count),
+        (
+            array(n_own, near, dtype=f32),
+            array(n_own, far, dtype=f32),
+            array(near + far, n_own, dtype=f32),
+        ),
+        (place, reach, reach.T, jnp.asarray(table)),
+        scalars=True,
+    )
+
+    later, query_s, grad_s, bias_t = lax.optimization_barrier((even, query, grad, bias_t))
+    kv_off = send(edges(kv, later), across)
     kv_2 = send(kv_1, pair)
-    kv_off = send(edges(kv, kv_1, kv_2), across)
-
-    query_s, grad_s, _ = lax.optimization_barrier((query, grad, key_o))
+    kv_corner = send(corners(kv_1, kv_2), across)
     query_o, grad_o = send(query_s, pair), send(grad_s, pair)
     qg, qg_o = (query, grad), (query_o, grad_o)
     qg_1 = send(strips(qg, qg_o), around)
@@ -392,26 +382,35 @@
     stat = array(heads, n_own, dtype=f32)
     kall, vall, *near_stats = call(
         near_stats_kernel,
-        (array(near, width), array(near, width), stat, stat, stat),
-        (q, g, k, v, flat(key_o), flat(value_o), kv_1, kv_2, bias_t),
+        (array(near + n_off, width), array(near + n_off, width), stat, stat, stat),
+        (q, g, k, v, flat(key_o), flat(value_o), kv_1, kv_2, kv_off, bias_t),
     )
     stats = call(
         far_stats_kernel,
         array(n_own, LANES),
-        (q, g, kv_off, bias_t, *near_stats),
+        (q, g, kv_corner, bias_t, *near_stats),
         [pltpu.VMEM((heads, n_own), f32)] * 3,
     )
     stats_grid = stats.reshape(rows, cols, LANES)
     stats_o = send(stats_grid, pair)
-    st_1 = send(strip_of(stats_grid, stats_o), around)
-    d_query = call(query_kernel, array(n_own, width), (q, g, kall, vall, kv_off, bias, stats))
+    qg_1, _ = lax.optimization_barrier((qg_1, stats_o))
+    qg_2 = send(qg_1, pair)
+    qg_beyond = jnp.concatenate([edges(qg), corners(qg_1, qg_2)], axis=1)
+    st_strip, qg_beyond, stats_q = lax.optimization_barrier(
+        (strip_of(stats_grid, stats_o), qg_beyond, stats)
+    )
+    st_1 = send(st_strip, around)
+    qg_off = send(qg_beyond, across)
+    d_query = call(
+        query_kernel,
+        array(n_own, width),
+        (q, g, kall, vall, kv_corner, bias_near, bias_far, stats_q),
+    )
     st_1, d_query = lax.optimization_barrier((st_1, d_query))
     st_2 = send(st_1, pair)
-    st_off = send(edge_of(stats_grid, st_1, st_2), across)
-
-    qg_1, _ = lax.optimization_barrier((qg_1, stats_o))
-    qg_2 = send(qg_1, pair)
-    qg_off = send(edges(qg, qg_1, qg_2), across)
+    st_off = send(
+        jnp.concatenate([edge_of(stats_grid), corner_of(st_1, st_2)], axis=0), across
+    )
 
     sums = array(n_own, width, dtype=f32)
     d_key, d_value = call(
@@ -419,7 +418,7 @@
         (sums, sums),
         (
             k, v, q, g, flat(query_o), flat(grad_o), qg_1, qg_2,
-            stats, flat(stats_o), st_1, st_2, bias,
+            stats, flat(stats_o), st_1, st_2, bias_near,
         ),
         [
             pltpu.VMEM((near, width), jnp.bfloat16),
@@ -431,8 +430,8 @@
     d_key, d_value = call(
         far_key_kernel,
         (array(n_own, width), array(n_own, width)),
-        (k, v, qg_off, st_off, bias, d_key, d_value),
-        [pltpu.VMEM((2 * heads, n_off), f32)],
+        (k, v, qg_off, st_off, bias_far, d_key, d_value),
+        [pltpu.VMEM((2 * heads, far), f32)],
     )
     shape = (rows, cols, width)
     return d_query.reshape(shape), d_key.reshape(shape), d_value.reshape(shape)

time: 55 us -> 48.6 us (0.88)
  waiting for transfers between devices: 26.4 us -> 12.9 us
  starting transfers between devices: 11.4 us -> 14.8 us
  other arithmetic: 1.31 us -> 3.98 us
  local copies, waits for them, and re-layouts: 2.71 us -> 3.87 us
    ppermute x14 -> x15, waiting for transfers between devices: 26.4 us -> 12.9 us  [send(): return lax.ppermute(block, axes, route)]
    ppermute x14 -> x15, starting transfers between devices: 11.4 us -> 14.8 us  [send(): return lax.ppermute(block, axes, route)]
    unnamed x10 -> x20, local copies, waits for them, and re-layouts: 1.49 us -> 3.41 us
    select_n x4 -> x17, other arithmetic: 0.97 us -> 2.8 us  [the longest x8 1.97 us: strip_of(): jnp.where(even, x[:, cols - RADIUS:], x[:, :RADIUS])]
    dynamic_slice x14 -> x0, local copies, waits for them, and re-layouts: 1.05 us -> none  [the longest x4 0.95 us: edge_of(): lax.dynamic_slice_in_dim(mine, jnp.where(even, 0, rows - RADIUS), RADIUS, 0)]
    another operation x7 -> x10, other arithmetic: 0.19 us -> 0.97 us  [the longest x6 0.74 us: strips(): return jnp.stack([strip_of(a, b) for a, b in zip(mine, other)])]
  transfers between devices with their start and end apart: 14 -> 15, of which waited for: 10 -> 8; matrix products, arithmetic and copies ran while one was open for 3% -> 9% of each run, Pallas kernels for 18% -> 20%
where the time goes in v3:
time: 48.6 us; the launch traced here: 48.3 us
  starting transfers between devices  14.8 us (30%)
  waiting for transfers between devices  12.9 us (27%)
  Pallas kernels  11.8 us (24%)
  other arithmetic  3.98 us (8%)
  local copies, waits for them, and re-layouts  3.87 us (8%)
  between operations  0.97 us (2%)
    ppermute x15, starting transfers between devices, send(): return lax.ppermute(block, axes, route)  14.8 us
    ppermute x15, waiting for transfers between devices, send(): return lax.ppermute(block, axes, route)  12.9 us
    pallas_call x6, Pallas kernels, call(): pl.pallas_call(body, out_shape=outs, in_specs=[smem] * scalars + [vmem] *...  11.8 us
    unnamed x20, local copies, waits for them, and re-layouts  3.41 us
    select_n x8, other arithmetic, strip_of(): jnp.where(even, x[:, cols - RADIUS:], x[:, :RADIUS])  1.97 us
  transfers between devices with their start and end apart: 15, of which 8 were waited for; matrix products, arithmetic and copies ran while one was open for 9% of the time, Pallas kernels for 20%

profile of v3, /device:TPU:0, one launch (start us, length us, event | category | flops | bytes accessed | tf_op | source)
XLA Modules:
  0.0 48.3 jit_solution(8895456009153612457)
XLA Ops:
  0.6 0.0 copy-start
  0.6 0.5 %collective-permute-start.1 = (bf16[8,16,512]{2,1,0:T(8,128)(2,1)}, bf16[8,16,512]{2,1,0:T(8,128)(2,1)S(1)}, u32[]{:S(2)}, u32[]{:S(2)}) collective-permute-start(bf16[8,16,512]{2,1,0:T(8,128)(2,1)} %param.8), channel_id=1, source_target_pairs={{0,4},{1,5},{2,6},{3,7},{4,0},{5,1},{6,2},{7,3},{8,12},{9,13},{10,... | collective-permute-start | bytes 393224 | tf_op jit(solution)/shard_map/ppermute | solution.py:339
  1.2 0.1 collective-permute-start
  1.2 0.9 %slice_select_fusion.10 = bf16[8,6,512]{2,1,0:T(8,128)(2,1)S(1)} fusion(bf16[8,16,512]{2,1,0:T(8,128)(2,1)} %param.8, pred[]{:T(512)S(6)} %eq.3), kind=kLoop, calls=%fused_computation.23 | loop fusion | flops 24576 | bytes 147457 | tf_op jit(solution)/shard_map/jit(_where)/select_n | solution.py:323
  2.1 0.0 copy-done
  2.1 0.0 copy-start.1
  2.2 0.9 %slice_select_fusion.8 = (bf16[8,6,512]{2,1,0:T(8,128)(2,1)S(1)}, bf16[8,6,512]{2,1,0:T(8,128)(2,1)S(1)}) fusion(bf16[8,16,512]{2,1,0:T(8,128)(2,1)} %param.9, pred[]{:T(512)S(6)} %eq.3, bf16[8,16,512]{2,1,0:T(8,128)(2,1)S(1)} %copy-done), kind=kLoop, calls=%fused_computation.21 | loop fusion | flops 49152 | bytes 294913 | tf_op jit(solution)/shard_map/jit(_where)/select_n | solution.py:323
  3.1 0.0 copy-done.1
  3.1 0.0 copy-start.2
  3.1 0.7 %slice_select_fusion = (bf16[6,16,512]{2,1,0:T(8,128)(2,1)}, bf16[6,16,512]{2,1,0:T(8,128)(2,1)}) fusion(bf16[8,16,512]{2,1,0:T(8,128)(2,1)S(1)} %copy-done.1, pred[]{:T(512)S(6)} %eq.3, bf16[8,16,512]{2,1,0:T(8,128)(2,1)S(1)} %copy-done), kind=kLoop, calls=%fused_computation.9 | loop fusion | flops 98304 | bytes 589825 | tf_op jit(solution)/shard_map/jit(_where)/select_n | solution.py:327
  3.8 0.2 copy-done.2
  4.1 0.1 pad.31.clone
  4.2 0.1 pad.3.clone
  4.3 0.0 copy-start.9
  4.3 0.7 %copy-done.9 = s32[2,64]{1,0:T(2,128)S(1)} copy-done((s32[2,64]{1,0:T(2,128)S(1)}, s32[2,64]{1,0:T(2,128)}, u32[]{:S(2)}) %copy-start.9) | copy-done | bytes 536
  5.0 0.1 copy.13
  5.2 0.1 pad_add_fusion.sc_ref
  5.2 0.0 collective-permute-done.1
  5.3 0.0 collective-permute-done
  5.4 0.0 copy-start.6
  5.4 0.0 copy-start.3
  5.5 3.1 %collective-permute-start.2 = (bf16[2,96,512]{2,1,0:T(8,128)(2,1)S(1)}, bf16[2,96,512]{2,1,0:T(8,128)(2,1)S(1)}, u32[]{:S(2)}, u32[]{:S(2)}) collective-permute-start(bf16[2,96,512]{2,1,0:T(8,128)(2,1)S(1)} %pad_maximum_fusion), channel_id=1, source_target_pairs={{0,1},{1,2},{2,3},{3,0},{4,7},{5,4},{6,5},{7,6},{8,9},{9,10},{10,1... | collective-permute-start | bytes 589832 | tf_op jit(solution)/shard_map/ppermute | solution.py:339
  8.5 0.0 copy-done.6
  8.5 0.9 %shard_map.85 = (f32[128,448]{1,0:T(8,128)S(1)}, f32[128,176]{1,0:T(8,128)S(1)}, f32[624,128]{1,0:T(8,128)S(1)}) custom-call(s32[2]{0:T(128)S(1)} %pad_add_fusion.sc_ref, f32[2,64]{1,0:T(2,128)S(1)} %convert_element_type.3.reach_ref, f32[64,2]{1,0:T(8,128)S(1)} %bitcast.73, s32[8,624]{1,0:T(8,128)S(1)} %copy-done.6), custom_call_target="tpu_custom_call" | custom-call | flops 1024 | bytes 1024 | tf_op jit(solution)/shard_map/pallas_call | solution.py:307
  9.5 1.9 %collective-permute-start.8 = (bf16[8,16,512]{2,1,0:T(8,128)(2,1)S(1)}, bf16[8,16,512]{2,1,0:T(8,128)(2,1)S(1)}, u32[]{:S(2)}, u32[]{:S(2)}) collective-permute-start(bf16[8,16,512]{2,1,0:T(8,128)(2,1)S(1)} %copy-done.1), channel_id=1, source_target_pairs={{0,4},{1,5},{2,6},{3,7},{4,0},{5,1},{6,2},{7,3},{8,12},{9,13},{10,... | collective-permute-start | bytes 393224 | tf_op jit(solution)/shard_map/ppermute | solution.py:339
  11.3 0.1 collective-permute-start.7
  11.5 1.3 %collective-permute-start.5 = (bf16[2,96,512]{2,1,0:T(8,128)(2,1)S(1)}, bf16[2,96,512]{2,1,0:T(8,128)(2,1)S(1)}, u32[]{:S(2)}, u32[]{:S(2)}) collective-permute-start(bf16[2,96,512]{2,1,0:T(8,128)(2,1)S(1)} %pad_maximum_fusion.1), channel_id=1, source_target_pairs={{0,2},{1,3},{2,0},{3,1},{4,8},{5,9},{6,10},{7,11},{8,4},{9,5},{10,... | collective-permute-start | bytes 589832 | tf_op jit(solution)/shard_map/ppermute | solution.py:339
  12.7 0.0 collective-permute-done.8
  12.7 0.0 collective-permute-done.7
  12.9 3.0 %collective-permute-done.2.lc_ref = bf16[2,96,512]{2,1,0:T(8,128)(2,1)S(1)} collective-permute-done((bf16[2,96,512]{2,1,0:T(8,128)(2,1)S(1)}, bf16[2,96,512]{2,1,0:T(8,128)(2,1)S(1)}, u32[]{:S(2)}, u32[]{:S(2)}) %collective-permute-start.2) | collective-permute-done | bytes 196640 | tf_op jit(solution)/shard_map/ppermute | solution.py:339
  15.8 0.0 collective-permute-start.3
  15.9 1.4 %collective-permute-done.3.s2_ref = bf16[2,96,512]{2,1,0:T(8,128)(2,1)S(1)} collective-permute-done((bf16[2,96,512]{2,1,0:T(8,128)(2,1)S(1)}, bf16[2,96,512]{2,1,0:T(8,128)(2,1)S(1)}, u32[]{:S(2)}, u32[]{:S(2)}) %collective-permute-start.3) | collective-permute-done | bytes 196640 | tf_op jit(solution)/shard_map/ppermute | solution.py:339
  17.3 0.1 maximum_bitcast_fusion.4
  17.4 3.6 %collective-permute-start.4 = (bf16[2,80,512]{2,1,0:T(8,128)(2,1)S(1)}, bf16[2,80,512]{2,1,0:T(8,128)(2,1)S(1)}, u32[]{:S(2)}, u32[]{:S(2)}) collective-permute-start(bf16[2,80,512]{2,1,0:T(8,128)(2,1)S(1)} %pad_maximum_fusion.3), channel_id=1, source_target_pairs={{0,2},{1,3},{2,0},{3,1},{4,8},{5,9},{6,10},{7,11},{8,4},{9,5},{10,... | collective-permute-start | bytes 491528 | tf_op jit(solution)/shard_map/ppermute | solution.py:339
  21.1 0.7 %pad_maximum_fusion.2 = bf16[2,96,512]{2,1,0:T(8,128)(2,1)} fusion(bf16[1,96,512]{2,1,0:T(8,128)(2,1)S(1)} %maximum_bitcast_fusion.3, bf16[1,96,512]{2,1,0:T(8,128)(2,1)S(1)} %maximum_bitcast_fusion.2), kind=kLoop, calls=%fused_computation.3 | loop fusion | flops 98304 | bytes 393216 | tf_op jit(solution)/shard_map/stack | solution.py:345
  21.8 0.0 collective-permute-start.9
  21.8 0.0 collective-permute-done.5.off_ref
  21.8 0.7 %copy-done.4 = bf16[2,96,512]{2,1,0:T(8,128)(2,1)} copy-done((bf16[2,96,512]{2,1,0:T(8,128)(2,1)}, bf16[2,96,512]{2,1,0:T(8,128)(2,1)S(1)}, u32[]{:S(2)}) %copy-start.4) | copy-done | bytes 196632
  22.5 0.9 %copy-done.5 = bf16[2,96,512]{2,1,0:T(8,128)(2,1)S(1)} copy-done((bf16[2,96,512]{2,1,0:T(8,128)(2,1)S(1)}, bf16[2,96,512]{2,1,0:T(8,128)(2,1)}, u32[]{:S(2)}) %copy-start.5) | copy-done | bytes 196632
  23.4 1.7 %shard_map.86 = (bf16[544,512]{1,0:T(8,128)(2,1)S(1)}, bf16[544,512]{1,0:T(8,128)(2,1)S(1)}, f32[16,128]{1,0:T(8,128)S(1)}, f32[16,128]{1,0:T(8,128)S(1)}, f32[16,128]{1,0:T(8,128)S(1)}) custom-call(bf16[128,512]{1,0:T(8,128)(2,1)S(1)} %bitcast.52, bf16[128,512]{1,0:T(8,128)(2,1)S(1)} %bitcast.56, bf16[128,512]{1,0:T(8,128)(2,1)S(1)} %bitcast.60, ...), custom_call_target="tpu_custom_call" | custom-call | flops 1024 | bytes 1024 | tf_op jit(solution)/shard_map/pallas_call | solution.py:307
  25.1 1.7 %collective-permute-done.4.off_ref.corner_ref = bf16[2,80,512]{2,1,0:T(8,128)(2,1)S(1)} collective-permute-done((bf16[2,80,512]{2,1,0:T(8,128)(2,1)S(1)}, bf16[2,80,512]{2,1,0:T(8,128)(2,1)S(1)}, u32[]{:S(2)}, u32[]{:S(2)}) %collective-permute-start.4) | collective-permute-done | bytes 163872 | tf_op jit(solution)/shard_map/ppermute | solution.py:339
  26.7 0.6 %shard_map.87.st_ref = bf16[128,128]{1,0:T(8,128)(2,1)S(1)} custom-call(bf16[128,512]{1,0:T(8,128)(2,1)S(1)} %bitcast.53, bf16[128,512]{1,0:T(8,128)(2,1)S(1)} %bitcast.57, bf16[2,80,512]{2,1,0:T(8,128)(2,1)S(1)} %collective-permute-done.4.off_ref.corner_ref, f32[624,128]{1,0:T(8,128)S(1)} %get-tuple-element.30.bias_ref, ...), custom_call_target="tpu_custom_call" | custom-call | flops 1024 | bytes 1024 | tf_op jit(solution)/shard_map/pallas_call | solution.py:307
  27.4 0.1 collective-permute-start.6
  27.5 1.2 %collective-permute-done.6 = bf16[8,16,128]{2,1,0:T(8,128)(2,1)S(1)} collective-permute-done((bf16[8,16,128]{2,1,0:T(8,128)(2,1)S(1)}, bf16[8,16,128]{2,1,0:T(8,128)(2,1)S(1)}, u32[]{:S(2)}, u32[]{:S(2)}) %collective-permute-start.6) | collective-permute-done | bytes 32800 | tf_op jit(solution)/shard_map/ppermute | solution.py:339
  28.7 0.8 %collective-permute-done.9.lc_ref = bf16[2,96,512]{2,1,0:T(8,128)(2,1)S(1)} collective-permute-done((bf16[2,96,512]{2,1,0:T(8,128)(2,1)}, bf16[2,96,512]{2,1,0:T(8,128)(2,1)S(1)}, u32[]{:S(2)}, u32[]{:S(2)}) %collective-permute-start.9) | collective-permute-done | bytes 196640 | tf_op jit(solution)/shard_map/ppermute | solution.py:339
  29.4 0.0 collective-permute-start.10
  29.5 1.4 %collective-permute-done.10.s2_ref = bf16[2,96,512]{2,1,0:T(8,128)(2,1)S(1)} collective-permute-done((bf16[2,96,512]{2,1,0:T(8,128)(2,1)S(1)}, bf16[2,96,512]{2,1,0:T(8,128)(2,1)S(1)}, u32[]{:S(2)}, u32[]{:S(2)}) %collective-permute-start.10) | collective-permute-done | bytes 196640 | tf_op jit(solution)/shard_map/ppermute | solution.py:339
  30.9 0.0 copy-start.7
  30.9 0.0 copy-start.8
  30.9 0.1 maximum_bitcast_fusion.6
  31.0 0.8 %copy-done.7 = bf16[6,16,512]{2,1,0:T(8,128)(2,1)S(1)} copy-done((bf16[6,16,512]{2,1,0:T(8,128)(2,1)S(1)}, bf16[6,16,512]{2,1,0:T(8,128)(2,1)}, u32[]{:S(2)}) %copy-start.7) | copy-done | bytes 98328
  31.8 0.0 copy-done.8
  31.9 1.3 %collective-permute-start.11 = (bf16[96,128]{1,0:T(8,128)(2,1)S(1)}, bf16[96,128]{1,0:T(8,128)(2,1)S(1)}, u32[]{:S(2)}, u32[]{:S(2)}) collective-permute-start(bf16[96,128]{1,0:T(8,128)(2,1)S(1)} %pad_maximum_fusion.4), channel_id=1, source_target_pairs={{0,1},{1,2},{2,3},{3,0},{4,7},{5,4},{6,5},{7,6},{8,9},{9,10},{10,1... | collective-permute-start | bytes 73736 | tf_op jit(solution)/shard_map/ppermute | solution.py:339
  33.1 0.9 %collective-permute-start.12 = (bf16[2,176,512]{2,1,0:T(8,128)(2,1)S(1)}, bf16[2,176,512]{2,1,0:T(8,128)(2,1)S(1)}, u32[]{:S(2)}, u32[]{:S(2)}) collective-permute-start(bf16[2,176,512]{2,1,0:T(8,128)(2,1)S(1)} %maximum_maximum_fusion), channel_id=1, source_target_pairs={{0,2},{1,3},{2,0},{3,1},{4,8},{5,9},{6,10},{7,11},{8,4},{9,5},{10,... | collective-permute-start | bytes 1081352 | tf_op jit(solution)/shard_map/ppermute | solution.py:339
  34.1 3.9 %shard_map.88 = bf16[128,512]{1,0:T(8,128)(2,1)} custom-call(bf16[128,512]{1,0:T(8,128)(2,1)S(1)} %bitcast.54, bf16[128,512]{1,0:T(8,128)(2,1)S(1)} %bitcast.58, bf16[544,512]{1,0:T(8,128)(2,1)S(1)} %get-tuple-element.39.kall_ref, bf16[544,512]{1,0:T(8,128)(2,1)S(1)} %get-tuple-element.40.vall_ref, ...), custom_call_target="tpu_custom_call" | custom-call | flops 1024 | bytes 1024 | tf_op jit(solution)/shard_map/pallas_call | solution.py:307
  37.9 0.0 collective-permute-done.11.st_lc
  38.0 0.0 collective-permute-start.13
  38.0 1.2 %collective-permute-done.13.st_s2 = bf16[96,128]{1,0:T(8,128)(2,1)S(1)} collective-permute-done((bf16[96,128]{1,0:T(8,128)(2,1)S(1)}, bf16[96,128]{1,0:T(8,128)(2,1)S(1)}, u32[]{:S(2)}, u32[]{:S(2)}) %collective-permute-start.13) | collective-permute-done | bytes 24608 | tf_op jit(solution)/shard_map/ppermute | solution.py:339
  39.2 0.1 maximum_maximum_fusion.1
  39.3 2.0 %collective-permute-start.14 = (bf16[176,128]{1,0:T(8,128)(2,1)S(1)}, bf16[176,128]{1,0:T(8,128)(2,1)S(1)}, u32[]{:S(2)}, u32[]{:S(2)}) collective-permute-start(bf16[176,128]{1,0:T(8,128)(2,1)S(1)} %maximum_maximum_fusion.1), channel_id=1, source_target_pairs={{0,2},{1,3},{2,0},{3,1},{4,8},{5,9},{6,10},{7,11},{8,4},{9,5},{10,... | collective-permute-start | bytes 135176 | tf_op jit(solution)/shard_map/ppermute | solution.py:339
  41.3 2.7 %shard_map.89 = (f32[128,512]{1,0:T(8,128)S(1)}, f32[128,512]{1,0:T(8,128)S(1)}) custom-call(bf16[128,512]{1,0:T(8,128)(2,1)S(1)} %bitcast.61, bf16[128,512]{1,0:T(8,128)(2,1)S(1)} %bitcast.64, bf16[128,512]{1,0:T(8,128)(2,1)S(1)} %bitcast.55, bf16[128,512]{1,0:T(8,128)(2,1)S(1)} %bitcast.59, bf16[128,512]{1,0:T(8,128)(2,1)S(1)} %bitcast.69, ...), custom_call_target="tpu_custom_call" | custom-call | flops 1024 | bytes 1024 | tf_op jit(solution)/shard_map/pallas_call | solution.py:307
  44.0 2.3 %collective-permute-done.14.st_off = bf16[176,128]{1,0:T(8,128)(2,1)S(1)} collective-permute-done((bf16[176,128]{1,0:T(8,128)(2,1)S(1)}, bf16[176,128]{1,0:T(8,128)(2,1)S(1)}, u32[]{:S(2)}, u32[]{:S(2)}) %collective-permute-start.14) | collective-permute-done | bytes 45088 | tf_op jit(solution)/shard_map/ppermute | solution.py:339
  46.3 0.0 collective-permute-done.12.off_ref
  46.3 2.0 %shard_map.90 = (bf16[128,512]{1,0:T(8,128)(2,1)}, bf16[128,512]{1,0:T(8,128)(2,1)}) custom-call(bf16[128,512]{1,0:T(8,128)(2,1)S(1)} %bitcast.62, bf16[128,512]{1,0:T(8,128)(2,1)S(1)} %bitcast.65, bf16[2,176,512]{2,1,0:T(8,128)(2,1)S(1)} %collective-permute-done.12.off_ref, bf16[176,128]{1,0:T(8,128)(2,1)S(1)} %collective-permute-done.14.st_off, ...), custom_call_target="tpu_custom_call" | custom-call | flops 1024 | bytes 1024 | tf_op jit(solution)/shard_map/pallas_call | solution.py:307
  (38 shorter events, 0.6 us)
Async XLA Ops:
  0.6 1.5 %copy-start = (bf16[8,16,512]{2,1,0:T(8,128)(2,1)S(1)}, bf16[8,16,512]{2,1,0:T(8,128)(2,1)}, u32[]{:S(2)}) copy-start(bf16[8,16,512]{2,1,0:T(8,128)(2,1)} %param.6) | copy-start | bytes 393220
  0.6 4.6 %collective-permute-start.1 = (bf16[8,16,512]{2,1,0:T(8,128)(2,1)}, bf16[8,16,512]{2,1,0:T(8,128)(2,1)S(1)}, u32[]{:S(2)}, u32[]{:S(2)}) collective-permute-start(bf16[8,16,512]{2,1,0:T(8,128)(2,1)} %param.8), channel_id=1, source_target_pairs={{0,4},{1,5},{2,6},{3,7},{4,0},{5,1},{6,2},{7,3},{8,12},{9,13},{10,... | collective-permute-start | bytes 393224 | tf_op jit(solution)/shard_map/ppermute | solution.py:339
  1.2 4.1 %collective-permute-start = (bf16[8,16,512]{2,1,0:T(8,128)(2,1)}, bf16[8,16,512]{2,1,0:T(8,128)(2,1)S(1)}, u32[]{:S(2)}, u32[]{:S(2)}) collective-permute-start(bf16[8,16,512]{2,1,0:T(8,128)(2,1)} %param.7), channel_id=1, source_target_pairs={{0,4},{1,5},{2,6},{3,7},{4,0},{5,1},{6,2},{7,3},{8,12},{9,13},{10,... | collective-permute-start | bytes 393224 | tf_op jit(solution)/shard_map/ppermute | solution.py:339
  2.1 1.0 %copy-start.1 = (bf16[8,16,512]{2,1,0:T(8,128)(2,1)S(1)}, bf16[8,16,512]{2,1,0:T(8,128)(2,1)}, u32[]{:S(2)}) copy-start(bf16[8,16,512]{2,1,0:T(8,128)(2,1)} %param.9) | copy-start | bytes 393220
  3.1 1.0 %copy-start.2 = (bf16[8,16,512]{2,1,0:T(8,128)(2,1)S(1)}, bf16[8,16,512]{2,1,0:T(8,128)(2,1)}, u32[]{:S(2)}) copy-start(bf16[8,16,512]{2,1,0:T(8,128)(2,1)} %param.7) | copy-start | bytes 393220
  4.3 0.7 %copy-start.9 = (s32[2,64]{1,0:T(2,128)S(1)}, s32[2,64]{1,0:T(2,128)}, u32[]{:S(2)}) copy-start(s32[2,64]{1,0:T(2,128)} %param.10) | copy-start | bytes 1540
  5.4 3.1 %copy-start.6 = (s32[8,624]{1,0:T(8,128)S(1)}, s32[8,624]{1,0:T(8,128)}, u32[]{:S(2)}) copy-start(s32[8,624]{1,0:T(8,128)} %constant.20.clone.table_ref) | copy-start | bytes 59908
  5.4 6.0 %copy-start.3 = (bf16[8,16,512]{2,1,0:T(8,128)(2,1)S(1)}, bf16[8,16,512]{2,1,0:T(8,128)(2,1)}, u32[]{:S(2)}) copy-start(bf16[8,16,512]{2,1,0:T(8,128)(2,1)} %param.8) | copy-start | bytes 393220
  5.5 10.4 %collective-permute-start.2 = (bf16[2,96,512]{2,1,0:T(8,128)(2,1)S(1)}, bf16[2,96,512]{2,1,0:T(8,128)(2,1)S(1)}, u32[]{:S(2)}, u32[]{:S(2)}) collective-permute-start(bf16[2,96,512]{2,1,0:T(8,128)(2,1)S(1)} %pad_maximum_fusion), channel_id=1, source_target_pairs={{0,1},{1,2},{2,3},{3,0},{4,7},{5,4},{6,5},{7,6},{8,9},{9,10},{10,1... | collective-permute-start | bytes 589832 | tf_op jit(solution)/shard_map/ppermute | solution.py:339
  9.5 3.3 %collective-permute-start.8 = (bf16[8,16,512]{2,1,0:T(8,128)(2,1)S(1)}, bf16[8,16,512]{2,1,0:T(8,128)(2,1)S(1)}, u32[]{:S(2)}, u32[]{:S(2)}) collective-permute-start(bf16[8,16,512]{2,1,0:T(8,128)(2,1)S(1)} %copy-done.1), channel_id=1, source_target_pairs={{0,4},{1,5},{2,6},{3,7},{4,0},{5,1},{6,2},{7,3},{8,12},{9,13},{10,... | collective-permute-start | bytes 393224 | tf_op jit(solution)/shard_map/ppermute | solution.py:339
  11.3 1.4 %collective-permute-start.7 = (bf16[8,16,512]{2,1,0:T(8,128)(2,1)S(1)}, bf16[8,16,512]{2,1,0:T(8,128)(2,1)S(1)}, u32[]{:S(2)}, u32[]{:S(2)}) collective-permute-start(bf16[8,16,512]{2,1,0:T(8,128)(2,1)S(1)} %copy-done), channel_id=1, source_target_pairs={{0,4},{1,5},{2,6},{3,7},{4,0},{5,1},{6,2},{7,3},{8,12},{9,13},{10,... | collective-permute-start | bytes 393224 | tf_op jit(solution)/shard_map/ppermute | solution.py:339
  11.5 10.3 %collective-permute-start.5 = (bf16[2,96,512]{2,1,0:T(8,128)(2,1)S(1)}, bf16[2,96,512]{2,1,0:T(8,128)(2,1)S(1)}, u32[]{:S(2)}, u32[]{:S(2)}) collective-permute-start(bf16[2,96,512]{2,1,0:T(8,128)(2,1)S(1)} %pad_maximum_fusion.1), channel_id=1, source_target_pairs={{0,2},{1,3},{2,0},{3,1},{4,8},{5,9},{6,10},{7,11},{8,4},{9,5},{10,... | collective-permute-start | bytes 589832 | tf_op jit(solution)/shard_map/ppermute | solution.py:339
  15.8 1.4 %collective-permute-start.3 = (bf16[2,96,512]{2,1,0:T(8,128)(2,1)S(1)}, bf16[2,96,512]{2,1,0:T(8,128)(2,1)S(1)}, u32[]{:S(2)}, u32[]{:S(2)}) collective-permute-start(bf16[2,96,512]{2,1,0:T(8,128)(2,1)S(1)} %collective-permute-done.2.lc_ref), channel_id=1, source_target_pairs={{0,4},{1,5},{2,6},{3,7},{4,0},{5,1},{6,2},{7,3},{8,12},{9,13},{10,... | collective-permute-start | bytes 589832 | tf_op jit(solution)/shard_map/ppermute | solution.py:339
  17.4 9.3 %collective-permute-start.4 = (bf16[2,80,512]{2,1,0:T(8,128)(2,1)S(1)}, bf16[2,80,512]{2,1,0:T(8,128)(2,1)S(1)}, u32[]{:S(2)}, u32[]{:S(2)}) collective-permute-start(bf16[2,80,512]{2,1,0:T(8,128)(2,1)S(1)} %pad_maximum_fusion.3), channel_id=1, source_target_pairs={{0,2},{1,3},{2,0},{3,1},{4,8},{5,9},{6,10},{7,11},{8,4},{9,5},{10,... | collective-permute-start | bytes 491528 | tf_op jit(solution)/shard_map/ppermute | solution.py:339
  21.8 7.7 %collective-permute-start.9 = (bf16[2,96,512]{2,1,0:T(8,128)(2,1)}, bf16[2,96,512]{2,1,0:T(8,128)(2,1)S(1)}, u32[]{:S(2)}, u32[]{:S(2)}) collective-permute-start(bf16[2,96,512]{2,1,0:T(8,128)(2,1)} %pad_maximum_fusion.2), channel_id=1, source_target_pairs={{0,1},{1,2},{2,3},{3,0},{4,7},{5,4},{6,5},{7,6},{8,9},{9,10},{10,1... | collective-permute-start | bytes 589832 | tf_op jit(solution)/shard_map/ppermute | solution.py:339
  21.8 0.7 %copy-start.4 = (bf16[2,96,512]{2,1,0:T(8,128)(2,1)}, bf16[2,96,512]{2,1,0:T(8,128)(2,1)S(1)}, u32[]{:S(2)}) copy-start(bf16[2,96,512]{2,1,0:T(8,128)(2,1)S(1)} %collective-permute-done.5.off_ref) | copy-start | bytes 589828
  22.5 0.9 %copy-start.5 = (bf16[2,96,512]{2,1,0:T(8,128)(2,1)S(1)}, bf16[2,96,512]{2,1,0:T(8,128)(2,1)}, u32[]{:S(2)}) copy-start(bf16[2,96,512]{2,1,0:T(8,128)(2,1)} %copy-done.4) | copy-start | bytes 589828
  27.4 1.3 %collective-permute-start.6 = (bf16[8,16,128]{2,1,0:T(8,128)(2,1)S(1)}, bf16[8,16,128]{2,1,0:T(8,128)(2,1)S(1)}, u32[]{:S(2)}, u32[]{:S(2)}) collective-permute-start(bf16[8,16,128]{2,1,0:T(8,128)(2,1)S(1)} %bitcast.66), channel_id=1, source_target_pairs={{0,4},{1,5},{2,6},{3,7},{4,0},{5,1},{6,2},{7,3},{8,12},{9,13},{10,... | collective-permute-start | bytes 98312 | tf_op jit(solution)/shard_map/ppermute | solution.py:339
  29.4 1.4 %collective-permute-start.10 = (bf16[2,96,512]{2,1,0:T(8,128)(2,1)S(1)}, bf16[2,96,512]{2,1,0:T(8,128)(2,1)S(1)}, u32[]{:S(2)}, u32[]{:S(2)}) collective-permute-start(bf16[2,96,512]{2,1,0:T(8,128)(2,1)S(1)} %collective-permute-done.9.lc_ref), channel_id=1, source_target_pairs={{0,4},{1,5},{2,6},{3,7},{4,0},{5,1},{6,2},{7,3},{8,12},{9,13},{10,... | collective-permute-start | bytes 589832 | tf_op jit(solution)/shard_map/ppermute | solution.py:339
  30.9 0.9 %copy-start.7 = (bf16[6,16,512]{2,1,0:T(8,128)(2,1)S(1)}, bf16[6,16,512]{2,1,0:T(8,128)(2,1)}, u32[]{:S(2)}) copy-start(bf16[6,16,512]{2,1,0:T(8,128)(2,1)} %get-tuple-element.63) | copy-start | bytes 294916
  30.9 0.9 %copy-start.8 = (bf16[6,16,512]{2,1,0:T(8,128)(2,1)S(1)}, bf16[6,16,512]{2,1,0:T(8,128)(2,1)}, u32[]{:S(2)}) copy-start(bf16[6,16,512]{2,1,0:T(8,128)(2,1)} %get-tuple-element.64) | copy-start | bytes 294916
  31.9 6.1 %collective-permute-start.11 = (bf16[96,128]{1,0:T(8,128)(2,1)S(1)}, bf16[96,128]{1,0:T(8,128)(2,1)S(1)}, u32[]{:S(2)}, u32[]{:S(2)}) collective-permute-start(bf16[96,128]{1,0:T(8,128)(2,1)S(1)} %pad_maximum_fusion.4), channel_id=1, source_target_pairs={{0,1},{1,2},{2,3},{3,0},{4,7},{5,4},{6,5},{7,6},{8,9},{9,10},{10,1... | collective-permute-start | bytes 73736 | tf_op jit(solution)/shard_map/ppermute | solution.py:339
  33.1 13.2 %collective-permute-start.12 = (bf16[2,176,512]{2,1,0:T(8,128)(2,1)S(1)}, bf16[2,176,512]{2,1,0:T(8,128)(2,1)S(1)}, u32[]{:S(2)}, u32[]{:S(2)}) collective-permute-start(bf16[2,176,512]{2,1,0:T(8,128)(2,1)S(1)} %maximum_maximum_fusion), channel_id=1, source_target_pairs={{0,2},{1,3},{2,0},{3,1},{4,8},{5,9},{6,10},{7,11},{8,4},{9,5},{10,... | collective-permute-start | bytes 1081352 | tf_op jit(solution)/shard_map/ppermute | solution.py:339
  38.0 1.2 %collective-permute-start.13 = (bf16[96,128]{1,0:T(8,128)(2,1)S(1)}, bf16[96,128]{1,0:T(8,128)(2,1)S(1)}, u32[]{:S(2)}, u32[]{:S(2)}) collective-permute-start(bf16[96,128]{1,0:T(8,128)(2,1)S(1)} %collective-permute-done.11.st_lc), channel_id=1, source_target_pairs={{0,4},{1,5},{2,6},{3,7},{4,0},{5,1},{6,2},{7,3},{8,12},{9,13},{10,... | collective-permute-start | bytes 73736 | tf_op jit(solution)/shard_map/ppermute | solution.py:339
  39.3 7.0 %collective-permute-start.14 = (bf16[176,128]{1,0:T(8,128)(2,1)S(1)}, bf16[176,128]{1,0:T(8,128)(2,1)S(1)}, u32[]{:S(2)}, u32[]{:S(2)}) collective-permute-start(bf16[176,128]{1,0:T(8,128)(2,1)S(1)} %maximum_maximum_fusion.1), channel_id=1, source_target_pairs={{0,2},{1,3},{2,0},{3,1},{4,8},{5,9},{6,10},{7,11},{8,4},{9,5},{10,... | collective-permute-start | bytes 135176 | tf_op jit(solution)/shard_map/ppermute | solution.py:339

commit v4 on v3

--- a/solution.py
+++ b/solution.py
@@ -319,7 +319,7 @@
 
     f32 = jnp.float32
     heads = width // HEAD_DIM
-    def strip_of(mine, other):
+    def strip_of(mine, other, even=even):
         side = [jnp.where(even, x[:, cols - RADIUS :], x[:, :RADIUS]) for x in (mine, other)]
         return jnp.concatenate([x.reshape(rows * RADIUS, -1) for x in side], axis=0)
 
@@ -341,8 +341,8 @@
     def flat(field):
         return field.reshape(n_own, field.shape[-1])
 
-    def strips(mine, other):
-        return jnp.stack([strip_of(a, b) for a, b in zip(mine, other)])
+    def strips(mine, other, even=even):
+        return jnp.stack([strip_of(a, b, even) for a, b in zip(mine, other)])
 
     def edges(mine, even=even):
         return jnp.stack([edge_of(a, even) for a in mine])
@@ -352,9 +352,17 @@
 
     key_o, value_o = send(key, pair), send(value, pair)
     kv, kv_o = (key, value), (key_o, value_o)
-    kv_strip, place = lax.optimization_barrier((strips(kv, kv_o), place))
+    query_o, grad_o = send(query, pair), send(grad, pair)
+    qg, qg_o = (query, grad), (query_o, grad_o)
+    kv_strip = strips(kv, kv_o)
+    later, _ = lax.optimization_barrier((even, kv_strip))
     kv_1 = send(kv_strip, around)
-
+    kv_off = send(edges(kv, later), across)
+    qg_1 = send(strips(qg, qg_o, later), around)
+    kv_2 = send(kv_1, pair)
+    kv_last = corners(kv_1, kv_2)
+    kv_corner = send(kv_last, across)
+    qg_1, place, _ = lax.optimization_barrier((qg_1, place, kv_last))
     reach = pole_reach.astype(f32)
     table = np.concatenate(
         [layout(rows, cols, odd, pole) for odd in (False, True) for pole in (False, True)]
@@ -370,13 +378,9 @@
         scalars=True,
     )
 
-    later, query_s, grad_s, bias_t = lax.optimization_barrier((even, query, grad, bias_t))
-    kv_off = send(edges(kv, later), across)
-    kv_2 = send(kv_1, pair)
-    kv_corner = send(corners(kv_1, kv_2), across)
-    query_o, grad_o = send(query_s, pair), send(grad_s, pair)
-    qg, qg_o = (query, grad), (query_o, grad_o)
-    qg_1 = send(strips(qg, qg_o), around)
+    qg_2 = send(qg_1, pair)
+    qg_beyond = jnp.concatenate([edges(qg, later), corners(qg_1, qg_2)], axis=1)
+    bias_t, qg_beyond = lax.optimization_barrier((bias_t, qg_beyond))
 
     q, k, v, g = (flat(x) for x in (query, key, value, grad))
     stat = array(heads, n_own, dtype=f32)
@@ -393,9 +397,6 @@
     )
     stats_grid = stats.reshape(rows, cols, LANES)
     stats_o = send(stats_grid, pair)
-    qg_1, _ = lax.optimization_barrier((qg_1, stats_o))
-    qg_2 = send(qg_1, pair)
-    qg_beyond = jnp.concatenate([edges(qg), corners(qg_1, qg_2)], axis=1)
     st_strip, qg_beyond, stats_q = lax.optimization_barrier(
         (strip_of(stats_grid, stats_o), qg_beyond, stats)
     )

time: 48.6 us -> 46.1 us (0.949)
  waiting for transfers between devices: 12.9 us -> 15.2 us
  starting transfers between devices: 14.8 us -> 12.6 us
  other arithmetic: 3.98 us -> 2.49 us
  local copies, waits for them, and re-layouts: 3.87 us -> 2.91 us
    ppermute x15, waiting for transfers between devices: 12.9 us -> 15.2 us  [send(): return lax.ppermute(block, axes, route)]
    ppermute x15, starting transfers between devices: 14.8 us -> 12.6 us  [send(): return lax.ppermute(block, axes, route)]
    unnamed x20 -> x14, local copies, waits for them, and re-layouts: 3.41 us -> 2.45 us
    select_n x8 -> x9, other arithmetic: 1.97 us -> 1.06 us  [strip_of(): jnp.where(even, x[:, cols - RADIUS:], x[:, :RADIUS])]
    concatenate x1, other arithmetic: 0.03 us -> 0.77 us  [shards(): qg_beyond = jnp.concatenate([edges(qg, later), corners(qg_1, qg_2)], axis=1)]
    another operation x6, other arithmetic: 0.74 us -> 0.08 us  [strips(): return jnp.stack([strip_of(a, b, even) for a, b in zip(mine, other)])]
    select_n x3 -> x5, other arithmetic: 0.72 us -> 0.06 us  [edge_of(): jnp.where(even, mine[:RADIUS], mine[rows - RADIUS:]).reshape(n_off, -1)]
  transfers between devices with their start and end apart: 15 -> 15, of which waited for: 8 -> 9; matrix products, arithmetic and copies ran while one was open for 9% -> 6% of each run, Pallas kernels for 20% -> 20%
where the time goes in v4:
time: 46.1 us; the launch traced here: 45.8 us
  waiting for transfers between devices  15.2 us (33%)
  starting transfers between devices  12.6 us (27%)
  Pallas kernels  11.7 us (25%)
  local copies, waits for them, and re-layouts  2.91 us (6%)
  other arithmetic  2.49 us (5%)
  between operations  1 us (2%)
    ppermute x15, waiting for transfers between devices, send(): return lax.ppermute(block, axes, route)  15.2 us
    ppermute x15, starting transfers between devices, send(): return lax.ppermute(block, axes, route)  12.6 us
    pallas_call x6, Pallas kernels, call(): pl.pallas_call(body, out_shape=outs, in_specs=[smem] * scalars + [vmem] *...  11.7 us
    unnamed x14, local copies, waits for them, and re-layouts  2.45 us
    select_n x9, other arithmetic, strip_of(): jnp.where(even, x[:, cols - RADIUS:], x[:, :RADIUS])  1.06 us
  transfers between devices with their start and end apart: 15, of which 9 were waited for; matrix products, arithmetic and copies ran while one was open for 6% of the time, Pallas kernels for 20%

profile of v4, /device:TPU:0, one launch (start us, length us, event | category | flops | bytes accessed | tf_op | source)
XLA Modules:
  0.0 45.8 jit_solution(6071095940785094445)
XLA Ops:
  0.6 0.0 copy-start.3
  0.6 0.5 %collective-permute-start.5 = (bf16[8,16,512]{2,1,0:T(8,128)(2,1)}, bf16[8,16,512]{2,1,0:T(8,128)(2,1)S(1)}, u32[]{:S(2)}, u32[]{:S(2)}) collective-permute-start(bf16[8,16,512]{2,1,0:T(8,128)(2,1)} %param.6), channel_id=1, source_target_pairs={{0,4},{1,5},{2,6},{3,7},{4,0},{5,1},{6,2},{7,3},{8,12},{9,13},{10,... | collective-permute-start | bytes 393224 | tf_op jit(solution)/shard_map/ppermute | solution.py:339
  1.2 0.1 collective-permute-start
  1.2 0.4 collective-permute-start.1
  1.7 0.1 collective-permute-start.6
  1.8 0.9 %slice_select_fusion.11 = bf16[8,6,512]{2,1,0:T(8,128)(2,1)S(1)} fusion(bf16[8,16,512]{2,1,0:T(8,128)(2,1)} %param.7, pred[]{:T(512)S(6)} %eq.3), kind=kLoop, calls=%fused_computation.24 | loop fusion | flops 24576 | bytes 147457 | tf_op jit(solution)/shard_map/jit(_where)/select_n | solution.py:323
  2.6 0.0 copy-done.3
  2.7 0.1 pad.33.clone
  2.8 0.1 pad.3.clone
  2.8 0.0 copy-start.6
  2.9 0.7 %copy-done.6 = s32[2,64]{1,0:T(2,128)S(1)} copy-done((s32[2,64]{1,0:T(2,128)S(1)}, s32[2,64]{1,0:T(2,128)}, u32[]{:S(2)}) %copy-start.6) | copy-done | bytes 536
  3.5 0.1 copy.13
  3.7 0.1 pad_add_fusion.sc_ref
  3.8 0.0 collective-permute-done
  3.8 0.0 collective-permute-done.1
  3.9 0.0 copy-start.1
  4.0 0.9 %copy-done.1 = bf16[8,16,512]{2,1,0:T(8,128)(2,1)S(1)} copy-done((bf16[8,16,512]{2,1,0:T(8,128)(2,1)S(1)}, bf16[8,16,512]{2,1,0:T(8,128)(2,1)}, u32[]{:S(2)}) %copy-start.1) | copy-done | bytes 131096
  4.8 0.0 copy-start.2
  4.9 0.9 %copy-done.2 = bf16[8,16,512]{2,1,0:T(8,128)(2,1)S(1)} copy-done((bf16[8,16,512]{2,1,0:T(8,128)(2,1)S(1)}, bf16[8,16,512]{2,1,0:T(8,128)(2,1)}, u32[]{:S(2)}) %copy-start.2) | copy-done | bytes 131096
  5.8 0.0 copy-start
  5.8 3.1 %collective-permute-start.2 = (bf16[2,96,512]{2,1,0:T(8,128)(2,1)S(1)}, bf16[2,96,512]{2,1,0:T(8,128)(2,1)S(1)}, u32[]{:S(2)}, u32[]{:S(2)}) collective-permute-start(bf16[2,96,512]{2,1,0:T(8,128)(2,1)S(1)} %pad_maximum_fusion), channel_id=1, source_target_pairs={{0,1},{1,2},{2,3},{3,0},{4,7},{5,4},{6,5},{7,6},{8,9},{9,10},{10,1... | collective-permute-start | bytes 589832 | tf_op jit(solution)/shard_map/ppermute | solution.py:339
  8.8 0.0 copy-done
  8.9 0.0 collective-permute-done.5
  9.0 0.0 collective-permute-done.6
  9.1 1.6 %collective-permute-start.7 = (bf16[2,96,512]{2,1,0:T(8,128)(2,1)S(1)}, bf16[2,96,512]{2,1,0:T(8,128)(2,1)S(1)}, u32[]{:S(2)}, u32[]{:S(2)}) collective-permute-start(bf16[2,96,512]{2,1,0:T(8,128)(2,1)S(1)} %pad_maximum_fusion.1), channel_id=1, source_target_pairs={{0,1},{1,2},{2,3},{3,0},{4,7},{5,4},{6,5},{7,6},{8,9},{9,10},{10,1... | collective-permute-start | bytes 589832 | tf_op jit(solution)/shard_map/ppermute | solution.py:339
  10.8 1.9 %collective-permute-start.9 = (bf16[2,96,512]{2,1,0:T(8,128)(2,1)S(1)}, bf16[2,96,512]{2,1,0:T(8,128)(2,1)S(1)}, u32[]{:S(2)}, u32[]{:S(2)}) collective-permute-start(bf16[2,96,512]{2,1,0:T(8,128)(2,1)S(1)} %pad_maximum_fusion.2), channel_id=1, source_target_pairs={{0,2},{1,3},{2,0},{3,1},{4,8},{5,9},{6,10},{7,11},{8,4},{9,5},{10,... | collective-permute-start | bytes 589832 | tf_op jit(solution)/shard_map/ppermute | solution.py:339
  12.7 3.8 %collective-permute-done.2.lc_ref = bf16[2,96,512]{2,1,0:T(8,128)(2,1)S(1)} collective-permute-done((bf16[2,96,512]{2,1,0:T(8,128)(2,1)S(1)}, bf16[2,96,512]{2,1,0:T(8,128)(2,1)S(1)}, u32[]{:S(2)}, u32[]{:S(2)}) %collective-permute-start.2) | collective-permute-done | bytes 196640 | tf_op jit(solution)/shard_map/ppermute | solution.py:339
  16.5 0.0 collective-permute-start.3
  16.6 1.4 %collective-permute-done.3.s2_ref = bf16[2,96,512]{2,1,0:T(8,128)(2,1)S(1)} collective-permute-done((bf16[2,96,512]{2,1,0:T(8,128)(2,1)S(1)}, bf16[2,96,512]{2,1,0:T(8,128)(2,1)S(1)}, u32[]{:S(2)}, u32[]{:S(2)}) %collective-permute-start.3) | collective-permute-done | bytes 196640 | tf_op jit(solution)/shard_map/ppermute | solution.py:339
  18.0 0.1 maximum_bitcast_fusion.4
  18.1 0.0 copy-start.4
  18.1 0.1 collective-permute-start.4
  18.2 2.2 %collective-permute-done.7.lc_ref = bf16[2,96,512]{2,1,0:T(8,128)(2,1)S(1)} collective-permute-done((bf16[2,96,512]{2,1,0:T(8,128)(2,1)S(1)}, bf16[2,96,512]{2,1,0:T(8,128)(2,1)S(1)}, u32[]{:S(2)}, u32[]{:S(2)}) %collective-permute-start.7) | collective-permute-done | bytes 196640 | tf_op jit(solution)/shard_map/ppermute | solution.py:339
  20.4 0.1 collective-permute-start.8
  20.5 0.0 copy-done.4
  20.5 0.9 %shard_map.85 = (f32[128,448]{1,0:T(8,128)S(1)}, f32[128,176]{1,0:T(8,128)S(1)}, f32[624,128]{1,0:T(8,128)S(1)}) custom-call(s32[2]{0:T(128)S(1)} %pad_add_fusion.sc_ref, f32[2,64]{1,0:T(2,128)S(1)} %convert_element_type.3.reach_ref, f32[64,2]{1,0:T(8,128)S(1)} %bitcast.73, s32[8,624]{1,0:T(8,128)S(1)} %copy-done.4), custom_call_target="tpu_custom_call" | custom-call | flops 1024 | bytes 1024 | tf_op jit(solution)/shard_map/pallas_call | solution.py:307
  21.5 0.3 collective-permute-done.8.s2_ref
  21.9 0.1 maximum_bitcast_fusion.6
  22.0 0.8 %maximum_maximum_fusion = bf16[2,176,512]{2,1,0:T(8,128)(2,1)} fusion(bf16[1,80,512]{2,1,0:T(8,128)(2,1)S(1)} %get-tuple-element.56, bf16[1,80,512]{2,1,0:T(8,128)(2,1)S(1)} %get-tuple-element.55, bf16[1,96,512]{2,1,0:T(8,128)(2,1)S(1)} %bitcast.76, bf16[1,96,512]{2,1,0:T(8,128)(2,1)S(1)} %bitcast.77), kind=kLoop, calls=%fused_computation | loop fusion | flops 1441792 | bytes 720896 | tf_op jit(solution)/shard_map/concatenate | solution.py:382
  22.8 2.6 %collective-permute-done.9.off_ref = bf16[2,96,512]{2,1,0:T(8,128)(2,1)S(1)} collective-permute-done((bf16[2,96,512]{2,1,0:T(8,128)(2,1)S(1)}, bf16[2,96,512]{2,1,0:T(8,128)(2,1)S(1)}, u32[]{:S(2)}, u32[]{:S(2)}) %collective-permute-start.9) | collective-permute-done | bytes 196640 | tf_op jit(solution)/shard_map/ppermute | solution.py:339
  25.3 1.6 %shard_map.86 = (bf16[544,512]{1,0:T(8,128)(2,1)S(1)}, bf16[544,512]{1,0:T(8,128)(2,1)S(1)}, f32[16,128]{1,0:T(8,128)S(1)}, f32[16,128]{1,0:T(8,128)S(1)}, f32[16,128]{1,0:T(8,128)S(1)}) custom-call(bf16[128,512]{1,0:T(8,128)(2,1)S(1)} %bitcast.52, bf16[128,512]{1,0:T(8,128)(2,1)S(1)} %bitcast.56, bf16[128,512]{1,0:T(8,128)(2,1)S(1)} %bitcast.60, ...), custom_call_target="tpu_custom_call" | custom-call | flops 1024 | bytes 1024 | tf_op jit(solution)/shard_map/pallas_call | solution.py:307
  27.0 0.1 collective-permute-done.4.off_ref.corner_ref
  27.1 0.0 copy-start.5
  27.1 0.6 %shard_map.87.st_ref = bf16[128,128]{1,0:T(8,128)(2,1)S(1)} custom-call(bf16[128,512]{1,0:T(8,128)(2,1)S(1)} %bitcast.53, bf16[128,512]{1,0:T(8,128)(2,1)S(1)} %bitcast.57, bf16[2,80,512]{2,1,0:T(8,128)(2,1)S(1)} %collective-permute-done.4.off_ref.corner_ref, f32[624,128]{1,0:T(8,128)S(1)} %get-tuple-element.29.bias_ref, ...), custom_call_target="tpu_custom_call" | custom-call | flops 1024 | bytes 1024 | tf_op jit(solution)/shard_map/pallas_call | solution.py:307
  27.7 0.1 collective-permute-start.10
  27.8 1.2 %collective-permute-done.10 = bf16[8,16,128]{2,1,0:T(8,128)(2,1)S(1)} collective-permute-done((bf16[8,16,128]{2,1,0:T(8,128)(2,1)S(1)}, bf16[8,16,128]{2,1,0:T(8,128)(2,1)S(1)}, u32[]{:S(2)}, u32[]{:S(2)}) %collective-permute-start.10) | collective-permute-done | bytes 32800 | tf_op jit(solution)/shard_map/ppermute | solution.py:339
  29.0 1.6 %collective-permute-start.11 = (bf16[96,128]{1,0:T(8,128)(2,1)S(1)}, bf16[96,128]{1,0:T(8,128)(2,1)S(1)}, u32[]{:S(2)}, u32[]{:S(2)}) collective-permute-start(bf16[96,128]{1,0:T(8,128)(2,1)S(1)} %pad_maximum_fusion.4), channel_id=1, source_target_pairs={{0,1},{1,2},{2,3},{3,0},{4,7},{5,4},{6,5},{7,6},{8,9},{9,10},{10,1... | collective-permute-start | bytes 73736 | tf_op jit(solution)/shard_map/ppermute | solution.py:339
  30.6 0.0 copy-done.5
  30.6 2.5 %collective-permute-start.12 = (bf16[2,176,512]{2,1,0:T(8,128)(2,1)S(1)}, bf16[2,176,512]{2,1,0:T(8,128)(2,1)S(1)}, u32[]{:S(2)}, u32[]{:S(2)}) collective-permute-start(bf16[2,176,512]{2,1,0:T(8,128)(2,1)S(1)} %copy-done.5), channel_id=1, source_target_pairs={{0,2},{1,3},{2,0},{3,1},{4,8},{5,9},{6,10},{7,11},{8,4},{9,5},{10,... | collective-permute-start | bytes 1081352 | tf_op jit(solution)/shard_map/ppermute | solution.py:339
  33.1 3.8 %shard_map.88 = bf16[128,512]{1,0:T(8,128)(2,1)} custom-call(bf16[128,512]{1,0:T(8,128)(2,1)S(1)} %bitcast.54, bf16[128,512]{1,0:T(8,128)(2,1)S(1)} %bitcast.58, bf16[544,512]{1,0:T(8,128)(2,1)S(1)} %get-tuple-element.35.kall_ref, bf16[544,512]{1,0:T(8,128)(2,1)S(1)} %get-tuple-element.36.vall_ref, ...), custom_call_target="tpu_custom_call" | custom-call | flops 1024 | bytes 1024 | tf_op jit(solution)/shard_map/pallas_call | solution.py:307
  36.9 0.0 collective-permute-done.11.st_lc
  36.9 0.0 collective-permute-start.13
  36.9 1.2 %collective-permute-done.13.st_s2 = bf16[96,128]{1,0:T(8,128)(2,1)S(1)} collective-permute-done((bf16[96,128]{1,0:T(8,128)(2,1)S(1)}, bf16[96,128]{1,0:T(8,128)(2,1)S(1)}, u32[]{:S(2)}, u32[]{:S(2)}) %collective-permute-start.13) | collective-permute-done | bytes 24608 | tf_op jit(solution)/shard_map/ppermute | solution.py:339
  38.1 0.1 maximum_maximum_fusion.1
  38.2 0.6 %collective-permute-start.14 = (bf16[176,128]{1,0:T(8,128)(2,1)S(1)}, bf16[176,128]{1,0:T(8,128)(2,1)S(1)}, u32[]{:S(2)}, u32[]{:S(2)}) collective-permute-start(bf16[176,128]{1,0:T(8,128)(2,1)S(1)} %maximum_maximum_fusion.1), channel_id=1, source_target_pairs={{0,2},{1,3},{2,0},{3,1},{4,8},{5,9},{6,10},{7,11},{8,4},{9,5},{10,... | collective-permute-start | bytes 135176 | tf_op jit(solution)/shard_map/ppermute | solution.py:339
  38.8 2.6 %shard_map.89 = (f32[128,512]{1,0:T(8,128)S(1)}, f32[128,512]{1,0:T(8,128)S(1)}) custom-call(bf16[128,512]{1,0:T(8,128)(2,1)S(1)} %bitcast.61, bf16[128,512]{1,0:T(8,128)(2,1)S(1)} %bitcast.64, bf16[128,512]{1,0:T(8,128)(2,1)S(1)} %bitcast.55, bf16[128,512]{1,0:T(8,128)(2,1)S(1)} %bitcast.59, bf16[128,512]{1,0:T(8,128)(2,1)S(1)} %bitcast.68, ...), custom_call_target="tpu_custom_call" | custom-call | flops 1024 | bytes 1024 | tf_op jit(solution)/shard_map/pallas_call | solution.py:307
  41.4 2.4 %collective-permute-done.14.st_off = bf16[176,128]{1,0:T(8,128)(2,1)S(1)} collective-permute-done((bf16[176,128]{1,0:T(8,128)(2,1)S(1)}, bf16[176,128]{1,0:T(8,128)(2,1)S(1)}, u32[]{:S(2)}, u32[]{:S(2)}) %collective-permute-start.14) | collective-permute-done | bytes 45088 | tf_op jit(solution)/shard_map/ppermute | solution.py:339
  43.8 0.0 collective-permute-done.12.off_ref
  43.8 2.0 %shard_map.90 = (bf16[128,512]{1,0:T(8,128)(2,1)}, bf16[128,512]{1,0:T(8,128)(2,1)}) custom-call(bf16[128,512]{1,0:T(8,128)(2,1)S(1)} %bitcast.62, bf16[128,512]{1,0:T(8,128)(2,1)S(1)} %bitcast.65, bf16[2,176,512]{2,1,0:T(8,128)(2,1)S(1)} %collective-permute-done.12.off_ref, bf16[176,128]{1,0:T(8,128)(2,1)S(1)} %collective-permute-done.14.st_off, ...), custom_call_target="tpu_custom_call" | custom-call | flops 1024 | bytes 1024 | tf_op jit(solution)/shard_map/pallas_call | solution.py:307
  (40 shorter events, 0.7 us)
Async XLA Ops:
  0.6 2.0 %copy-start.3 = (bf16[8,16,512]{2,1,0:T(8,128)(2,1)S(1)}, bf16[8,16,512]{2,1,0:T(8,128)(2,1)}, u32[]{:S(2)}) copy-start(bf16[8,16,512]{2,1,0:T(8,128)(2,1)} %param.8) | copy-start | bytes 393220
  0.6 8.2 %collective-permute-start.5 = (bf16[8,16,512]{2,1,0:T(8,128)(2,1)}, bf16[8,16,512]{2,1,0:T(8,128)(2,1)S(1)}, u32[]{:S(2)}, u32[]{:S(2)}) collective-permute-start(bf16[8,16,512]{2,1,0:T(8,128)(2,1)} %param.6), channel_id=1, source_target_pairs={{0,4},{1,5},{2,6},{3,7},{4,0},{5,1},{6,2},{7,3},{8,12},{9,13},{10,... | collective-permute-start | bytes 393224 | tf_op jit(solution)/shard_map/ppermute | solution.py:339
  1.2 2.6 %collective-permute-start = (bf16[8,16,512]{2,1,0:T(8,128)(2,1)}, bf16[8,16,512]{2,1,0:T(8,128)(2,1)S(1)}, u32[]{:S(2)}, u32[]{:S(2)}) collective-permute-start(bf16[8,16,512]{2,1,0:T(8,128)(2,1)} %param.7), channel_id=1, source_target_pairs={{0,4},{1,5},{2,6},{3,7},{4,0},{5,1},{6,2},{7,3},{8,12},{9,13},{10,... | collective-permute-start | bytes 393224 | tf_op jit(solution)/shard_map/ppermute | solution.py:339
  1.2 2.5 %collective-permute-start.1 = (bf16[8,16,512]{2,1,0:T(8,128)(2,1)}, bf16[8,16,512]{2,1,0:T(8,128)(2,1)S(1)}, u32[]{:S(2)}, u32[]{:S(2)}) collective-permute-start(bf16[8,16,512]{2,1,0:T(8,128)(2,1)} %param.8), channel_id=1, source_target_pairs={{0,4},{1,5},{2,6},{3,7},{4,0},{5,1},{6,2},{7,3},{8,12},{9,13},{10,... | collective-permute-start | bytes 393224 | tf_op jit(solution)/shard_map/ppermute | solution.py:339
  1.7 7.3 %collective-permute-start.6 = (bf16[8,16,512]{2,1,0:T(8,128)(2,1)}, bf16[8,16,512]{2,1,0:T(8,128)(2,1)S(1)}, u32[]{:S(2)}, u32[]{:S(2)}) collective-permute-start(bf16[8,16,512]{2,1,0:T(8,128)(2,1)} %param.9), channel_id=1, source_target_pairs={{0,4},{1,5},{2,6},{3,7},{4,0},{5,1},{6,2},{7,3},{8,12},{9,13},{10,... | collective-permute-start | bytes 393224 | tf_op jit(solution)/shard_map/ppermute | solution.py:339
  2.8 0.7 %copy-start.6 = (s32[2,64]{1,0:T(2,128)S(1)}, s32[2,64]{1,0:T(2,128)}, u32[]{:S(2)}) copy-start(s32[2,64]{1,0:T(2,128)} %param.10) | copy-start | bytes 1540
  3.9 0.9 %copy-start.1 = (bf16[8,16,512]{2,1,0:T(8,128)(2,1)S(1)}, bf16[8,16,512]{2,1,0:T(8,128)(2,1)}, u32[]{:S(2)}) copy-start(bf16[8,16,512]{2,1,0:T(8,128)(2,1)} %param.9) | copy-start | bytes 393220
  4.8 0.9 %copy-start.2 = (bf16[8,16,512]{2,1,0:T(8,128)(2,1)S(1)}, bf16[8,16,512]{2,1,0:T(8,128)(2,1)}, u32[]{:S(2)}) copy-start(bf16[8,16,512]{2,1,0:T(8,128)(2,1)} %param.7) | copy-start | bytes 393220
  5.8 3.1 %copy-start = (bf16[8,16,512]{2,1,0:T(8,128)(2,1)S(1)}, bf16[8,16,512]{2,1,0:T(8,128)(2,1)}, u32[]{:S(2)}) copy-start(bf16[8,16,512]{2,1,0:T(8,128)(2,1)} %param.6) | copy-start | bytes 393220
  5.8 10.8 %collective-permute-start.2 = (bf16[2,96,512]{2,1,0:T(8,128)(2,1)S(1)}, bf16[2,96,512]{2,1,0:T(8,128)(2,1)S(1)}, u32[]{:S(2)}, u32[]{:S(2)}) collective-permute-start(bf16[2,96,512]{2,1,0:T(8,128)(2,1)S(1)} %pad_maximum_fusion), channel_id=1, source_target_pairs={{0,1},{1,2},{2,3},{3,0},{4,7},{5,4},{6,5},{7,6},{8,9},{9,10},{10,1... | collective-permute-start | bytes 589832 | tf_op jit(solution)/shard_map/ppermute | solution.py:339
  9.1 11.3 %collective-permute-start.7 = (bf16[2,96,512]{2,1,0:T(8,128)(2,1)S(1)}, bf16[2,96,512]{2,1,0:T(8,128)(2,1)S(1)}, u32[]{:S(2)}, u32[]{:S(2)}) collective-permute-start(bf16[2,96,512]{2,1,0:T(8,128)(2,1)S(1)} %pad_maximum_fusion.1), channel_id=1, source_target_pairs={{0,1},{1,2},{2,3},{3,0},{4,7},{5,4},{6,5},{7,6},{8,9},{9,10},{10,1... | collective-permute-start | bytes 589832 | tf_op jit(solution)/shard_map/ppermute | solution.py:339
  10.8 14.5 %collective-permute-start.9 = (bf16[2,96,512]{2,1,0:T(8,128)(2,1)S(1)}, bf16[2,96,512]{2,1,0:T(8,128)(2,1)S(1)}, u32[]{:S(2)}, u32[]{:S(2)}) collective-permute-start(bf16[2,96,512]{2,1,0:T(8,128)(2,1)S(1)} %pad_maximum_fusion.2), channel_id=1, source_target_pairs={{0,2},{1,3},{2,0},{3,1},{4,8},{5,9},{6,10},{7,11},{8,4},{9,5},{10,... | collective-permute-start | bytes 589832 | tf_op jit(solution)/shard_map/ppermute | solution.py:339
  16.5 1.4 %collective-permute-start.3 = (bf16[2,96,512]{2,1,0:T(8,128)(2,1)S(1)}, bf16[2,96,512]{2,1,0:T(8,128)(2,1)S(1)}, u32[]{:S(2)}, u32[]{:S(2)}) collective-permute-start(bf16[2,96,512]{2,1,0:T(8,128)(2,1)S(1)} %collective-permute-done.2.lc_ref), channel_id=1, source_target_pairs={{0,4},{1,5},{2,6},{3,7},{4,0},{5,1},{6,2},{7,3},{8,12},{9,13},{10,... | collective-permute-start | bytes 589832 | tf_op jit(solution)/shard_map/ppermute | solution.py:339
  18.1 2.4 %copy-start.4 = (s32[8,624]{1,0:T(8,128)S(1)}, s32[8,624]{1,0:T(8,128)}, u32[]{:S(2)}) copy-start(s32[8,624]{1,0:T(8,128)} %constant.20.clone.table_ref) | copy-start | bytes 59908
  18.1 9.0 %collective-permute-start.4 = (bf16[2,80,512]{2,1,0:T(8,128)(2,1)S(1)}, bf16[2,80,512]{2,1,0:T(8,128)(2,1)S(1)}, u32[]{:S(2)}, u32[]{:S(2)}) collective-permute-start(bf16[2,80,512]{2,1,0:T(8,128)(2,1)S(1)} %pad_maximum_fusion.3), channel_id=1, source_target_pairs={{0,2},{1,3},{2,0},{3,1},{4,8},{5,9},{6,10},{7,11},{8,4},{9,5},{10,... | collective-permute-start | bytes 491528 | tf_op jit(solution)/shard_map/ppermute | solution.py:339
  20.4 1.4 %collective-permute-start.8 = (bf16[2,96,512]{2,1,0:T(8,128)(2,1)S(1)}, bf16[2,96,512]{2,1,0:T(8,128)(2,1)S(1)}, u32[]{:S(2)}, u32[]{:S(2)}) collective-permute-start(bf16[2,96,512]{2,1,0:T(8,128)(2,1)S(1)} %collective-permute-done.7.lc_ref), channel_id=1, source_target_pairs={{0,4},{1,5},{2,6},{3,7},{4,0},{5,1},{6,2},{7,3},{8,12},{9,13},{10,... | collective-permute-start | bytes 589832 | tf_op jit(solution)/shard_map/ppermute | solution.py:339
  27.1 3.5 %copy-start.5 = (bf16[2,176,512]{2,1,0:T(8,128)(2,1)S(1)}, bf16[2,176,512]{2,1,0:T(8,128)(2,1)}, u32[]{:S(2)}) copy-start(bf16[2,176,512]{2,1,0:T(8,128)(2,1)} %maximum_maximum_fusion) | copy-start | bytes 1081348
  27.7 1.3 %collective-permute-start.10 = (bf16[8,16,128]{2,1,0:T(8,128)(2,1)S(1)}, bf16[8,16,128]{2,1,0:T(8,128)(2,1)S(1)}, u32[]{:S(2)}, u32[]{:S(2)}) collective-permute-start(bf16[8,16,128]{2,1,0:T(8,128)(2,1)S(1)} %bitcast.66), channel_id=1, source_target_pairs={{0,4},{1,5},{2,6},{3,7},{4,0},{5,1},{6,2},{7,3},{8,12},{9,13},{10,... | collective-permute-start | bytes 98312 | tf_op jit(solution)/shard_map/ppermute | solution.py:339
  29.0 7.9 %collective-permute-start.11 = (bf16[96,128]{1,0:T(8,128)(2,1)S(1)}, bf16[96,128]{1,0:T(8,128)(2,1)S(1)}, u32[]{:S(2)}, u32[]{:S(2)}) collective-permute-start(bf16[96,128]{1,0:T(8,128)(2,1)S(1)} %pad_maximum_fusion.4), channel_id=1, source_target_pairs={{0,1},{1,2},{2,3},{3,0},{4,7},{5,4},{6,5},{7,6},{8,9},{9,10},{10,1... | collective-permute-start | bytes 73736 | tf_op jit(solution)/shard_map/ppermute | solution.py:339
  30.6 13.2 %collective-permute-start.12 = (bf16[2,176,512]{2,1,0:T(8,128)(2,1)S(1)}, bf16[2,176,512]{2,1,0:T(8,128)(2,1)S(1)}, u32[]{:S(2)}, u32[]{:S(2)}) collective-permute-start(bf16[2,176,512]{2,1,0:T(8,128)(2,1)S(1)} %copy-done.5), channel_id=1, source_target_pairs={{0,2},{1,3},{2,0},{3,1},{4,8},{5,9},{6,10},{7,11},{8,4},{9,5},{10,... | collective-permute-start | bytes 1081352 | tf_op jit(solution)/shard_map/ppermute | solution.py:339
  36.9 1.2 %collective-permute-start.13 = (bf16[96,128]{1,0:T(8,128)(2,1)S(1)}, bf16[96,128]{1,0:T(8,128)(2,1)S(1)}, u32[]{:S(2)}, u32[]{:S(2)}) collective-permute-start(bf16[96,128]{1,0:T(8,128)(2,1)S(1)} %collective-permute-done.11.st_lc), channel_id=1, source_target_pairs={{0,4},{1,5},{2,6},{3,7},{4,0},{5,1},{6,2},{7,3},{8,12},{9,13},{10,... | collective-permute-start | bytes 73736 | tf_op jit(solution)/shard_map/ppermute | solution.py:339
  38.2 5.6 %collective-permute-start.14 = (bf16[176,128]{1,0:T(8,128)(2,1)S(1)}, bf16[176,128]{1,0:T(8,128)(2,1)S(1)}, u32[]{:S(2)}, u32[]{:S(2)}) collective-permute-start(bf16[176,128]{1,0:T(8,128)(2,1)S(1)} %maximum_maximum_fusion.1), channel_id=1, source_target_pairs={{0,2},{1,3},{2,0},{3,1},{4,8},{5,9},{6,10},{7,11},{8,4},{9,5},{10,... | collective-permute-start | bytes 135176 | tf_op jit(solution)/shard_map/ppermute | solution.py:339

commit v5 on v4

--- a/solution.py
+++ b/solution.py
@@ -61,9 +61,18 @@
 
 
 def mask_kernel(
-    rows, cols, lat_count, lon_count, sc_ref, reach_ref, reach_t_ref, table_ref,
-    near_ref, far_ref, out_t_ref,
-):
+    rows, cols, lat_count, lon_count, sc_ref, reach_hbm, table_hbm,
+    near_ref, far_ref, out_t_ref, reach_vm, table_ref, sems,
+):
+    copies = [
+        pltpu.make_async_copy(reach_hbm, reach_vm, sems.at[0]),
+        pltpu.make_async_copy(table_hbm, table_ref, sems.at[1]),
+    ]
+    for copy in copies:
+        copy.start()
+    for copy in copies:
+        copy.wait()
+    reach = reach_vm[...].astype(jnp.float32)
     lat, lon = sc_ref[0], sc_ref[1]
     total_rows, total_cols = rows * lat_count, cols * lon_count
     odd = lax.rem(lat, 2)
@@ -76,8 +85,9 @@
     g_key = r_key + row0
     turned = lax.rem(c_key + (col0 + total_cols // 2 + total_cols), total_cols)
     pick = lax.broadcasted_iota(jnp.int32, (total_cols, outer), 0) == turned
-    north_key = jnp.sum(jnp.where(pick, reach_t_ref[:, 0:1], 0.0), axis=0, keepdims=True)
-    south_key = jnp.sum(jnp.where(pick, reach_t_ref[:, 1:2], 0.0), axis=0, keepdims=True)
+    pick = jnp.where(pick, 1.0, 0.0)
+    key_reach = jnp.dot(reach, pick, preferred_element_type=jnp.float32)
+    north_key, south_key = key_reach[0:1], key_reach[1:2]
     g_f = g_key.astype(jnp.float32)
     behind_n = g_key < 0
     behind_s = g_key >= total_rows
@@ -89,8 +99,8 @@
     shift = cols.bit_length() - 1
     r_n, c_n = lax.shift_right_logical(n, shift), n & (cols - 1)
     pick_n = lax.broadcasted_iota(jnp.int32, (rows * cols, total_cols), 1) == (c_n + col0)
-    north_n = jnp.sum(jnp.where(pick_n, reach_ref[0:1, :], 0.0), axis=1, keepdims=True)
-    south_n = jnp.sum(jnp.where(pick_n, reach_ref[1:2, :], 0.0), axis=1, keepdims=True)
+    north_n = jnp.sum(jnp.where(pick_n, reach[0:1, :], 0.0), axis=1, keepdims=True)
+    south_n = jnp.sum(jnp.where(pick_n, reach[1:2, :], 0.0), axis=1, keepdims=True)
     g_n = (r_n + row0).astype(jnp.float32)
     north_ok = jnp.where(north_n > g_n, 1.0, 0.0)
     south_ok = jnp.where(south_n > total_rows - 1 - g_n, 1.0, 0.0)
@@ -168,11 +178,11 @@
 
 
 def near_stats_kernel(
-    q_ref, g_ref, k_ref, v_ref, k_oth, v_oth, lc_ref, s2_ref, off_ref, bias_ref,
+    q_ref, g_ref, k_ref, v_ref, k_oth, v_oth, lc_ref, s2_ref, bias_ref,
     kall_ref, vall_ref, top_ref, sum_ref, dot_ref,
 ):
-    assemble(kall_ref, k_ref, k_oth, lc_ref.at[0], s2_ref.at[0], off_ref.at[0])
-    assemble(vall_ref, v_ref, v_oth, lc_ref.at[1], s2_ref.at[1], off_ref.at[1])
+    assemble(kall_ref, k_ref, k_oth, lc_ref.at[0], s2_ref.at[0])
+    assemble(vall_ref, v_ref, v_oth, lc_ref.at[1], s2_ref.at[1])
     near = kall_ref.shape[0]
     partial_stats(
         q_ref, g_ref, kall_ref, vall_ref, bias_ref[0:near, :], top_ref, sum_ref, dot_ref
@@ -180,12 +190,13 @@
 
 
 def far_stats_kernel(
-    q_ref, g_ref, off_ref, bias_ref, top_ref, sum_ref, dot_ref, st_ref, top2, sum2, dot2
-):
-    near = bias_ref.shape[0] - off_ref.shape[1]
-    partial_stats(
-        q_ref, g_ref, off_ref.at[0], off_ref.at[1], bias_ref[near:, :], top2, sum2, dot2
-    )
+    q_ref, g_ref, off_ref, corner_ref, bias_ref, top_ref, sum_ref, dot_ref,
+    st_ref, kall_ref, vall_ref, top2, sum2, dot2,
+):
+    assemble(kall_ref, off_ref.at[0], corner_ref.at[0])
+    assemble(vall_ref, off_ref.at[1], corner_ref.at[1])
+    near = bias_ref.shape[0] - kall_ref.shape[0]
+    partial_stats(q_ref, g_ref, kall_ref, vall_ref, bias_ref[near:, :], top2, sum2, dot2)
     top = jnp.maximum(top_ref[...], top2[...])
     a, b = jnp.exp2(top_ref[...] - top), jnp.exp2(top2[...] - top)
     total = sum_ref[...] * a + sum2[...] * b
@@ -202,11 +213,12 @@
 
 
 def query_kernel(
-    q_ref, g_ref, kall_ref, vall_ref, corner_ref, near_ref, far_ref, st_ref, dq_ref
+    q_ref, g_ref, k_near, v_near, k_far, v_far, bias_near, bias_far, st_ref, dq_ref
 ):
     heads = q_ref.shape[1] // HEAD_DIM
-    near = near_ref.shape[1]
+    per = LANES // HEAD_DIM
     row = lax.broadcasted_iota(jnp.int32, (LANES, LANES), 0)
+    sides = ((k_near, v_near, bias_near), (k_far, v_far, bias_far))
 
     def stat_of(h):
         choose = (row == h) | (row == h + heads) | (row == h + 2 * heads)
@@ -216,24 +228,18 @@
     def wide(x, count):
         return jnp.concatenate([x] * -(-count // LANES), axis=1)[:, :count]
 
-    per = LANES // HEAD_DIM
     for at, first in groups(q_ref.shape[1]):
-        k_far = jnp.concatenate([kall_ref[near:, at], corner_ref[0, :, at]], axis=0)
-        v_far = jnp.concatenate([vall_ref[near:, at], corner_ref[1, :, at]], axis=0)
-        sides = (
-            (kall_ref[0:near, at], vall_ref[0:near, at], near_ref[...]),
-            (k_far, v_far, far_ref[...]),
-        )
         qs, gs = spread(q_ref[:, at]), spread(g_ref[:, at])
         logs = [stat_of(first + j) for j in range(per)]
         dots = [stat_of(first + j + 3 * heads) for j in range(per)]
         total = jnp.zeros((q_ref.shape[0], LANES), jnp.float32)
-        for kg, vg, bias in sides:
+        for keys, values, bias in sides:
+            kg, vg = keys[:, at], values[:, at]
             count = kg.shape[0]
             s, gp = dot_nt(qs, kg), dot_nt(gs, vg)
             ds = []
             for j in range(per):
-                p = jnp.exp2(part(s, j, 0) * (SCALE * LOG2E) + (bias - wide(logs[j], count)))
+                p = jnp.exp2(part(s, j, 0) * (SCALE * LOG2E) + (bias[...] - wide(logs[j], count)))
                 ds.append((p * (part(gp, j, 0) - wide(dots[j], count))).astype(jnp.bfloat16))
             ds = jnp.concatenate(ds, axis=0)
             total += gather(jnp.dot(ds, kg, preferred_element_type=jnp.float32))
@@ -303,11 +309,12 @@
     smem = pl.BlockSpec(memory_space=pltpu.SMEM)
     vmem = pl.BlockSpec(memory_space=pltpu.VMEM)
 
-    def call(body, outs, operands, scratch=(), flops=1 << 10, scalars=False):
+    def call(body, outs, operands, scratch=(), flops=1 << 10, scalars=False, space=pltpu.VMEM):
         return pl.pallas_call(
             body,
             out_shape=outs,
-            in_specs=[smem] * scalars + [vmem] * (len(operands) - scalars),
+            in_specs=[smem] * scalars
+            + [pl.BlockSpec(memory_space=space)] * (len(operands) - scalars),
             out_specs=jax.tree.map(lambda _: vmem, outs),
             scratch_shapes=scratch,
             compiler_params=pltpu.CompilerParams(vmem_limit_bytes=16 << 20),
@@ -319,11 +326,11 @@
 
     f32 = jnp.float32
     heads = width // HEAD_DIM
-    def strip_of(mine, other, even=even):
+    def strip_of(mine, other):
         side = [jnp.where(even, x[:, cols - RADIUS :], x[:, :RADIUS]) for x in (mine, other)]
         return jnp.concatenate([x.reshape(rows * RADIUS, -1) for x in side], axis=0)
 
-    def edge_of(mine, even=even):
+    def edge_of(mine):
         return jnp.where(even, mine[:RADIUS], mine[rows - RADIUS :]).reshape(n_off, -1)
 
     def corner_of(first, second):
@@ -341,29 +348,28 @@
     def flat(field):
         return field.reshape(n_own, field.shape[-1])
 
-    def strips(mine, other, even=even):
-        return jnp.stack([strip_of(a, b, even) for a, b in zip(mine, other)])
-
-    def edges(mine, even=even):
-        return jnp.stack([edge_of(a, even) for a in mine])
+    def strips(mine, other):
+        return jnp.stack([strip_of(a, b) for a, b in zip(mine, other)])
+
+    def edges(mine):
+        return jnp.stack([edge_of(a) for a in mine])
 
     def corners(first, second):
         return jnp.stack([corner_of(a, b) for a, b in zip(first, second)])
 
     key_o, value_o = send(key, pair), send(value, pair)
-    kv, kv_o = (key, value), (key_o, value_o)
     query_o, grad_o = send(query, pair), send(grad, pair)
-    qg, qg_o = (query, grad), (query_o, grad_o)
-    kv_strip = strips(kv, kv_o)
-    later, _ = lax.optimization_barrier((even, kv_strip))
+    mine = lax.optimization_barrier(jnp.stack([key, value, query, grad]))
+    kv_strip = strips(mine[:2], (key_o, value_o))
+    later, _ = lax.optimization_barrier((mine, kv_strip))
+    kv_edge = edges(later[:2])
     kv_1 = send(kv_strip, around)
-    kv_off = send(edges(kv, later), across)
-    qg_1 = send(strips(qg, qg_o, later), around)
+    kv_off = send(kv_edge, across)
+    qg_1 = send(strips(later[2:], (query_o, grad_o)), around)
     kv_2 = send(kv_1, pair)
     kv_last = corners(kv_1, kv_2)
     kv_corner = send(kv_last, across)
-    qg_1, place, _ = lax.optimization_barrier((qg_1, place, kv_last))
-    reach = pole_reach.astype(f32)
+    qg_1, place, pole_reach, _ = lax.optimization_barrier((qg_1, place, pole_reach, kv_last))
     table = np.concatenate(
         [layout(rows, cols, odd, pole) for odd in (False, True) for pole in (False, True)]
     )
@@ -374,25 +380,31 @@
             array(n_own, far, dtype=f32),
             array(near + far, n_own, dtype=f32),
         ),
-        (place, reach, reach.T, jnp.asarray(table)),
+        (place, pole_reach, jnp.asarray(table)),
+        [
+            pltpu.VMEM(pole_reach.shape, jnp.int32),
+            pltpu.VMEM(table.shape, jnp.int32),
+            pltpu.SemaphoreType.DMA((2,)),
+        ],
         scalars=True,
+        space=pltpu.HBM,
     )
 
     qg_2 = send(qg_1, pair)
-    qg_beyond = jnp.concatenate([edges(qg, later), corners(qg_1, qg_2)], axis=1)
+    qg_beyond = jnp.concatenate([edges(later[2:]), corners(qg_1, qg_2)], axis=1)
     bias_t, qg_beyond = lax.optimization_barrier((bias_t, qg_beyond))
 
-    q, k, v, g = (flat(x) for x in (query, key, value, grad))
+    k, v, q, g = (flat(x) for x in mine)
     stat = array(heads, n_own, dtype=f32)
-    kall, vall, *near_stats = call(
+    k_near, v_near, *near_stats = call(
         near_stats_kernel,
-        (array(near + n_off, width), array(near + n_off, width), stat, stat, stat),
-        (q, g, k, v, flat(key_o), flat(value_o), kv_1, kv_2, kv_off, bias_t),
-    )
-    stats = call(
+        (array(near, width), array(near, width), stat, stat, stat),
+        (q, g, k, v, flat(key_o), flat(value_o), kv_1, kv_2, bias_t),
+    )
+    stats, k_far, v_far = call(
         far_stats_kernel,
-        array(n_own, LANES),
-        (q, g, kv_corner, bias_t, *near_stats),
+        (array(n_own, LANES), array(far, width), array(far, width)),
+        (q, g, kv_off, kv_corner, bias_t, *near_stats),
         [pltpu.VMEM((heads, n_own), f32)] * 3,
     )
     stats_grid = stats.reshape(rows, cols, LANES)
@@ -402,10 +414,11 @@
     )
     st_1 = send(st_strip, around)
     qg_off = send(qg_beyond, across)
+    sums = array(n_own, width, dtype=f32)
     d_query = call(
         query_kernel,
         array(n_own, width),
-        (q, g, kall, vall, kv_corner, bias_near, bias_far, stats_q),
+        (q, g, k_near, v_near, k_far, v_far, bias_near, bias_far, stats_q),
     )
     st_1, d_query = lax.optimization_barrier((st_1, d_query))
     st_2 = send(st_1, pair)
@@ -413,7 +426,6 @@
         jnp.concatenate([edge_of(stats_grid), corner_of(st_1, st_2)], axis=0), across
     )
 
-    sums = array(n_own, width, dtype=f32)
     d_key, d_value = call(
         near_key_kernel,
         (sums, sums),

time: 46.1 us -> 43.7 us (0.948)
  local copies, waits for them, and re-layouts: 2.91 us -> 0.48 us
  waiting for transfers between devices: 15.2 us -> 17 us
  starting transfers between devices: 12.6 us -> 11.3 us
  other arithmetic: 2.49 us -> 2.02 us
    unnamed x14 -> x4, local copies, waits for them, and re-layouts: 2.45 us -> 0.01 us
    ppermute x15, waiting for transfers between devices: 15.2 us -> 17 us  [send(): return lax.ppermute(block, axes, route)]
    ppermute x15, starting transfers between devices: 12.6 us -> 11.3 us  [send(): return lax.ppermute(block, axes, route)]
    another operation x7 -> x8, other arithmetic: 0.1 us -> 1.26 us  [the longest x1 1.16 us: shards(): mine = lax.optimization_barrier(jnp.stack([key, value, query, grad]))]
    select_n x9 -> x8, other arithmetic: 1.06 us -> 0.19 us  [strip_of(): jnp.where(even, x[:, cols - RADIUS:], x[:, :RADIUS])]
    concatenate x1, other arithmetic: 0.77 us -> 0.03 us  [shards(): qg_beyond = jnp.concatenate([edges(later[2:]), corners(qg_1, qg_2)], axis=1)]
where the time goes in v5:
time: 43.7 us; the launch traced here: 43.5 us
  waiting for transfers between devices  17 us (39%)
  Pallas kernels  11.7 us (27%)
  starting transfers between devices  11.3 us (26%)
  other arithmetic  2.02 us (5%)
  between operations  0.99 us (2%)
  local copies, waits for them, and re-layouts  0.48 us (1%)
    ppermute x15, waiting for transfers between devices, send(): return lax.ppermute(block, axes, route)  17 us
    pallas_call x6, Pallas kernels, call(): pl.pallas_call(body, out_shape=outs, in_specs=[smem] * scalars + [pl.Bloc...  11.7 us
    ppermute x15, starting transfers between devices, send(): return lax.ppermute(block, axes, route)  11.3 us
    another operation x1, other arithmetic, shards(): mine = lax.optimization_barrier(jnp.stack([key, value, query, grad]))  1.16 us
  transfers between devices with their start and end apart: 15, of which 9 were waited for; matrix products, arithmetic and copies ran while one was open for 6% of the time, Pallas kernels for 20%

profile of v5, /device:TPU:0, one launch (start us, length us, event | category | flops | bytes accessed | tf_op | source)
XLA Modules:
  0.0 43.5 jit_solution(3747258534757277187)
XLA Ops:
  0.6 0.5 %collective-permute-start.6 = (bf16[8,16,512]{2,1,0:T(8,128)(2,1)}, bf16[8,16,512]{2,1,0:T(8,128)(2,1)S(1)}, u32[]{:S(2)}, u32[]{:S(2)}) collective-permute-start(bf16[8,16,512]{2,1,0:T(8,128)(2,1)} %param.6), channel_id=1, source_target_pairs={{0,4},{1,5},{2,6},{3,7},{4,0},{5,1},{6,2},{7,3},{8,12},{9,13},{10,... | collective-permute-start | bytes 393224 | tf_op jit(solution)/shard_map/ppermute | solution.py:346
  1.1 0.1 collective-permute-start
  1.2 0.4 collective-permute-start.1
  1.7 0.1 collective-permute-start.7
  1.7 1.2 %pad_maximum_fusion = bf16[4,8,16,512]{3,2,1,0:T(8,128)(2,1)S(1)} fusion(bf16[1,8,16,512]{3,2,1,0:T(8,128)(2,1)} %bitcast.92, bf16[1,8,16,512]{3,2,1,0:T(8,128)(2,1)} %bitcast.91, bf16[1,8,16,512]{3,2,1,0:T(8,128)(2,1)} %bitcast.90, bf16[1,8,16,512]{3,2,1,0:T(8,128)(2,1)} %bitcast.89), kind=kLoop, calls=%fused_computation | loop fusion | flops 786432 | bytes 1048576 | tf_op jit(solution)/shard_map/stack | solution.py:362
  2.9 0.1 fusion.6
  3.1 0.1 pad.31.clone
  3.1 0.1 pad.3.clone
  3.3 0.1 pad_add_fusion.sc_ref
  3.4 0.0 collective-permute-done
  3.4 0.0 collective-permute-done.1
  3.5 3.1 %collective-permute-start.3 = (bf16[2,96,512]{2,1,0:T(8,128)(2,1)S(1)}, bf16[2,96,512]{2,1,0:T(8,128)(2,1)S(1)}, u32[]{:S(2)}, u32[]{:S(2)}) collective-permute-start(bf16[2,96,512]{2,1,0:T(8,128)(2,1)S(1)} %pad_maximum_fusion.1), channel_id=1, source_target_pairs={{0,1},{1,2},{2,3},{3,0},{4,7},{5,4},{6,5},{7,6},{8,9},{9,10},{10,1... | collective-permute-start | bytes 589832 | tf_op jit(solution)/shard_map/ppermute | solution.py:346
  6.6 0.0 collective-permute-done.6
  6.7 0.0 collective-permute-done.7
  7.0 1.6 %collective-permute-start.8 = (bf16[2,96,512]{2,1,0:T(8,128)(2,1)S(1)}, bf16[2,96,512]{2,1,0:T(8,128)(2,1)S(1)}, u32[]{:S(2)}, u32[]{:S(2)}) collective-permute-start(bf16[2,96,512]{2,1,0:T(8,128)(2,1)S(1)} %pad_maximum_fusion.3), channel_id=1, source_target_pairs={{0,1},{1,2},{2,3},{3,0},{4,7},{5,4},{6,5},{7,6},{8,9},{9,10},{10,1... | collective-permute-start | bytes 589832 | tf_op jit(solution)/shard_map/ppermute | solution.py:346
  8.6 1.1 %collective-permute-start.2 = (bf16[2,96,512]{2,1,0:T(8,128)(2,1)S(1)}, bf16[2,96,512]{2,1,0:T(8,128)(2,1)S(1)}, u32[]{:S(2)}, u32[]{:S(2)}) collective-permute-start(bf16[2,96,512]{2,1,0:T(8,128)(2,1)S(1)} %pad_maximum_fusion.2), channel_id=1, source_target_pairs={{0,2},{1,3},{2,0},{3,1},{4,8},{5,9},{6,10},{7,11},{8,4},{9,5},{10,... | collective-permute-start | bytes 589832 | tf_op jit(solution)/shard_map/ppermute | solution.py:346
  9.7 4.6 %collective-permute-done.3.lc_ref = bf16[2,96,512]{2,1,0:T(8,128)(2,1)S(1)} collective-permute-done((bf16[2,96,512]{2,1,0:T(8,128)(2,1)S(1)}, bf16[2,96,512]{2,1,0:T(8,128)(2,1)S(1)}, u32[]{:S(2)}, u32[]{:S(2)}) %collective-permute-start.3) | collective-permute-done | bytes 196640 | tf_op jit(solution)/shard_map/ppermute | solution.py:346
  14.3 0.0 collective-permute-start.4
  14.3 1.4 %collective-permute-done.4.s2_ref = bf16[2,96,512]{2,1,0:T(8,128)(2,1)S(1)} collective-permute-done((bf16[2,96,512]{2,1,0:T(8,128)(2,1)S(1)}, bf16[2,96,512]{2,1,0:T(8,128)(2,1)S(1)}, u32[]{:S(2)}, u32[]{:S(2)}) %collective-permute-start.4) | collective-permute-done | bytes 196640 | tf_op jit(solution)/shard_map/ppermute | solution.py:346
  15.8 0.1 maximum_bitcast_fusion.4
  15.9 0.0 copy-start
  15.9 0.0 copy-start.1
  15.9 0.1 collective-permute-start.5
  16.0 2.2 %collective-permute-done.8.lc_ref = bf16[2,96,512]{2,1,0:T(8,128)(2,1)S(1)} collective-permute-done((bf16[2,96,512]{2,1,0:T(8,128)(2,1)S(1)}, bf16[2,96,512]{2,1,0:T(8,128)(2,1)S(1)}, u32[]{:S(2)}, u32[]{:S(2)}) %collective-permute-start.8) | collective-permute-done | bytes 196640 | tf_op jit(solution)/shard_map/ppermute | solution.py:346
  18.2 0.1 collective-permute-start.9
  18.3 0.0 copy-done
  18.3 0.0 copy-done.1
  18.3 1.0 %shard_map.85 = (f32[128,448]{1,0:T(8,128)S(1)}, f32[128,176]{1,0:T(8,128)S(1)}, f32[624,128]{1,0:T(8,128)S(1)}) custom-call(s32[2]{0:T(128)S(1)} %pad_add_fusion.sc_ref, s32[2,64]{1,0:T(2,128)S(1)} %copy-done.1, s32[8,624]{1,0:T(8,128)S(1)} %copy-done), custom_call_target="tpu_custom_call" | custom-call | flops 1024 | bytes 1024 | tf_op jit(solution)/shard_map/pallas_call | solution.py:313
  19.4 0.3 collective-permute-done.9.s2_ref
  19.6 0.1 maximum_bitcast_fusion.6
  19.8 1.4 %shard_map.86 = (bf16[448,512]{1,0:T(8,128)(2,1)S(1)}, bf16[448,512]{1,0:T(8,128)(2,1)S(1)}, f32[16,128]{1,0:T(8,128)S(1)}, f32[16,128]{1,0:T(8,128)S(1)}, f32[16,128]{1,0:T(8,128)S(1)}) custom-call(bf16[128,512]{1,0:T(8,128)(2,1)S(1)} %bitcast.67, bf16[128,512]{1,0:T(8,128)(2,1)S(1)} %bitcast.63, bf16[128,512]{1,0:T(8,128)(2,1)S(1)} %bitcast.74, ...), custom_call_target="tpu_custom_call" | custom-call | flops 1024 | bytes 1024 | tf_op jit(solution)/shard_map/pallas_call | solution.py:313
  21.2 1.9 %collective-permute-done.2.off_ref = bf16[2,96,512]{2,1,0:T(8,128)(2,1)S(1)} collective-permute-done((bf16[2,96,512]{2,1,0:T(8,128)(2,1)S(1)}, bf16[2,96,512]{2,1,0:T(8,128)(2,1)S(1)}, u32[]{:S(2)}, u32[]{:S(2)}) %collective-permute-start.2) | collective-permute-done | bytes 196640 | tf_op jit(solution)/shard_map/ppermute | solution.py:346
  23.1 1.8 %collective-permute-done.5.corner_ref = bf16[2,80,512]{2,1,0:T(8,128)(2,1)S(1)} collective-permute-done((bf16[2,80,512]{2,1,0:T(8,128)(2,1)S(1)}, bf16[2,80,512]{2,1,0:T(8,128)(2,1)S(1)}, u32[]{:S(2)}, u32[]{:S(2)}) %collective-permute-start.5) | collective-permute-done | bytes 163872 | tf_op jit(solution)/shard_map/ppermute | solution.py:346
  24.8 0.8 %shard_map.87 = (bf16[128,128]{1,0:T(8,128)(2,1)S(1)}, bf16[176,512]{1,0:T(8,128)(2,1)S(1)}, bf16[176,512]{1,0:T(8,128)(2,1)S(1)}) custom-call(bf16[128,512]{1,0:T(8,128)(2,1)S(1)} %bitcast.68, bf16[128,512]{1,0:T(8,128)(2,1)S(1)} %bitcast.64, bf16[2,96,512]{2,1,0:T(8,128)(2,1)S(1)} %collective-permute-done.2.off_ref, ...), custom_call_target="tpu_custom_call" | custom-call | flops 1024 | bytes 1024 | tf_op jit(solution)/shard_map/pallas_call | solution.py:313
  25.7 0.1 collective-permute-start.10
  25.8 1.2 %collective-permute-done.10 = bf16[8,16,128]{2,1,0:T(8,128)(2,1)S(1)} collective-permute-done((bf16[8,16,128]{2,1,0:T(8,128)(2,1)S(1)}, bf16[8,16,128]{2,1,0:T(8,128)(2,1)S(1)}, u32[]{:S(2)}, u32[]{:S(2)}) %collective-permute-start.10) | collective-permute-done | bytes 32800 | tf_op jit(solution)/shard_map/ppermute | solution.py:346
  27.0 0.6 %collective-permute-start.11 = (bf16[96,128]{1,0:T(8,128)(2,1)S(1)}, bf16[96,128]{1,0:T(8,128)(2,1)S(1)}, u32[]{:S(2)}, u32[]{:S(2)}) collective-permute-start(bf16[96,128]{1,0:T(8,128)(2,1)S(1)} %pad_maximum_fusion.5), channel_id=1, source_target_pairs={{0,1},{1,2},{2,3},{3,0},{4,7},{5,4},{6,5},{7,6},{8,9},{9,10},{10,1... | collective-permute-start | bytes 73736 | tf_op jit(solution)/shard_map/ppermute | solution.py:346
  27.6 3.4 %collective-permute-start.12 = (bf16[2,176,512]{2,1,0:T(8,128)(2,1)S(1)}, bf16[2,176,512]{2,1,0:T(8,128)(2,1)S(1)}, u32[]{:S(2)}, u32[]{:S(2)}) collective-permute-start(bf16[2,176,512]{2,1,0:T(8,128)(2,1)S(1)} %maximum_maximum_fusion), channel_id=1, source_target_pairs={{0,2},{1,3},{2,0},{3,1},{4,8},{5,9},{6,10},{7,11},{8,4},{9,5},{10,... | collective-permute-start | bytes 1081352 | tf_op jit(solution)/shard_map/ppermute | solution.py:346
  31.0 3.8 %shard_map.88 = bf16[128,512]{1,0:T(8,128)(2,1)} custom-call(bf16[128,512]{1,0:T(8,128)(2,1)S(1)} %bitcast.69, bf16[128,512]{1,0:T(8,128)(2,1)S(1)} %bitcast.65, bf16[448,512]{1,0:T(8,128)(2,1)S(1)} %get-tuple-element.41.k_near, bf16[448,512]{1,0:T(8,128)(2,1)S(1)} %get-tuple-element.42.v_near, bf16[176,512]{1,0:T(8,128)(2,1)S(1)} %get-tuple-element.43.k_far, ...), custom_call_target="tpu_custom_call" | custom-call | flops 1024 | bytes 1024 | tf_op jit(solution)/shard_map/pallas_call | solution.py:313
  34.8 0.0 collective-permute-done.11.st_lc
  34.8 0.0 collective-permute-start.13
  34.8 1.2 %collective-permute-done.13.st_s2 = bf16[96,128]{1,0:T(8,128)(2,1)S(1)} collective-permute-done((bf16[96,128]{1,0:T(8,128)(2,1)S(1)}, bf16[96,128]{1,0:T(8,128)(2,1)S(1)}, u32[]{:S(2)}, u32[]{:S(2)}) %collective-permute-start.13) | collective-permute-done | bytes 24608 | tf_op jit(solution)/shard_map/ppermute | solution.py:346
  36.0 0.1 maximum_maximum_fusion.1
  36.1 0.1 collective-permute-start.14
  36.2 2.6 %shard_map.89 = (f32[128,512]{1,0:T(8,128)S(1)}, f32[128,512]{1,0:T(8,128)S(1)}) custom-call(bf16[128,512]{1,0:T(8,128)(2,1)S(1)} %bitcast.75, bf16[128,512]{1,0:T(8,128)(2,1)S(1)} %bitcast.72, bf16[128,512]{1,0:T(8,128)(2,1)S(1)} %bitcast.70, bf16[128,512]{1,0:T(8,128)(2,1)S(1)} %bitcast.66, bf16[128,512]{1,0:T(8,128)(2,1)S(1)} %bitcast.79, ...), custom_call_target="tpu_custom_call" | custom-call | flops 1024 | bytes 1024 | tf_op jit(solution)/shard_map/pallas_call | solution.py:313
  38.8 2.7 %collective-permute-done.14.st_off = bf16[176,128]{1,0:T(8,128)(2,1)S(1)} collective-permute-done((bf16[176,128]{1,0:T(8,128)(2,1)S(1)}, bf16[176,128]{1,0:T(8,128)(2,1)S(1)}, u32[]{:S(2)}, u32[]{:S(2)}) %collective-permute-start.14) | collective-permute-done | bytes 45088 | tf_op jit(solution)/shard_map/ppermute | solution.py:346
  41.5 0.0 collective-permute-done.12.off_ref
  41.5 2.0 %shard_map.90 = (bf16[128,512]{1,0:T(8,128)(2,1)}, bf16[128,512]{1,0:T(8,128)(2,1)}) custom-call(bf16[128,512]{1,0:T(8,128)(2,1)S(1)} %bitcast.76, bf16[128,512]{1,0:T(8,128)(2,1)S(1)} %bitcast.73, bf16[2,176,512]{2,1,0:T(8,128)(2,1)S(1)} %collective-permute-done.12.off_ref, bf16[176,128]{1,0:T(8,128)(2,1)S(1)} %collective-permute-done.14.st_off, ...), custom_call_target="tpu_custom_call" | custom-call | flops 1024 | bytes 1024 | tf_op jit(solution)/shard_map/pallas_call | solution.py:313
  (38 shorter events, 0.7 us)
Async XLA Ops:
  0.6 6.0 %collective-permute-start.6 = (bf16[8,16,512]{2,1,0:T(8,128)(2,1)}, bf16[8,16,512]{2,1,0:T(8,128)(2,1)S(1)}, u32[]{:S(2)}, u32[]{:S(2)}) collective-permute-start(bf16[8,16,512]{2,1,0:T(8,128)(2,1)} %param.6), channel_id=1, source_target_pairs={{0,4},{1,5},{2,6},{3,7},{4,0},{5,1},{6,2},{7,3},{8,12},{9,13},{10,... | collective-permute-start | bytes 393224 | tf_op jit(solution)/shard_map/ppermute | solution.py:346
  1.1 2.2 %collective-permute-start = (bf16[8,16,512]{2,1,0:T(8,128)(2,1)}, bf16[8,16,512]{2,1,0:T(8,128)(2,1)S(1)}, u32[]{:S(2)}, u32[]{:S(2)}) collective-permute-start(bf16[8,16,512]{2,1,0:T(8,128)(2,1)} %param.7), channel_id=1, source_target_pairs={{0,4},{1,5},{2,6},{3,7},{4,0},{5,1},{6,2},{7,3},{8,12},{9,13},{10,... | collective-permute-start | bytes 393224 | tf_op jit(solution)/shard_map/ppermute | solution.py:346
  1.2 2.1 %collective-permute-start.1 = (bf16[8,16,512]{2,1,0:T(8,128)(2,1)}, bf16[8,16,512]{2,1,0:T(8,128)(2,1)S(1)}, u32[]{:S(2)}, u32[]{:S(2)}) collective-permute-start(bf16[8,16,512]{2,1,0:T(8,128)(2,1)} %param.8), channel_id=1, source_target_pairs={{0,4},{1,5},{2,6},{3,7},{4,0},{5,1},{6,2},{7,3},{8,12},{9,13},{10,... | collective-permute-start | bytes 393224 | tf_op jit(solution)/shard_map/ppermute | solution.py:346
  1.7 5.0 %collective-permute-start.7 = (bf16[8,16,512]{2,1,0:T(8,128)(2,1)}, bf16[8,16,512]{2,1,0:T(8,128)(2,1)S(1)}, u32[]{:S(2)}, u32[]{:S(2)}) collective-permute-start(bf16[8,16,512]{2,1,0:T(8,128)(2,1)} %param.9), channel_id=1, source_target_pairs={{0,4},{1,5},{2,6},{3,7},{4,0},{5,1},{6,2},{7,3},{8,12},{9,13},{10,... | collective-permute-start | bytes 393224 | tf_op jit(solution)/shard_map/ppermute | solution.py:346
  3.5 10.8 %collective-permute-start.3 = (bf16[2,96,512]{2,1,0:T(8,128)(2,1)S(1)}, bf16[2,96,512]{2,1,0:T(8,128)(2,1)S(1)}, u32[]{:S(2)}, u32[]{:S(2)}) collective-permute-start(bf16[2,96,512]{2,1,0:T(8,128)(2,1)S(1)} %pad_maximum_fusion.1), channel_id=1, source_target_pairs={{0,1},{1,2},{2,3},{3,0},{4,7},{5,4},{6,5},{7,6},{8,9},{9,10},{10,1... | collective-permute-start | bytes 589832 | tf_op jit(solution)/shard_map/ppermute | solution.py:346
  7.0 11.2 %collective-permute-start.8 = (bf16[2,96,512]{2,1,0:T(8,128)(2,1)S(1)}, bf16[2,96,512]{2,1,0:T(8,128)(2,1)S(1)}, u32[]{:S(2)}, u32[]{:S(2)}) collective-permute-start(bf16[2,96,512]{2,1,0:T(8,128)(2,1)S(1)} %pad_maximum_fusion.3), channel_id=1, source_target_pairs={{0,1},{1,2},{2,3},{3,0},{4,7},{5,4},{6,5},{7,6},{8,9},{9,10},{10,1... | collective-permute-start | bytes 589832 | tf_op jit(solution)/shard_map/ppermute | solution.py:346
  8.6 14.5 %collective-permute-start.2 = (bf16[2,96,512]{2,1,0:T(8,128)(2,1)S(1)}, bf16[2,96,512]{2,1,0:T(8,128)(2,1)S(1)}, u32[]{:S(2)}, u32[]{:S(2)}) collective-permute-start(bf16[2,96,512]{2,1,0:T(8,128)(2,1)S(1)} %pad_maximum_fusion.2), channel_id=1, source_target_pairs={{0,2},{1,3},{2,0},{3,1},{4,8},{5,9},{6,10},{7,11},{8,4},{9,5},{10,... | collective-permute-start | bytes 589832 | tf_op jit(solution)/shard_map/ppermute | solution.py:346
  14.3 1.4 %collective-permute-start.4 = (bf16[2,96,512]{2,1,0:T(8,128)(2,1)S(1)}, bf16[2,96,512]{2,1,0:T(8,128)(2,1)S(1)}, u32[]{:S(2)}, u32[]{:S(2)}) collective-permute-start(bf16[2,96,512]{2,1,0:T(8,128)(2,1)S(1)} %collective-permute-done.3.lc_ref), channel_id=1, source_target_pairs={{0,4},{1,5},{2,6},{3,7},{4,0},{5,1},{6,2},{7,3},{8,12},{9,13},{10,... | collective-permute-start | bytes 589832 | tf_op jit(solution)/shard_map/ppermute | solution.py:346
  15.9 2.5 %copy-start = (s32[8,624]{1,0:T(8,128)S(1)}, s32[8,624]{1,0:T(8,128)}, u32[]{:S(2)}) copy-start(s32[8,624]{1,0:T(8,128)} %constant.20.clone.table_hbm) | copy-start | bytes 59908
  15.9 2.5 %copy-start.1 = (s32[2,64]{1,0:T(2,128)S(1)}, s32[2,64]{1,0:T(2,128)}, u32[]{:S(2)}) copy-start(s32[2,64]{1,0:T(2,128)} %reach_hbm) | copy-start | bytes 1540
  15.9 8.9 %collective-permute-start.5 = (bf16[2,80,512]{2,1,0:T(8,128)(2,1)S(1)}, bf16[2,80,512]{2,1,0:T(8,128)(2,1)S(1)}, u32[]{:S(2)}, u32[]{:S(2)}) collective-permute-start(bf16[2,80,512]{2,1,0:T(8,128)(2,1)S(1)} %pad_maximum_fusion.4), channel_id=1, source_target_pairs={{0,2},{1,3},{2,0},{3,1},{4,8},{5,9},{6,10},{7,11},{8,4},{9,5},{10,... | collective-permute-start | bytes 491528 | tf_op jit(solution)/shard_map/ppermute | solution.py:346
  18.2 1.4 %collective-permute-start.9 = (bf16[2,96,512]{2,1,0:T(8,128)(2,1)S(1)}, bf16[2,96,512]{2,1,0:T(8,128)(2,1)S(1)}, u32[]{:S(2)}, u32[]{:S(2)}) collective-permute-start(bf16[2,96,512]{2,1,0:T(8,128)(2,1)S(1)} %collective-permute-done.8.lc_ref), channel_id=1, source_target_pairs={{0,4},{1,5},{2,6},{3,7},{4,0},{5,1},{6,2},{7,3},{8,12},{9,13},{10,... | collective-permute-start | bytes 589832 | tf_op jit(solution)/shard_map/ppermute | solution.py:346
  25.7 1.3 %collective-permute-start.10 = (bf16[8,16,128]{2,1,0:T(8,128)(2,1)S(1)}, bf16[8,16,128]{2,1,0:T(8,128)(2,1)S(1)}, u32[]{:S(2)}, u32[]{:S(2)}) collective-permute-start(bf16[8,16,128]{2,1,0:T(8,128)(2,1)S(1)} %bitcast.77), channel_id=1, source_target_pairs={{0,4},{1,5},{2,6},{3,7},{4,0},{5,1},{6,2},{7,3},{8,12},{9,13},{10,... | collective-permute-start | bytes 98312 | tf_op jit(solution)/shard_map/ppermute | solution.py:346
  27.0 7.8 %collective-permute-start.11 = (bf16[96,128]{1,0:T(8,128)(2,1)S(1)}, bf16[96,128]{1,0:T(8,128)(2,1)S(1)}, u32[]{:S(2)}, u32[]{:S(2)}) collective-permute-start(bf16[96,128]{1,0:T(8,128)(2,1)S(1)} %pad_maximum_fusion.5), channel_id=1, source_target_pairs={{0,1},{1,2},{2,3},{3,0},{4,7},{5,4},{6,5},{7,6},{8,9},{9,10},{10,1... | collective-permute-start | bytes 73736 | tf_op jit(solution)/shard_map/ppermute | solution.py:346
  27.6 13.9 %collective-permute-start.12 = (bf16[2,176,512]{2,1,0:T(8,128)(2,1)S(1)}, bf16[2,176,512]{2,1,0:T(8,128)(2,1)S(1)}, u32[]{:S(2)}, u32[]{:S(2)}) collective-permute-start(bf16[2,176,512]{2,1,0:T(8,128)(2,1)S(1)} %maximum_maximum_fusion), channel_id=1, source_target_pairs={{0,2},{1,3},{2,0},{3,1},{4,8},{5,9},{6,10},{7,11},{8,4},{9,5},{10,... | collective-permute-start | bytes 1081352 | tf_op jit(solution)/shard_map/ppermute | solution.py:346
  34.8 1.2 %collective-permute-start.13 = (bf16[96,128]{1,0:T(8,128)(2,1)S(1)}, bf16[96,128]{1,0:T(8,128)(2,1)S(1)}, u32[]{:S(2)}, u32[]{:S(2)}) collective-permute-start(bf16[96,128]{1,0:T(8,128)(2,1)S(1)} %collective-permute-done.11.st_lc), channel_id=1, source_target_pairs={{0,4},{1,5},{2,6},{3,7},{4,0},{5,1},{6,2},{7,3},{8,12},{9,13},{10,... | collective-permute-start | bytes 73736 | tf_op jit(solution)/shard_map/ppermute | solution.py:346
  36.1 5.4 %collective-permute-start.14 = (bf16[176,128]{1,0:T(8,128)(2,1)S(1)}, bf16[176,128]{1,0:T(8,128)(2,1)S(1)}, u32[]{:S(2)}, u32[]{:S(2)}) collective-permute-start(bf16[176,128]{1,0:T(8,128)(2,1)S(1)} %maximum_maximum_fusion.1), channel_id=1, source_target_pairs={{0,2},{1,3},{2,0},{3,1},{4,8},{5,9},{6,10},{7,11},{8,4},{9,5},{10,... | collective-permute-start | bytes 135176 | tf_op jit(solution)/shard_map/ppermute | solution.py:346

commit v6 on v5

--- a/solution.py
+++ b/solution.py
@@ -35,7 +35,7 @@
 
 def pieces(rows, cols):
     corners = 2 * RADIUS * RADIUS
-    pad = -corners % 16
+    pad = -corners % 8
     strip = 2 * rows * RADIUS
     return rows * cols, rows * cols, strip, strip, RADIUS * cols, corners + pad
 
@@ -213,8 +213,12 @@
 
 
 def query_kernel(
-    q_ref, g_ref, k_near, v_near, k_far, v_far, bias_near, bias_far, st_ref, dq_ref
-):
+    q_ref, g_ref, k_near, v_near, k_far, v_far, bias_near, bias_far, st_ref, *refs
+):
+    dq_ref = refs[-1]
+    half = q_ref.shape[1] // 2
+    if len(refs) > 1:
+        dq_ref[:, 0:half] = refs[0][...]
     heads = q_ref.shape[1] // HEAD_DIM
     per = LANES // HEAD_DIM
     row = lax.broadcasted_iota(jnp.int32, (LANES, LANES), 0)
@@ -229,6 +233,8 @@
         return jnp.concatenate([x] * -(-count // LANES), axis=1)[:, :count]
 
     for at, first in groups(q_ref.shape[1]):
+        if (at.start >= half) != (len(refs) > 1):
+            continue
         qs, gs = spread(q_ref[:, at]), spread(g_ref[:, at])
         logs = [stat_of(first + j) for j in range(per)]
         dots = [stat_of(first + j + 3 * heads) for j in range(per)]
@@ -409,26 +415,22 @@
     )
     stats_grid = stats.reshape(rows, cols, LANES)
     stats_o = send(stats_grid, pair)
-    st_strip, qg_beyond, stats_q = lax.optimization_barrier(
-        (strip_of(stats_grid, stats_o), qg_beyond, stats)
-    )
+    st_strip, stats_q = lax.optimization_barrier((strip_of(stats_grid, stats_o), stats))
     st_1 = send(st_strip, around)
     qg_off = send(qg_beyond, across)
-    sums = array(n_own, width, dtype=f32)
-    d_query = call(
-        query_kernel,
-        array(n_own, width),
-        (q, g, k_near, v_near, k_far, v_far, bias_near, bias_far, stats_q),
-    )
+    query_side = (q, g, k_near, v_near, k_far, v_far, bias_near, bias_far)
+    d_query = call(query_kernel, array(n_own, width // 2), (*query_side, stats_q))
     st_1, d_query = lax.optimization_barrier((st_1, d_query))
     st_2 = send(st_1, pair)
+    _, stats_q = lax.optimization_barrier((st_2, stats))
     st_off = send(
         jnp.concatenate([edge_of(stats_grid), corner_of(st_1, st_2)], axis=0), across
     )
 
+    d_query = call(query_kernel, array(n_own, width), (*query_side, stats_q, d_query))
     d_key, d_value = call(
         near_key_kernel,
-        (sums, sums),
+        (array(n_own, width, dtype=f32),) * 2,
         (
             k, v, q, g, flat(query_o), flat(grad_o), qg_1, qg_2,
             stats, flat(stats_o), st_1, st_2, bias_near,

time: 43.7 us -> 42.6 us (0.975)
  waiting for transfers between devices: 17 us -> 16 us
    ppermute x15, waiting for transfers between devices: 17 us -> 16 us  [send(): return lax.ppermute(block, axes, route)]
    pallas_call x6 -> x7, Pallas kernels: 11.7 us -> 12 us  [call(): pl.pallas_call(body, out_shape=outs, in_specs=[smem] * scalars + [pl.Bloc...]
  transfers between devices with their start and end apart: 15 -> 15, of which waited for: 9 -> 9; matrix products, arithmetic and copies ran while one was open for 6% -> 5% of each run, Pallas kernels for 20% -> 21%
where the time goes in v6:
time: 42.6 us; the launch traced here: 42.5 us
  waiting for transfers between devices  16 us (38%)
  Pallas kernels  12 us (28%)
  starting transfers between devices  11.3 us (27%)
  other arithmetic  1.82 us (4%)
  between operations  1.03 us (2%)
    ppermute x15, waiting for transfers between devices, send(): return lax.ppermute(block, axes, route)  16 us
    pallas_call x7, Pallas kernels, call(): pl.pallas_call(body, out_shape=outs, in_specs=[smem] * scalars + [pl.Bloc...  12 us
    ppermute x15, starting transfers between devices, send(): return lax.ppermute(block, axes, route)  11.3 us
    another operation x1, other arithmetic, shards(): mine = lax.optimization_barrier(jnp.stack([key, value, query, grad]))  1.16 us
  transfers between devices with their start and end apart: 15, of which 9 were waited for; matrix products, arithmetic and copies ran while one was open for 5% of the time, Pallas kernels for 21%

profile of v6, /device:TPU:0, one launch (start us, length us, event | category | flops | bytes accessed | tf_op | source)
XLA Modules:
  0.0 42.5 jit_solution(16840447880978759714)
XLA Ops:
  0.6 0.5 %collective-permute-start.4 = (bf16[8,16,512]{2,1,0:T(8,128)(2,1)}, bf16[8,16,512]{2,1,0:T(8,128)(2,1)S(1)}, u32[]{:S(2)}, u32[]{:S(2)}) collective-permute-start(bf16[8,16,512]{2,1,0:T(8,128)(2,1)} %param.6), channel_id=1, source_target_pairs={{0,4},{1,5},{2,6},{3,7},{4,0},{5,1},{6,2},{7,3},{8,12},{9,13},{10,... | collective-permute-start | bytes 393224 | tf_op jit(solution)/shard_map/ppermute | solution.py:352
  1.1 0.1 collective-permute-start
  1.2 0.4 %collective-permute-start.1 = (bf16[8,16,512]{2,1,0:T(8,128)(2,1)}, bf16[8,16,512]{2,1,0:T(8,128)(2,1)S(1)}, u32[]{:S(2)}, u32[]{:S(2)}) collective-permute-start(bf16[8,16,512]{2,1,0:T(8,128)(2,1)} %param.8), channel_id=1, source_target_pairs={{0,4},{1,5},{2,6},{3,7},{4,0},{5,1},{6,2},{7,3},{8,12},{9,13},{10,... | collective-permute-start | bytes 393224 | tf_op jit(solution)/shard_map/ppermute | solution.py:352
  1.7 0.1 collective-permute-start.5
  1.7 1.2 %pad_maximum_fusion = bf16[4,8,16,512]{3,2,1,0:T(8,128)(2,1)S(1)} fusion(bf16[1,8,16,512]{3,2,1,0:T(8,128)(2,1)} %bitcast.94, bf16[1,8,16,512]{3,2,1,0:T(8,128)(2,1)} %bitcast.93, bf16[1,8,16,512]{3,2,1,0:T(8,128)(2,1)} %bitcast.92, bf16[1,8,16,512]{3,2,1,0:T(8,128)(2,1)} %bitcast.91), kind=kLoop, calls=%fused_computation | loop fusion | flops 786432 | bytes 1048576 | tf_op jit(solution)/shard_map/stack | solution.py:368
  2.9 0.1 slice_bitcast_fusion.3
  3.1 0.1 pad_add_fusion.sc_ref
  3.2 0.0 collective-permute-done
  3.2 0.0 collective-permute-done.1
  3.4 3.1 %collective-permute-start.2 = (bf16[2,96,512]{2,1,0:T(8,128)(2,1)S(1)}, bf16[2,96,512]{2,1,0:T(8,128)(2,1)S(1)}, u32[]{:S(2)}, u32[]{:S(2)}) collective-permute-start(bf16[2,96,512]{2,1,0:T(8,128)(2,1)S(1)} %pad_maximum_fusion.1), channel_id=1, source_target_pairs={{0,1},{1,2},{2,3},{3,0},{4,7},{5,4},{6,5},{7,6},{8,9},{9,10},{10,1... | collective-permute-start | bytes 589832 | tf_op jit(solution)/shard_map/ppermute | solution.py:352
  6.5 0.0 collective-permute-done.4
  6.5 0.0 collective-permute-done.5
  6.8 1.6 %collective-permute-start.6 = (bf16[2,96,512]{2,1,0:T(8,128)(2,1)S(1)}, bf16[2,96,512]{2,1,0:T(8,128)(2,1)S(1)}, u32[]{:S(2)}, u32[]{:S(2)}) collective-permute-start(bf16[2,96,512]{2,1,0:T(8,128)(2,1)S(1)} %pad_maximum_fusion.2), channel_id=1, source_target_pairs={{0,1},{1,2},{2,3},{3,0},{4,7},{5,4},{6,5},{7,6},{8,9},{9,10},{10,1... | collective-permute-start | bytes 589832 | tf_op jit(solution)/shard_map/ppermute | solution.py:352
  8.5 1.1 %collective-permute-start.8 = (bf16[2,96,512]{2,1,0:T(8,128)(2,1)S(1)}, bf16[2,96,512]{2,1,0:T(8,128)(2,1)S(1)}, u32[]{:S(2)}, u32[]{:S(2)}) collective-permute-start(bf16[2,96,512]{2,1,0:T(8,128)(2,1)S(1)} %pad_maximum_fusion.3), channel_id=1, source_target_pairs={{0,2},{1,3},{2,0},{3,1},{4,8},{5,9},{6,10},{7,11},{8,4},{9,5},{10,... | collective-permute-start | bytes 589832 | tf_op jit(solution)/shard_map/ppermute | solution.py:352
  9.6 4.6 %collective-permute-done.2.lc_ref = bf16[2,96,512]{2,1,0:T(8,128)(2,1)S(1)} collective-permute-done((bf16[2,96,512]{2,1,0:T(8,128)(2,1)S(1)}, bf16[2,96,512]{2,1,0:T(8,128)(2,1)S(1)}, u32[]{:S(2)}, u32[]{:S(2)}) %collective-permute-start.2) | collective-permute-done | bytes 196640 | tf_op jit(solution)/shard_map/ppermute | solution.py:352
  14.1 0.0 collective-permute-start.3
  14.2 1.4 %collective-permute-done.3.s2_ref = bf16[2,96,512]{2,1,0:T(8,128)(2,1)S(1)} collective-permute-done((bf16[2,96,512]{2,1,0:T(8,128)(2,1)S(1)}, bf16[2,96,512]{2,1,0:T(8,128)(2,1)S(1)}, u32[]{:S(2)}, u32[]{:S(2)}) %collective-permute-start.3) | collective-permute-done | bytes 196640 | tf_op jit(solution)/shard_map/ppermute | solution.py:352
  15.7 0.0 copy-start
  15.7 0.0 copy-start.1
  15.7 0.1 collective-permute-start.9
  15.8 2.2 %collective-permute-done.6.lc_ref = bf16[2,96,512]{2,1,0:T(8,128)(2,1)S(1)} collective-permute-done((bf16[2,96,512]{2,1,0:T(8,128)(2,1)S(1)}, bf16[2,96,512]{2,1,0:T(8,128)(2,1)S(1)}, u32[]{:S(2)}, u32[]{:S(2)}) %collective-permute-start.6) | collective-permute-done | bytes 196640 | tf_op jit(solution)/shard_map/ppermute | solution.py:352
  18.0 0.1 collective-permute-start.7
  18.2 0.0 copy-done
  18.2 0.0 copy-done.1
  18.2 1.0 %shard_map.85 = (f32[128,448]{1,0:T(8,128)S(1)}, f32[128,168]{1,0:T(8,128)S(1)}, f32[616,128]{1,0:T(8,128)S(1)}) custom-call(s32[2]{0:T(128)S(1)} %pad_add_fusion.sc_ref, s32[2,64]{1,0:T(2,128)S(1)} %copy-done.1, s32[8,616]{1,0:T(8,128)S(1)} %copy-done), custom_call_target="tpu_custom_call" | custom-call | flops 1024 | bytes 1024 | tf_op jit(solution)/shard_map/pallas_call | solution.py:319
  19.2 0.3 collective-permute-done.7.s2_ref
  19.6 1.4 %shard_map.86 = (bf16[448,512]{1,0:T(8,128)(2,1)S(1)}, bf16[448,512]{1,0:T(8,128)(2,1)S(1)}, f32[16,128]{1,0:T(8,128)S(1)}, f32[16,128]{1,0:T(8,128)S(1)}, f32[16,128]{1,0:T(8,128)S(1)}) custom-call(bf16[128,512]{1,0:T(8,128)(2,1)S(1)} %bitcast.68, bf16[128,512]{1,0:T(8,128)(2,1)S(1)} %bitcast.63, bf16[128,512]{1,0:T(8,128)(2,1)S(1)} %bitcast.76, ...), custom_call_target="tpu_custom_call" | custom-call | flops 1024 | bytes 1024 | tf_op jit(solution)/shard_map/pallas_call | solution.py:319
  21.0 1.8 %collective-permute-done.8.off_ref = bf16[2,96,512]{2,1,0:T(8,128)(2,1)S(1)} collective-permute-done((bf16[2,96,512]{2,1,0:T(8,128)(2,1)S(1)}, bf16[2,96,512]{2,1,0:T(8,128)(2,1)S(1)}, u32[]{:S(2)}, u32[]{:S(2)}) %collective-permute-start.8) | collective-permute-done | bytes 196640 | tf_op jit(solution)/shard_map/ppermute | solution.py:352
  22.8 1.6 %collective-permute-done.9.corner_ref = bf16[2,72,512]{2,1,0:T(8,128)(2,1)S(1)} collective-permute-done((bf16[2,72,512]{2,1,0:T(8,128)(2,1)S(1)}, bf16[2,72,512]{2,1,0:T(8,128)(2,1)S(1)}, u32[]{:S(2)}, u32[]{:S(2)}) %collective-permute-start.9) | collective-permute-done | bytes 147488 | tf_op jit(solution)/shard_map/ppermute | solution.py:352
  24.3 0.8 %shard_map.87 = (bf16[128,128]{1,0:T(8,128)(2,1)S(1)}, bf16[168,512]{1,0:T(8,128)(2,1)S(1)}, bf16[168,512]{1,0:T(8,128)(2,1)S(1)}) custom-call(bf16[128,512]{1,0:T(8,128)(2,1)S(1)} %bitcast.69, bf16[128,512]{1,0:T(8,128)(2,1)S(1)} %bitcast.64, bf16[2,96,512]{2,1,0:T(8,128)(2,1)S(1)} %collective-permute-done.8.off_ref, ...), custom_call_target="tpu_custom_call" | custom-call | flops 1024 | bytes 1024 | tf_op jit(solution)/shard_map/pallas_call | solution.py:319
  25.2 0.1 collective-permute-start.10
  25.3 1.2 %collective-permute-done.10 = bf16[8,16,128]{2,1,0:T(8,128)(2,1)S(1)} collective-permute-done((bf16[8,16,128]{2,1,0:T(8,128)(2,1)S(1)}, bf16[8,16,128]{2,1,0:T(8,128)(2,1)S(1)}, u32[]{:S(2)}, u32[]{:S(2)}) %collective-permute-start.10) | collective-permute-done | bytes 32800 | tf_op jit(solution)/shard_map/ppermute | solution.py:352
  26.5 0.7 %collective-permute-start.11 = (bf16[96,128]{1,0:T(8,128)(2,1)S(1)}, bf16[96,128]{1,0:T(8,128)(2,1)S(1)}, u32[]{:S(2)}, u32[]{:S(2)}) collective-permute-start(bf16[96,128]{1,0:T(8,128)(2,1)S(1)} %pad_maximum_fusion.6), channel_id=1, source_target_pairs={{0,1},{1,2},{2,3},{3,0},{4,7},{5,4},{6,5},{7,6},{8,9},{9,10},{10,1... | collective-permute-start | bytes 73736 | tf_op jit(solution)/shard_map/ppermute | solution.py:352
  27.2 3.3 %collective-permute-start.13 = (bf16[2,168,512]{2,1,0:T(8,128)(2,1)S(1)}, bf16[2,168,512]{2,1,0:T(8,128)(2,1)S(1)}, u32[]{:S(2)}, u32[]{:S(2)}) collective-permute-start(bf16[2,168,512]{2,1,0:T(8,128)(2,1)S(1)} %maximum_maximum_fusion), channel_id=1, source_target_pairs={{0,2},{1,3},{2,0},{3,1},{4,8},{5,9},{6,10},{7,11},{8,4},{9,5},{10,... | collective-permute-start | bytes 1032200 | tf_op jit(solution)/shard_map/ppermute | solution.py:352
  30.5 1.7 %shard_map.88.refs_0_ = bf16[128,256]{1,0:T(8,128)(2,1)S(1)} custom-call(bf16[128,512]{1,0:T(8,128)(2,1)S(1)} %bitcast.70, bf16[128,512]{1,0:T(8,128)(2,1)S(1)} %bitcast.65, bf16[448,512]{1,0:T(8,128)(2,1)S(1)} %get-tuple-element.35.k_near, bf16[448,512]{1,0:T(8,128)(2,1)S(1)} %get-tuple-element.36.v_near, bf16[168,512]{1,0:T(8,128)(2,1)S(1)} %get-tuple-element.40.k_far, ...), custom_call_target="tpu_custom_call" | custom-call | flops 1024 | bytes 1024 | tf_op jit(solution)/shard_map/pallas_call | solution.py:319
  32.2 0.0 collective-permute-done.11.st_lc
  32.2 0.1 collective-permute-start.12
  32.3 1.2 %collective-permute-done.12.st_s2 = bf16[96,128]{1,0:T(8,128)(2,1)S(1)} collective-permute-done((bf16[96,128]{1,0:T(8,128)(2,1)S(1)}, bf16[96,128]{1,0:T(8,128)(2,1)S(1)}, u32[]{:S(2)}, u32[]{:S(2)}) %collective-permute-start.12) | collective-permute-done | bytes 24608 | tf_op jit(solution)/shard_map/ppermute | solution.py:352
  33.5 0.1 collective-permute-start.14
  33.6 2.4 %shard_map.89 = bf16[128,512]{1,0:T(8,128)(2,1)} custom-call(bf16[128,512]{1,0:T(8,128)(2,1)S(1)} %bitcast.71, bf16[128,512]{1,0:T(8,128)(2,1)S(1)} %bitcast.66, bf16[448,512]{1,0:T(8,128)(2,1)S(1)} %get-tuple-element.35.k_near, bf16[448,512]{1,0:T(8,128)(2,1)S(1)} %get-tuple-element.36.v_near, bf16[168,512]{1,0:T(8,128)(2,1)S(1)} %get-tuple-element.40.k_far, ...), custom_call_target="tpu_custom_call" | custom-call | flops 1024 | bytes 1024 | tf_op jit(solution)/shard_map/pallas_call | solution.py:319
  36.0 2.6 %shard_map.90 = (f32[128,512]{1,0:T(8,128)S(1)}, f32[128,512]{1,0:T(8,128)S(1)}) custom-call(bf16[128,512]{1,0:T(8,128)(2,1)S(1)} %bitcast.77, bf16[128,512]{1,0:T(8,128)(2,1)S(1)} %bitcast.74, bf16[128,512]{1,0:T(8,128)(2,1)S(1)} %bitcast.72, bf16[128,512]{1,0:T(8,128)(2,1)S(1)} %bitcast.67, bf16[128,512]{1,0:T(8,128)(2,1)S(1)} %bitcast.81, ...), custom_call_target="tpu_custom_call" | custom-call | flops 1024 | bytes 1024 | tf_op jit(solution)/shard_map/pallas_call | solution.py:319
  38.6 1.9 %collective-permute-done.14.st_off = bf16[168,128]{1,0:T(8,128)(2,1)S(1)} collective-permute-done((bf16[168,128]{1,0:T(8,128)(2,1)S(1)}, bf16[168,128]{1,0:T(8,128)(2,1)S(1)}, u32[]{:S(2)}, u32[]{:S(2)}) %collective-permute-start.14) | collective-permute-done | bytes 43040 | tf_op jit(solution)/shard_map/ppermute | solution.py:352
  40.5 0.0 collective-permute-done.13.off_ref
  40.5 2.0 %shard_map.91 = (bf16[128,512]{1,0:T(8,128)(2,1)}, bf16[128,512]{1,0:T(8,128)(2,1)}) custom-call(bf16[128,512]{1,0:T(8,128)(2,1)S(1)} %bitcast.78, bf16[128,512]{1,0:T(8,128)(2,1)S(1)} %bitcast.75, bf16[2,168,512]{2,1,0:T(8,128)(2,1)S(1)} %collective-permute-done.13.off_ref, bf16[168,128]{1,0:T(8,128)(2,1)S(1)} %collective-permute-done.14.st_off, ...), custom_call_target="tpu_custom_call" | custom-call | flops 1024 | bytes 1024 | tf_op jit(solution)/shard_map/pallas_call | solution.py:319
  (42 shorter events, 0.8 us)
Async XLA Ops:
  0.6 5.9 %collective-permute-start.4 = (bf16[8,16,512]{2,1,0:T(8,128)(2,1)}, bf16[8,16,512]{2,1,0:T(8,128)(2,1)S(1)}, u32[]{:S(2)}, u32[]{:S(2)}) collective-permute-start(bf16[8,16,512]{2,1,0:T(8,128)(2,1)} %param.6), channel_id=1, source_target_pairs={{0,4},{1,5},{2,6},{3,7},{4,0},{5,1},{6,2},{7,3},{8,12},{9,13},{10,... | collective-permute-start | bytes 393224 | tf_op jit(solution)/shard_map/ppermute | solution.py:352
  1.1 2.1 %collective-permute-start = (bf16[8,16,512]{2,1,0:T(8,128)(2,1)}, bf16[8,16,512]{2,1,0:T(8,128)(2,1)S(1)}, u32[]{:S(2)}, u32[]{:S(2)}) collective-permute-start(bf16[8,16,512]{2,1,0:T(8,128)(2,1)} %param.7), channel_id=1, source_target_pairs={{0,4},{1,5},{2,6},{3,7},{4,0},{5,1},{6,2},{7,3},{8,12},{9,13},{10,... | collective-permute-start | bytes 393224 | tf_op jit(solution)/shard_map/ppermute | solution.py:352
  1.2 2.0 %collective-permute-start.1 = (bf16[8,16,512]{2,1,0:T(8,128)(2,1)}, bf16[8,16,512]{2,1,0:T(8,128)(2,1)S(1)}, u32[]{:S(2)}, u32[]{:S(2)}) collective-permute-start(bf16[8,16,512]{2,1,0:T(8,128)(2,1)} %param.8), channel_id=1, source_target_pairs={{0,4},{1,5},{2,6},{3,7},{4,0},{5,1},{6,2},{7,3},{8,12},{9,13},{10,... | collective-permute-start | bytes 393224 | tf_op jit(solution)/shard_map/ppermute | solution.py:352
  1.7 4.8 %collective-permute-start.5 = (bf16[8,16,512]{2,1,0:T(8,128)(2,1)}, bf16[8,16,512]{2,1,0:T(8,128)(2,1)S(1)}, u32[]{:S(2)}, u32[]{:S(2)}) collective-permute-start(bf16[8,16,512]{2,1,0:T(8,128)(2,1)} %param.9), channel_id=1, source_target_pairs={{0,4},{1,5},{2,6},{3,7},{4,0},{5,1},{6,2},{7,3},{8,12},{9,13},{10,... | collective-permute-start | bytes 393224 | tf_op jit(solution)/shard_map/ppermute | solution.py:352
  3.4 10.8 %collective-permute-start.2 = (bf16[2,96,512]{2,1,0:T(8,128)(2,1)S(1)}, bf16[2,96,512]{2,1,0:T(8,128)(2,1)S(1)}, u32[]{:S(2)}, u32[]{:S(2)}) collective-permute-start(bf16[2,96,512]{2,1,0:T(8,128)(2,1)S(1)} %pad_maximum_fusion.1), channel_id=1, source_target_pairs={{0,1},{1,2},{2,3},{3,0},{4,7},{5,4},{6,5},{7,6},{8,9},{9,10},{10,1... | collective-permute-start | bytes 589832 | tf_op jit(solution)/shard_map/ppermute | solution.py:352
  6.8 11.2 %collective-permute-start.6 = (bf16[2,96,512]{2,1,0:T(8,128)(2,1)S(1)}, bf16[2,96,512]{2,1,0:T(8,128)(2,1)S(1)}, u32[]{:S(2)}, u32[]{:S(2)}) collective-permute-start(bf16[2,96,512]{2,1,0:T(8,128)(2,1)S(1)} %pad_maximum_fusion.2), channel_id=1, source_target_pairs={{0,1},{1,2},{2,3},{3,0},{4,7},{5,4},{6,5},{7,6},{8,9},{9,10},{10,1... | collective-permute-start | bytes 589832 | tf_op jit(solution)/shard_map/ppermute | solution.py:352
  8.5 14.3 %collective-permute-start.8 = (bf16[2,96,512]{2,1,0:T(8,128)(2,1)S(1)}, bf16[2,96,512]{2,1,0:T(8,128)(2,1)S(1)}, u32[]{:S(2)}, u32[]{:S(2)}) collective-permute-start(bf16[2,96,512]{2,1,0:T(8,128)(2,1)S(1)} %pad_maximum_fusion.3), channel_id=1, source_target_pairs={{0,2},{1,3},{2,0},{3,1},{4,8},{5,9},{6,10},{7,11},{8,4},{9,5},{10,... | collective-permute-start | bytes 589832 | tf_op jit(solution)/shard_map/ppermute | solution.py:352
  14.1 1.4 %collective-permute-start.3 = (bf16[2,96,512]{2,1,0:T(8,128)(2,1)S(1)}, bf16[2,96,512]{2,1,0:T(8,128)(2,1)S(1)}, u32[]{:S(2)}, u32[]{:S(2)}) collective-permute-start(bf16[2,96,512]{2,1,0:T(8,128)(2,1)S(1)} %collective-permute-done.2.lc_ref), channel_id=1, source_target_pairs={{0,4},{1,5},{2,6},{3,7},{4,0},{5,1},{6,2},{7,3},{8,12},{9,13},{10,... | collective-permute-start | bytes 589832 | tf_op jit(solution)/shard_map/ppermute | solution.py:352
  15.7 2.5 %copy-start = (s32[8,616]{1,0:T(8,128)S(1)}, s32[8,616]{1,0:T(8,128)}, u32[]{:S(2)}) copy-start(s32[8,616]{1,0:T(8,128)} %constant.17.clone.table_hbm) | copy-start | bytes 59140
  15.7 2.5 %copy-start.1 = (s32[2,64]{1,0:T(2,128)S(1)}, s32[2,64]{1,0:T(2,128)}, u32[]{:S(2)}) copy-start(s32[2,64]{1,0:T(2,128)} %reach_hbm) | copy-start | bytes 1540
  15.7 8.6 %collective-permute-start.9 = (bf16[2,72,512]{2,1,0:T(8,128)(2,1)S(1)}, bf16[2,72,512]{2,1,0:T(8,128)(2,1)S(1)}, u32[]{:S(2)}, u32[]{:S(2)}) collective-permute-start(bf16[2,72,512]{2,1,0:T(8,128)(2,1)S(1)} %pad_maximum_fusion.4), channel_id=1, source_target_pairs={{0,2},{1,3},{2,0},{3,1},{4,8},{5,9},{6,10},{7,11},{8,4},{9,5},{10,... | collective-permute-start | bytes 442376 | tf_op jit(solution)/shard_map/ppermute | solution.py:352
  18.0 1.4 %collective-permute-start.7 = (bf16[2,96,512]{2,1,0:T(8,128)(2,1)S(1)}, bf16[2,96,512]{2,1,0:T(8,128)(2,1)S(1)}, u32[]{:S(2)}, u32[]{:S(2)}) collective-permute-start(bf16[2,96,512]{2,1,0:T(8,128)(2,1)S(1)} %collective-permute-done.6.lc_ref), channel_id=1, source_target_pairs={{0,4},{1,5},{2,6},{3,7},{4,0},{5,1},{6,2},{7,3},{8,12},{9,13},{10,... | collective-permute-start | bytes 589832 | tf_op jit(solution)/shard_map/ppermute | solution.py:352
  25.2 1.3 %collective-permute-start.10 = (bf16[8,16,128]{2,1,0:T(8,128)(2,1)S(1)}, bf16[8,16,128]{2,1,0:T(8,128)(2,1)S(1)}, u32[]{:S(2)}, u32[]{:S(2)}) collective-permute-start(bf16[8,16,128]{2,1,0:T(8,128)(2,1)S(1)} %bitcast.79), channel_id=1, source_target_pairs={{0,4},{1,5},{2,6},{3,7},{4,0},{5,1},{6,2},{7,3},{8,12},{9,13},{10,... | collective-permute-start | bytes 98312 | tf_op jit(solution)/shard_map/ppermute | solution.py:352
  26.5 5.7 %collective-permute-start.11 = (bf16[96,128]{1,0:T(8,128)(2,1)S(1)}, bf16[96,128]{1,0:T(8,128)(2,1)S(1)}, u32[]{:S(2)}, u32[]{:S(2)}) collective-permute-start(bf16[96,128]{1,0:T(8,128)(2,1)S(1)} %pad_maximum_fusion.6), channel_id=1, source_target_pairs={{0,1},{1,2},{2,3},{3,0},{4,7},{5,4},{6,5},{7,6},{8,9},{9,10},{10,1... | collective-permute-start | bytes 73736 | tf_op jit(solution)/shard_map/ppermute | solution.py:352
  27.2 13.2 %collective-permute-start.13 = (bf16[2,168,512]{2,1,0:T(8,128)(2,1)S(1)}, bf16[2,168,512]{2,1,0:T(8,128)(2,1)S(1)}, u32[]{:S(2)}, u32[]{:S(2)}) collective-permute-start(bf16[2,168,512]{2,1,0:T(8,128)(2,1)S(1)} %maximum_maximum_fusion), channel_id=1, source_target_pairs={{0,2},{1,3},{2,0},{3,1},{4,8},{5,9},{6,10},{7,11},{8,4},{9,5},{10,... | collective-permute-start | bytes 1032200 | tf_op jit(solution)/shard_map/ppermute | solution.py:352
  32.2 1.3 %collective-permute-start.12 = (bf16[96,128]{1,0:T(8,128)(2,1)S(1)}, bf16[96,128]{1,0:T(8,128)(2,1)S(1)}, u32[]{:S(2)}, u32[]{:S(2)}) collective-permute-start(bf16[96,128]{1,0:T(8,128)(2,1)S(1)} %collective-permute-done.11.st_lc), channel_id=1, source_target_pairs={{0,4},{1,5},{2,6},{3,7},{4,0},{5,1},{6,2},{7,3},{8,12},{9,13},{10,... | collective-permute-start | bytes 73736 | tf_op jit(solution)/shard_map/ppermute | solution.py:352
  33.5 7.0 %collective-permute-start.14 = (bf16[168,128]{1,0:T(8,128)(2,1)S(1)}, bf16[168,128]{1,0:T(8,128)(2,1)S(1)}, u32[]{:S(2)}, u32[]{:S(2)}) collective-permute-start(bf16[168,128]{1,0:T(8,128)(2,1)S(1)} %pad_maximum_fusion.5), channel_id=1, source_target_pairs={{0,2},{1,3},{2,0},{3,1},{4,8},{5,9},{6,10},{7,11},{8,4},{9,5},{10,... | collective-permute-start | bytes 129032 | tf_op jit(solution)/shard_map/ppermute | solution.py:352

commit v7 on v6

--- a/solution.py
+++ b/solution.py
@@ -212,13 +212,17 @@
     st_ref[...] = jnp.concatenate(terms, axis=0).T.astype(jnp.bfloat16)
 
 
+def first_lanes(width):
+    return width // LANES * 3 // 4 * LANES
+
+
 def query_kernel(
     q_ref, g_ref, k_near, v_near, k_far, v_far, bias_near, bias_far, st_ref, *refs
 ):
     dq_ref = refs[-1]
-    half = q_ref.shape[1] // 2
+    split = first_lanes(q_ref.shape[1])
     if len(refs) > 1:
-        dq_ref[:, 0:half] = refs[0][...]
+        dq_ref[:, 0:split] = refs[0][...]
     heads = q_ref.shape[1] // HEAD_DIM
     per = LANES // HEAD_DIM
     row = lax.broadcasted_iota(jnp.int32, (LANES, LANES), 0)
@@ -233,7 +237,7 @@
         return jnp.concatenate([x] * -(-count // LANES), axis=1)[:, :count]
 
     for at, first in groups(q_ref.shape[1]):
-        if (at.start >= half) != (len(refs) > 1):
+        if (at.start >= split) != (len(refs) > 1):
             continue
         qs, gs = spread(q_ref[:, at]), spread(g_ref[:, at])
         logs = [stat_of(first + j) for j in range(per)]
@@ -332,6 +336,7 @@
 
     f32 = jnp.float32
     heads = width // HEAD_DIM
+
     def strip_of(mine, other):
         side = [jnp.where(even, x[:, cols - RADIUS :], x[:, :RADIUS]) for x in (mine, other)]
         return jnp.concatenate([x.reshape(rows * RADIUS, -1) for x in side], axis=0)
@@ -375,7 +380,7 @@
     kv_2 = send(kv_1, pair)
     kv_last = corners(kv_1, kv_2)
     kv_corner = send(kv_last, across)
-    qg_1, place, pole_reach, _ = lax.optimization_barrier((qg_1, place, pole_reach, kv_last))
+    place, pole_reach, _ = lax.optimization_barrier((place, pole_reach, kv_1))
     table = np.concatenate(
         [layout(rows, cols, odd, pole) for odd in (False, True) for pole in (False, True)]
     )
@@ -396,10 +401,6 @@
         space=pltpu.HBM,
     )
 
-    qg_2 = send(qg_1, pair)
-    qg_beyond = jnp.concatenate([edges(later[2:]), corners(qg_1, qg_2)], axis=1)
-    bias_t, qg_beyond = lax.optimization_barrier((bias_t, qg_beyond))
-
     k, v, q, g = (flat(x) for x in mine)
     stat = array(heads, n_own, dtype=f32)
     k_near, v_near, *near_stats = call(
@@ -407,6 +408,10 @@
         (array(near, width), array(near, width), stat, stat, stat),
         (q, g, k, v, flat(key_o), flat(value_o), kv_1, kv_2, bias_t),
     )
+    qg_1, _ = lax.optimization_barrier((qg_1, near_stats[0]))
+    qg_2 = send(qg_1, pair)
+    qg_beyond = jnp.concatenate([edges(later[2:]), corners(qg_1, qg_2)], axis=1)
+    near_stats[0], qg_2 = lax.optimization_barrier((near_stats[0], qg_2))
     stats, k_far, v_far = call(
         far_stats_kernel,
         (array(n_own, LANES), array(far, width), array(far, width)),
@@ -419,7 +424,7 @@
     st_1 = send(st_strip, around)
     qg_off = send(qg_beyond, across)
     query_side = (q, g, k_near, v_near, k_far, v_far, bias_near, bias_far)
-    d_query = call(query_kernel, array(n_own, width // 2), (*query_side, stats_q))
+    d_query = call(query_kernel, array(n_own, first_lanes(width)), (*query_side, stats_q))
     st_1, d_query = lax.optimization_barrier((st_1, d_query))
     st_2 = send(st_1, pair)
     _, stats_q = lax.optimization_barrier((st_2, stats))

time: 42.6 us -> 41.8 us (0.981)
  waiting for transfers between devices: 16 us -> 11.4 us
  starting transfers between devices: 11.3 us -> 15.1 us
    ppermute x15, waiting for transfers between devices: 16 us -> 11.4 us  [send(): return lax.ppermute(block, axes, route)]
    ppermute x15, starting transfers between devices: 11.3 us -> 15.1 us  [send(): return lax.ppermute(block, axes, route)]
  transfers between devices with their start and end apart: 15 -> 15, of which waited for: 9 -> 8; matrix products, arithmetic and copies ran while one was open for 5% -> 5% of each run, Pallas kernels for 21% -> 22%
where the time goes in v7:
time: 41.8 us; the launch traced here: 41.7 us
  starting transfers between devices  15.1 us (36%)
  Pallas kernels  11.9 us (28%)
  waiting for transfers between devices  11.4 us (27%)
  other arithmetic  1.82 us (4%)
  between operations  1.06 us (3%)
    ppermute x15, starting transfers between devices, send(): return lax.ppermute(block, axes, route)  15.1 us
    pallas_call x7, Pallas kernels, call(): pl.pallas_call(body, out_shape=outs, in_specs=[smem] * scalars + [pl.Bloc...  11.9 us
    ppermute x15, waiting for transfers between devices, send(): return lax.ppermute(block, axes, route)  11.4 us
    another operation x1, other arithmetic, shards(): mine = lax.optimization_barrier(jnp.stack([key, value, query, grad]))  1.16 us
  transfers between devices with their start and end apart: 15, of which 8 were waited for; matrix products, arithmetic and copies ran while one was open for 5% of the time, Pallas kernels for 22%

profile of v7, /device:TPU:0, one launch (start us, length us, event | category | flops | bytes accessed | tf_op | source)
XLA Modules:
  0.0 41.7 jit_solution(10268795752268604576)
XLA Ops:
  0.6 0.5 %collective-permute-start = (bf16[8,16,512]{2,1,0:T(8,128)(2,1)}, bf16[8,16,512]{2,1,0:T(8,128)(2,1)S(1)}, u32[]{:S(2)}, u32[]{:S(2)}) collective-permute-start(bf16[8,16,512]{2,1,0:T(8,128)(2,1)} %param.7), channel_id=1, source_target_pairs={{0,4},{1,5},{2,6},{3,7},{4,0},{5,1},{6,2},{7,3},{8,12},{9,13},{10,... | collective-permute-start | bytes 393224 | tf_op jit(solution)/shard_map/ppermute | solution.py:357
  1.1 0.1 collective-permute-start.1
  1.2 0.4 %collective-permute-start.7 = (bf16[8,16,512]{2,1,0:T(8,128)(2,1)}, bf16[8,16,512]{2,1,0:T(8,128)(2,1)S(1)}, u32[]{:S(2)}, u32[]{:S(2)}) collective-permute-start(bf16[8,16,512]{2,1,0:T(8,128)(2,1)} %param.9), channel_id=1, source_target_pairs={{0,4},{1,5},{2,6},{3,7},{4,0},{5,1},{6,2},{7,3},{8,12},{9,13},{10,... | collective-permute-start | bytes 393224 | tf_op jit(solution)/shard_map/ppermute | solution.py:357
  1.7 0.1 collective-permute-start.6
  1.7 1.2 %pad_maximum_fusion = bf16[4,8,16,512]{3,2,1,0:T(8,128)(2,1)S(1)} fusion(bf16[1,8,16,512]{3,2,1,0:T(8,128)(2,1)} %bitcast.93, bf16[1,8,16,512]{3,2,1,0:T(8,128)(2,1)} %bitcast.94, bf16[1,8,16,512]{3,2,1,0:T(8,128)(2,1)} %bitcast.92, bf16[1,8,16,512]{3,2,1,0:T(8,128)(2,1)} %bitcast.91), kind=kLoop, calls=%fused_computation | loop fusion | flops 786432 | bytes 1048576 | tf_op jit(solution)/shard_map/stack | solution.py:373
  2.9 0.1 slice_bitcast_fusion.3
  3.1 0.1 pad_add_fusion.sc_ref
  3.2 0.0 collective-permute-done
  3.2 0.0 collective-permute-done.1
  3.4 3.1 %collective-permute-start.2 = (bf16[2,96,512]{2,1,0:T(8,128)(2,1)S(1)}, bf16[2,96,512]{2,1,0:T(8,128)(2,1)S(1)}, u32[]{:S(2)}, u32[]{:S(2)}) collective-permute-start(bf16[2,96,512]{2,1,0:T(8,128)(2,1)S(1)} %pad_maximum_fusion.1), channel_id=1, source_target_pairs={{0,1},{1,2},{2,3},{3,0},{4,7},{5,4},{6,5},{7,6},{8,9},{9,10},{10,1... | collective-permute-start | bytes 589832 | tf_op jit(solution)/shard_map/ppermute | solution.py:357
  6.5 2.7 %collective-permute-start.4 = (bf16[2,96,512]{2,1,0:T(8,128)(2,1)S(1)}, bf16[2,96,512]{2,1,0:T(8,128)(2,1)S(1)}, u32[]{:S(2)}, u32[]{:S(2)}) collective-permute-start(bf16[2,96,512]{2,1,0:T(8,128)(2,1)S(1)} %pad_maximum_fusion.2), channel_id=1, source_target_pairs={{0,2},{1,3},{2,0},{3,1},{4,8},{5,9},{6,10},{7,11},{8,4},{9,5},{10,... | collective-permute-start | bytes 589832 | tf_op jit(solution)/shard_map/ppermute | solution.py:357
  9.2 0.0 collective-permute-done.7
  9.2 0.0 collective-permute-done.6
  9.5 0.0 copy-start
  9.5 0.0 copy-start.1
  9.5 0.1 collective-permute-start.8
  9.6 4.5 %collective-permute-done.2.lc_ref = bf16[2,96,512]{2,1,0:T(8,128)(2,1)S(1)} collective-permute-done((bf16[2,96,512]{2,1,0:T(8,128)(2,1)S(1)}, bf16[2,96,512]{2,1,0:T(8,128)(2,1)S(1)}, u32[]{:S(2)}, u32[]{:S(2)}) %collective-permute-start.2) | collective-permute-done | bytes 196640 | tf_op jit(solution)/shard_map/ppermute | solution.py:357
  14.1 0.0 copy-done
  14.1 0.0 copy-done.1
  14.1 1.0 %shard_map.85 = (f32[128,448]{1,0:T(8,128)S(1)}, f32[128,168]{1,0:T(8,128)S(1)}, f32[616,128]{1,0:T(8,128)S(1)}) custom-call(s32[2]{0:T(128)S(1)} %pad_add_fusion.sc_ref, s32[2,64]{1,0:T(2,128)S(1)} %copy-done.1, s32[8,616]{1,0:T(8,128)S(1)} %copy-done), custom_call_target="tpu_custom_call" | custom-call | flops 1024 | bytes 1024 | tf_op jit(solution)/shard_map/pallas_call | solution.py:323
  15.1 0.1 collective-permute-start.3
  15.3 1.4 %collective-permute-done.3.s2_ref = bf16[2,96,512]{2,1,0:T(8,128)(2,1)S(1)} collective-permute-done((bf16[2,96,512]{2,1,0:T(8,128)(2,1)S(1)}, bf16[2,96,512]{2,1,0:T(8,128)(2,1)S(1)}, u32[]{:S(2)}, u32[]{:S(2)}) %collective-permute-start.3) | collective-permute-done | bytes 196640 | tf_op jit(solution)/shard_map/ppermute | solution.py:357
  16.7 4.3 %collective-permute-start.5 = (bf16[2,72,512]{2,1,0:T(8,128)(2,1)S(1)}, bf16[2,72,512]{2,1,0:T(8,128)(2,1)S(1)}, u32[]{:S(2)}, u32[]{:S(2)}) collective-permute-start(bf16[2,72,512]{2,1,0:T(8,128)(2,1)S(1)} %pad_maximum_fusion.4), channel_id=1, source_target_pairs={{0,2},{1,3},{2,0},{3,1},{4,8},{5,9},{6,10},{7,11},{8,4},{9,5},{10,... | collective-permute-start | bytes 442376 | tf_op jit(solution)/shard_map/ppermute | solution.py:357
  21.0 1.4 %shard_map.86 = (bf16[448,512]{1,0:T(8,128)(2,1)S(1)}, bf16[448,512]{1,0:T(8,128)(2,1)S(1)}, f32[16,128]{1,0:T(8,128)S(1)}, f32[16,128]{1,0:T(8,128)S(1)}, f32[16,128]{1,0:T(8,128)S(1)}) custom-call(bf16[128,512]{1,0:T(8,128)(2,1)S(1)} %bitcast.68, bf16[128,512]{1,0:T(8,128)(2,1)S(1)} %bitcast.63, bf16[128,512]{1,0:T(8,128)(2,1)S(1)} %bitcast.76, ...), custom_call_target="tpu_custom_call" | custom-call | flops 1024 | bytes 1024 | tf_op jit(solution)/shard_map/pallas_call | solution.py:323
  22.4 0.0 collective-permute-done.8.lc_ref
  22.4 0.1 collective-permute-start.9
  22.6 1.4 %collective-permute-done.9.s2_ref = bf16[2,96,512]{2,1,0:T(8,128)(2,1)S(1)} collective-permute-done((bf16[2,96,512]{2,1,0:T(8,128)(2,1)S(1)}, bf16[2,96,512]{2,1,0:T(8,128)(2,1)S(1)}, u32[]{:S(2)}, u32[]{:S(2)}) %collective-permute-start.9) | collective-permute-done | bytes 196640 | tf_op jit(solution)/shard_map/ppermute | solution.py:357
  24.0 0.0 collective-permute-done.4.off_ref
  24.0 0.4 collective-permute-done.5.corner_ref
  24.3 0.8 %shard_map.87 = (bf16[128,128]{1,0:T(8,128)(2,1)S(1)}, bf16[168,512]{1,0:T(8,128)(2,1)S(1)}, bf16[168,512]{1,0:T(8,128)(2,1)S(1)}) custom-call(bf16[128,512]{1,0:T(8,128)(2,1)S(1)} %bitcast.69, bf16[128,512]{1,0:T(8,128)(2,1)S(1)} %bitcast.64, bf16[2,96,512]{2,1,0:T(8,128)(2,1)S(1)} %collective-permute-done.4.off_ref, ...), custom_call_target="tpu_custom_call" | custom-call | flops 1024 | bytes 1024 | tf_op jit(solution)/shard_map/pallas_call | solution.py:323
  25.2 0.1 collective-permute-start.10
  25.4 1.1 %collective-permute-done.10 = bf16[8,16,128]{2,1,0:T(8,128)(2,1)S(1)} collective-permute-done((bf16[8,16,128]{2,1,0:T(8,128)(2,1)S(1)}, bf16[8,16,128]{2,1,0:T(8,128)(2,1)S(1)}, u32[]{:S(2)}, u32[]{:S(2)}) %collective-permute-start.10) | collective-permute-done | bytes 32800 | tf_op jit(solution)/shard_map/ppermute | solution.py:357
  26.5 0.1 collective-permute-start.11
  26.6 2.8 %collective-permute-start.13 = (bf16[2,168,512]{2,1,0:T(8,128)(2,1)S(1)}, bf16[2,168,512]{2,1,0:T(8,128)(2,1)S(1)}, u32[]{:S(2)}, u32[]{:S(2)}) collective-permute-start(bf16[2,168,512]{2,1,0:T(8,128)(2,1)S(1)} %maximum_maximum_fusion), channel_id=1, source_target_pairs={{0,2},{1,3},{2,0},{3,1},{4,8},{5,9},{6,10},{7,11},{8,4},{9,5},{10,... | collective-permute-start | bytes 1032200 | tf_op jit(solution)/shard_map/ppermute | solution.py:357
  29.4 2.4 %shard_map.88.refs_0_ = bf16[128,384]{1,0:T(8,128)(2,1)S(1)} custom-call(bf16[128,512]{1,0:T(8,128)(2,1)S(1)} %bitcast.70, bf16[128,512]{1,0:T(8,128)(2,1)S(1)} %bitcast.65, bf16[448,512]{1,0:T(8,128)(2,1)S(1)} %get-tuple-element.32.k_near, bf16[448,512]{1,0:T(8,128)(2,1)S(1)} %get-tuple-element.33.v_near, bf16[168,512]{1,0:T(8,128)(2,1)S(1)} %get-tuple-element.40.k_far, ...), custom_call_target="tpu_custom_call" | custom-call | flops 1024 | bytes 1024 | tf_op jit(solution)/shard_map/pallas_call | solution.py:323
  31.8 0.4 %collective-permute-done.11.st_lc = bf16[96,128]{1,0:T(8,128)(2,1)S(1)} collective-permute-done((bf16[96,128]{1,0:T(8,128)(2,1)S(1)}, bf16[96,128]{1,0:T(8,128)(2,1)S(1)}, u32[]{:S(2)}, u32[]{:S(2)}) %collective-permute-start.11) | collective-permute-done | bytes 24608 | tf_op jit(solution)/shard_map/ppermute | solution.py:357
  32.3 0.0 collective-permute-start.12
  32.3 1.2 %collective-permute-done.12.st_s2 = bf16[96,128]{1,0:T(8,128)(2,1)S(1)} collective-permute-done((bf16[96,128]{1,0:T(8,128)(2,1)S(1)}, bf16[96,128]{1,0:T(8,128)(2,1)S(1)}, u32[]{:S(2)}, u32[]{:S(2)}) %collective-permute-start.12) | collective-permute-done | bytes 24608 | tf_op jit(solution)/shard_map/ppermute | solution.py:357
  33.5 0.9 %collective-permute-start.14 = (bf16[168,128]{1,0:T(8,128)(2,1)S(1)}, bf16[168,128]{1,0:T(8,128)(2,1)S(1)}, u32[]{:S(2)}, u32[]{:S(2)}) collective-permute-start(bf16[168,128]{1,0:T(8,128)(2,1)S(1)} %pad_maximum_fusion.5), channel_id=1, source_target_pairs={{0,2},{1,3},{2,0},{3,1},{4,8},{5,9},{6,10},{7,11},{8,4},{9,5},{10,... | collective-permute-start | bytes 129032 | tf_op jit(solution)/shard_map/ppermute | solution.py:357
  34.4 1.6 %shard_map.89 = bf16[128,512]{1,0:T(8,128)(2,1)} custom-call(bf16[128,512]{1,0:T(8,128)(2,1)S(1)} %bitcast.71, bf16[128,512]{1,0:T(8,128)(2,1)S(1)} %bitcast.66, bf16[448,512]{1,0:T(8,128)(2,1)S(1)} %get-tuple-element.32.k_near, bf16[448,512]{1,0:T(8,128)(2,1)S(1)} %get-tuple-element.33.v_near, bf16[168,512]{1,0:T(8,128)(2,1)S(1)} %get-tuple-element.40.k_far, ...), custom_call_target="tpu_custom_call" | custom-call | flops 1024 | bytes 1024 | tf_op jit(solution)/shard_map/pallas_call | solution.py:323
  36.0 2.6 %shard_map.90 = (f32[128,512]{1,0:T(8,128)S(1)}, f32[128,512]{1,0:T(8,128)S(1)}) custom-call(bf16[128,512]{1,0:T(8,128)(2,1)S(1)} %bitcast.77, bf16[128,512]{1,0:T(8,128)(2,1)S(1)} %bitcast.74, bf16[128,512]{1,0:T(8,128)(2,1)S(1)} %bitcast.72, bf16[128,512]{1,0:T(8,128)(2,1)S(1)} %bitcast.67, bf16[128,512]{1,0:T(8,128)(2,1)S(1)} %bitcast.82, ...), custom_call_target="tpu_custom_call" | custom-call | flops 1024 | bytes 1024 | tf_op jit(solution)/shard_map/pallas_call | solution.py:323
  38.7 1.0 %collective-permute-done.14.st_off = bf16[168,128]{1,0:T(8,128)(2,1)S(1)} collective-permute-done((bf16[168,128]{1,0:T(8,128)(2,1)S(1)}, bf16[168,128]{1,0:T(8,128)(2,1)S(1)}, u32[]{:S(2)}, u32[]{:S(2)}) %collective-permute-start.14) | collective-permute-done | bytes 43040 | tf_op jit(solution)/shard_map/ppermute | solution.py:357
  39.7 0.0 collective-permute-done.13.off_ref
  39.7 2.0 %shard_map.91 = (bf16[128,512]{1,0:T(8,128)(2,1)}, bf16[128,512]{1,0:T(8,128)(2,1)}) custom-call(bf16[128,512]{1,0:T(8,128)(2,1)S(1)} %bitcast.78, bf16[128,512]{1,0:T(8,128)(2,1)S(1)} %bitcast.75, bf16[2,168,512]{2,1,0:T(8,128)(2,1)S(1)} %collective-permute-done.13.off_ref, bf16[168,128]{1,0:T(8,128)(2,1)S(1)} %collective-permute-done.14.st_off, ...), custom_call_target="tpu_custom_call" | custom-call | flops 1024 | bytes 1024 | tf_op jit(solution)/shard_map/pallas_call | solution.py:323
  (42 shorter events, 0.8 us)
Async XLA Ops:
  0.6 2.6 %collective-permute-start = (bf16[8,16,512]{2,1,0:T(8,128)(2,1)}, bf16[8,16,512]{2,1,0:T(8,128)(2,1)S(1)}, u32[]{:S(2)}, u32[]{:S(2)}) collective-permute-start(bf16[8,16,512]{2,1,0:T(8,128)(2,1)} %param.7), channel_id=1, source_target_pairs={{0,4},{1,5},{2,6},{3,7},{4,0},{5,1},{6,2},{7,3},{8,12},{9,13},{10,... | collective-permute-start | bytes 393224 | tf_op jit(solution)/shard_map/ppermute | solution.py:357
  1.1 2.1 %collective-permute-start.1 = (bf16[8,16,512]{2,1,0:T(8,128)(2,1)}, bf16[8,16,512]{2,1,0:T(8,128)(2,1)S(1)}, u32[]{:S(2)}, u32[]{:S(2)}) collective-permute-start(bf16[8,16,512]{2,1,0:T(8,128)(2,1)} %param.8), channel_id=1, source_target_pairs={{0,4},{1,5},{2,6},{3,7},{4,0},{5,1},{6,2},{7,3},{8,12},{9,13},{10,... | collective-permute-start | bytes 393224 | tf_op jit(solution)/shard_map/ppermute | solution.py:357
  1.2 8.0 %collective-permute-start.7 = (bf16[8,16,512]{2,1,0:T(8,128)(2,1)}, bf16[8,16,512]{2,1,0:T(8,128)(2,1)S(1)}, u32[]{:S(2)}, u32[]{:S(2)}) collective-permute-start(bf16[8,16,512]{2,1,0:T(8,128)(2,1)} %param.9), channel_id=1, source_target_pairs={{0,4},{1,5},{2,6},{3,7},{4,0},{5,1},{6,2},{7,3},{8,12},{9,13},{10,... | collective-permute-start | bytes 393224 | tf_op jit(solution)/shard_map/ppermute | solution.py:357
  1.7 7.5 %collective-permute-start.6 = (bf16[8,16,512]{2,1,0:T(8,128)(2,1)}, bf16[8,16,512]{2,1,0:T(8,128)(2,1)S(1)}, u32[]{:S(2)}, u32[]{:S(2)}) collective-permute-start(bf16[8,16,512]{2,1,0:T(8,128)(2,1)} %param.6), channel_id=1, source_target_pairs={{0,4},{1,5},{2,6},{3,7},{4,0},{5,1},{6,2},{7,3},{8,12},{9,13},{10,... | collective-permute-start | bytes 393224 | tf_op jit(solution)/shard_map/ppermute | solution.py:357
  3.4 10.8 %collective-permute-start.2 = (bf16[2,96,512]{2,1,0:T(8,128)(2,1)S(1)}, bf16[2,96,512]{2,1,0:T(8,128)(2,1)S(1)}, u32[]{:S(2)}, u32[]{:S(2)}) collective-permute-start(bf16[2,96,512]{2,1,0:T(8,128)(2,1)S(1)} %pad_maximum_fusion.1), channel_id=1, source_target_pairs={{0,1},{1,2},{2,3},{3,0},{4,7},{5,4},{6,5},{7,6},{8,9},{9,10},{10,1... | collective-permute-start | bytes 589832 | tf_op jit(solution)/shard_map/ppermute | solution.py:357
  6.5 17.5 %collective-permute-start.4 = (bf16[2,96,512]{2,1,0:T(8,128)(2,1)S(1)}, bf16[2,96,512]{2,1,0:T(8,128)(2,1)S(1)}, u32[]{:S(2)}, u32[]{:S(2)}) collective-permute-start(bf16[2,96,512]{2,1,0:T(8,128)(2,1)S(1)} %pad_maximum_fusion.2), channel_id=1, source_target_pairs={{0,2},{1,3},{2,0},{3,1},{4,8},{5,9},{6,10},{7,11},{8,4},{9,5},{10,... | collective-permute-start | bytes 589832 | tf_op jit(solution)/shard_map/ppermute | solution.py:357
  9.5 4.7 %copy-start = (s32[8,616]{1,0:T(8,128)S(1)}, s32[8,616]{1,0:T(8,128)}, u32[]{:S(2)}) copy-start(s32[8,616]{1,0:T(8,128)} %constant.17.clone.table_hbm) | copy-start | bytes 59140
  9.5 4.7 %copy-start.1 = (s32[2,64]{1,0:T(2,128)S(1)}, s32[2,64]{1,0:T(2,128)}, u32[]{:S(2)}) copy-start(s32[2,64]{1,0:T(2,128)} %reach_hbm) | copy-start | bytes 1540
  9.5 12.9 %collective-permute-start.8 = (bf16[2,96,512]{2,1,0:T(8,128)(2,1)S(1)}, bf16[2,96,512]{2,1,0:T(8,128)(2,1)S(1)}, u32[]{:S(2)}, u32[]{:S(2)}) collective-permute-start(bf16[2,96,512]{2,1,0:T(8,128)(2,1)S(1)} %pad_maximum_fusion.3), channel_id=1, source_target_pairs={{0,1},{1,2},{2,3},{3,0},{4,7},{5,4},{6,5},{7,6},{8,9},{9,10},{10,1... | collective-permute-start | bytes 589832 | tf_op jit(solution)/shard_map/ppermute | solution.py:357
  15.1 1.5 %collective-permute-start.3 = (bf16[2,96,512]{2,1,0:T(8,128)(2,1)S(1)}, bf16[2,96,512]{2,1,0:T(8,128)(2,1)S(1)}, u32[]{:S(2)}, u32[]{:S(2)}) collective-permute-start(bf16[2,96,512]{2,1,0:T(8,128)(2,1)S(1)} %collective-permute-done.2.lc_ref), channel_id=1, source_target_pairs={{0,4},{1,5},{2,6},{3,7},{4,0},{5,1},{6,2},{7,3},{8,12},{9,13},{10,... | collective-permute-start | bytes 589832 | tf_op jit(solution)/shard_map/ppermute | solution.py:357
  16.7 7.6 %collective-permute-start.5 = (bf16[2,72,512]{2,1,0:T(8,128)(2,1)S(1)}, bf16[2,72,512]{2,1,0:T(8,128)(2,1)S(1)}, u32[]{:S(2)}, u32[]{:S(2)}) collective-permute-start(bf16[2,72,512]{2,1,0:T(8,128)(2,1)S(1)} %pad_maximum_fusion.4), channel_id=1, source_target_pairs={{0,2},{1,3},{2,0},{3,1},{4,8},{5,9},{6,10},{7,11},{8,4},{9,5},{10,... | collective-permute-start | bytes 442376 | tf_op jit(solution)/shard_map/ppermute | solution.py:357
  22.4 1.5 %collective-permute-start.9 = (bf16[2,96,512]{2,1,0:T(8,128)(2,1)S(1)}, bf16[2,96,512]{2,1,0:T(8,128)(2,1)S(1)}, u32[]{:S(2)}, u32[]{:S(2)}) collective-permute-start(bf16[2,96,512]{2,1,0:T(8,128)(2,1)S(1)} %collective-permute-done.8.lc_ref), channel_id=1, source_target_pairs={{0,4},{1,5},{2,6},{3,7},{4,0},{5,1},{6,2},{7,3},{8,12},{9,13},{10,... | collective-permute-start | bytes 589832 | tf_op jit(solution)/shard_map/ppermute | solution.py:357
  25.2 1.3 %collective-permute-start.10 = (bf16[8,16,128]{2,1,0:T(8,128)(2,1)S(1)}, bf16[8,16,128]{2,1,0:T(8,128)(2,1)S(1)}, u32[]{:S(2)}, u32[]{:S(2)}) collective-permute-start(bf16[8,16,128]{2,1,0:T(8,128)(2,1)S(1)} %bitcast.79), channel_id=1, source_target_pairs={{0,4},{1,5},{2,6},{3,7},{4,0},{5,1},{6,2},{7,3},{8,12},{9,13},{10,... | collective-permute-start | bytes 98312 | tf_op jit(solution)/shard_map/ppermute | solution.py:357
  26.5 5.8 %collective-permute-start.11 = (bf16[96,128]{1,0:T(8,128)(2,1)S(1)}, bf16[96,128]{1,0:T(8,128)(2,1)S(1)}, u32[]{:S(2)}, u32[]{:S(2)}) collective-permute-start(bf16[96,128]{1,0:T(8,128)(2,1)S(1)} %pad_maximum_fusion.6), channel_id=1, source_target_pairs={{0,1},{1,2},{2,3},{3,0},{4,7},{5,4},{6,5},{7,6},{8,9},{9,10},{10,1... | collective-permute-start | bytes 73736 | tf_op jit(solution)/shard_map/ppermute | solution.py:357
  26.6 13.1 %collective-permute-start.13 = (bf16[2,168,512]{2,1,0:T(8,128)(2,1)S(1)}, bf16[2,168,512]{2,1,0:T(8,128)(2,1)S(1)}, u32[]{:S(2)}, u32[]{:S(2)}) collective-permute-start(bf16[2,168,512]{2,1,0:T(8,128)(2,1)S(1)} %maximum_maximum_fusion), channel_id=1, source_target_pairs={{0,2},{1,3},{2,0},{3,1},{4,8},{5,9},{6,10},{7,11},{8,4},{9,5},{10,... | collective-permute-start | bytes 1032200 | tf_op jit(solution)/shard_map/ppermute | solution.py:357
  32.3 1.2 %collective-permute-start.12 = (bf16[96,128]{1,0:T(8,128)(2,1)S(1)}, bf16[96,128]{1,0:T(8,128)(2,1)S(1)}, u32[]{:S(2)}, u32[]{:S(2)}) collective-permute-start(bf16[96,128]{1,0:T(8,128)(2,1)S(1)} %collective-permute-done.11.st_lc), channel_id=1, source_target_pairs={{0,4},{1,5},{2,6},{3,7},{4,0},{5,1},{6,2},{7,3},{8,12},{9,13},{10,... | collective-permute-start | bytes 73736 | tf_op jit(solution)/shard_map/ppermute | solution.py:357
  33.5 6.2 %collective-permute-start.14 = (bf16[168,128]{1,0:T(8,128)(2,1)S(1)}, bf16[168,128]{1,0:T(8,128)(2,1)S(1)}, u32[]{:S(2)}, u32[]{:S(2)}) collective-permute-start(bf16[168,128]{1,0:T(8,128)(2,1)S(1)} %pad_maximum_fusion.5), channel_id=1, source_target_pairs={{0,2},{1,3},{2,0},{3,1},{4,8},{5,9},{6,10},{7,11},{8,4},{9,5},{10,... | collective-permute-start | bytes 129032 | tf_op jit(solution)/shard_map/ppermute | solution.py:357

commit v8 on v7

--- a/solution.py
+++ b/solution.py
@@ -293,6 +293,12 @@
     key_sums(k_ref, v_ref, qall, gall, stall, bias_ref[...], stat_rows, finish)
 
 
+def second_leg_kernel(count, *refs):
+    outs = len(refs) - 4 - 3
+    near_key_kernel(*refs[count:outs], *refs[outs + 1 :])
+    query_kernel(*refs[:count], refs[outs])
+
+
 def far_key_kernel(
     k_ref, v_ref, off_ref, st_off, bias_ref, dk_in, dv_in, dk_ref, dv_ref, stat_rows
 ):
@@ -432,11 +438,12 @@
         jnp.concatenate([edge_of(stats_grid), corner_of(st_1, st_2)], axis=0), across
     )
 
-    d_query = call(query_kernel, array(n_own, width), (*query_side, stats_q, d_query))
-    d_key, d_value = call(
-        near_key_kernel,
-        (array(n_own, width, dtype=f32),) * 2,
+    first_args = (*query_side, stats_q, d_query)
+    d_query, d_key, d_value = call(
+        functools.partial(second_leg_kernel, len(first_args)),
+        (array(n_own, width), *(array(n_own, width, dtype=f32),) * 2),
         (
+            *first_args,
             k, v, q, g, flat(query_o), flat(grad_o), qg_1, qg_2,
             stats, flat(stats_o), st_1, st_2, bias_near,
         ),

time: 41.8 us -> 41.8 us (level)
    pallas_call x7 -> x6, Pallas kernels: 11.9 us -> 11.6 us  [call(): pl.pallas_call(body, out_shape=outs, in_specs=[smem] * scalars + [pl.Bloc...]
  transfers between devices with their start and end apart: 15 -> 15, of which waited for: 8 -> 8; matrix products, arithmetic and copies ran while one was open for 5% -> 5% of each run, Pallas kernels for 22% -> 21%
where the time goes in v8:
time: 41.8 us; the launch traced here: 41.7 us
  starting transfers between devices  15.1 us (36%)
  waiting for transfers between devices  11.8 us (28%)
  Pallas kernels  11.6 us (28%)
  other arithmetic  1.82 us (4%)
  between operations  1.05 us (3%)
    ppermute x15, starting transfers between devices, send(): return lax.ppermute(block, axes, route)  15.1 us
    ppermute x15, waiting for transfers between devices, send(): return lax.ppermute(block, axes, route)  11.8 us
    pallas_call x6, Pallas kernels, call(): pl.pallas_call(body, out_shape=outs, in_specs=[smem] * scalars + [pl.Bloc...  11.6 us
    another operation x1, other arithmetic, shards(): mine = lax.optimization_barrier(jnp.stack([key, value, query, grad]))  1.16 us
  transfers between devices with their start and end apart: 15, of which 8 were waited for; matrix products, arithmetic and copies ran while one was open for 5% of the time, Pallas kernels for 21%

profile of v8, /device:TPU:0, one launch (start us, length us, event | category | flops | bytes accessed | tf_op | source)
XLA Modules:
  0.0 41.7 jit_solution(8316360934005970817)
XLA Ops:
  0.6 0.5 %collective-permute-start = (bf16[8,16,512]{2,1,0:T(8,128)(2,1)}, bf16[8,16,512]{2,1,0:T(8,128)(2,1)S(1)}, u32[]{:S(2)}, u32[]{:S(2)}) collective-permute-start(bf16[8,16,512]{2,1,0:T(8,128)(2,1)} %param.7), channel_id=1, source_target_pairs={{0,4},{1,5},{2,6},{3,7},{4,0},{5,1},{6,2},{7,3},{8,12},{9,13},{10,... | collective-permute-start | bytes 393224 | tf_op jit(solution)/shard_map/ppermute | solution.py:363
  1.1 0.1 collective-permute-start.1
  1.2 0.4 %collective-permute-start.7 = (bf16[8,16,512]{2,1,0:T(8,128)(2,1)}, bf16[8,16,512]{2,1,0:T(8,128)(2,1)S(1)}, u32[]{:S(2)}, u32[]{:S(2)}) collective-permute-start(bf16[8,16,512]{2,1,0:T(8,128)(2,1)} %param.9), channel_id=1, source_target_pairs={{0,4},{1,5},{2,6},{3,7},{4,0},{5,1},{6,2},{7,3},{8,12},{9,13},{10,... | collective-permute-start | bytes 393224 | tf_op jit(solution)/shard_map/ppermute | solution.py:363
  1.7 0.1 collective-permute-start.6
  1.7 1.2 %pad_maximum_fusion = bf16[4,8,16,512]{3,2,1,0:T(8,128)(2,1)S(1)} fusion(bf16[1,8,16,512]{3,2,1,0:T(8,128)(2,1)} %bitcast.92, bf16[1,8,16,512]{3,2,1,0:T(8,128)(2,1)} %bitcast.93, bf16[1,8,16,512]{3,2,1,0:T(8,128)(2,1)} %bitcast.91, bf16[1,8,16,512]{3,2,1,0:T(8,128)(2,1)} %bitcast.90), kind=kLoop, calls=%fused_computation | loop fusion | flops 786432 | bytes 1048576 | tf_op jit(solution)/shard_map/stack | solution.py:379
  2.9 0.1 slice_bitcast_fusion.3
  3.1 0.1 pad_add_fusion.sc_ref
  3.2 0.0 collective-permute-done
  3.2 0.0 collective-permute-done.1
  3.4 3.1 %collective-permute-start.2 = (bf16[2,96,512]{2,1,0:T(8,128)(2,1)S(1)}, bf16[2,96,512]{2,1,0:T(8,128)(2,1)S(1)}, u32[]{:S(2)}, u32[]{:S(2)}) collective-permute-start(bf16[2,96,512]{2,1,0:T(8,128)(2,1)S(1)} %pad_maximum_fusion.1), channel_id=1, source_target_pairs={{0,1},{1,2},{2,3},{3,0},{4,7},{5,4},{6,5},{7,6},{8,9},{9,10},{10,1... | collective-permute-start | bytes 589832 | tf_op jit(solution)/shard_map/ppermute | solution.py:363
  6.5 2.7 %collective-permute-start.4 = (bf16[2,96,512]{2,1,0:T(8,128)(2,1)S(1)}, bf16[2,96,512]{2,1,0:T(8,128)(2,1)S(1)}, u32[]{:S(2)}, u32[]{:S(2)}) collective-permute-start(bf16[2,96,512]{2,1,0:T(8,128)(2,1)S(1)} %pad_maximum_fusion.2), channel_id=1, source_target_pairs={{0,2},{1,3},{2,0},{3,1},{4,8},{5,9},{6,10},{7,11},{8,4},{9,5},{10,... | collective-permute-start | bytes 589832 | tf_op jit(solution)/shard_map/ppermute | solution.py:363
  9.2 0.0 collective-permute-done.7
  9.2 0.0 collective-permute-done.6
  9.5 0.0 copy-start
  9.5 0.0 copy-start.1
  9.5 0.1 collective-permute-start.8
  9.6 4.5 %collective-permute-done.2.lc_ref = bf16[2,96,512]{2,1,0:T(8,128)(2,1)S(1)} collective-permute-done((bf16[2,96,512]{2,1,0:T(8,128)(2,1)S(1)}, bf16[2,96,512]{2,1,0:T(8,128)(2,1)S(1)}, u32[]{:S(2)}, u32[]{:S(2)}) %collective-permute-start.2) | collective-permute-done | bytes 196640 | tf_op jit(solution)/shard_map/ppermute | solution.py:363
  14.1 0.0 copy-done
  14.1 0.0 copy-done.1
  14.1 1.0 %shard_map.85 = (f32[128,448]{1,0:T(8,128)S(1)}, f32[128,168]{1,0:T(8,128)S(1)}, f32[616,128]{1,0:T(8,128)S(1)}) custom-call(s32[2]{0:T(128)S(1)} %pad_add_fusion.sc_ref, s32[2,64]{1,0:T(2,128)S(1)} %copy-done.1, s32[8,616]{1,0:T(8,128)S(1)} %copy-done), custom_call_target="tpu_custom_call" | custom-call | flops 1024 | bytes 1024 | tf_op jit(solution)/shard_map/pallas_call | solution.py:329
  15.1 0.1 collective-permute-start.3
  15.3 1.4 %collective-permute-done.3.s2_ref = bf16[2,96,512]{2,1,0:T(8,128)(2,1)S(1)} collective-permute-done((bf16[2,96,512]{2,1,0:T(8,128)(2,1)S(1)}, bf16[2,96,512]{2,1,0:T(8,128)(2,1)S(1)}, u32[]{:S(2)}, u32[]{:S(2)}) %collective-permute-start.3) | collective-permute-done | bytes 196640 | tf_op jit(solution)/shard_map/ppermute | solution.py:363
  16.7 4.3 %collective-permute-start.5 = (bf16[2,72,512]{2,1,0:T(8,128)(2,1)S(1)}, bf16[2,72,512]{2,1,0:T(8,128)(2,1)S(1)}, u32[]{:S(2)}, u32[]{:S(2)}) collective-permute-start(bf16[2,72,512]{2,1,0:T(8,128)(2,1)S(1)} %pad_maximum_fusion.4), channel_id=1, source_target_pairs={{0,2},{1,3},{2,0},{3,1},{4,8},{5,9},{6,10},{7,11},{8,4},{9,5},{10,... | collective-permute-start | bytes 442376 | tf_op jit(solution)/shard_map/ppermute | solution.py:363
  21.0 1.4 %shard_map.86 = (bf16[448,512]{1,0:T(8,128)(2,1)S(1)}, bf16[448,512]{1,0:T(8,128)(2,1)S(1)}, f32[16,128]{1,0:T(8,128)S(1)}, f32[16,128]{1,0:T(8,128)S(1)}, f32[16,128]{1,0:T(8,128)S(1)}) custom-call(bf16[128,512]{1,0:T(8,128)(2,1)S(1)} %bitcast.68, bf16[128,512]{1,0:T(8,128)(2,1)S(1)} %bitcast.63, bf16[128,512]{1,0:T(8,128)(2,1)S(1)} %bitcast.76, ...), custom_call_target="tpu_custom_call" | custom-call | flops 1024 | bytes 1024 | tf_op jit(solution)/shard_map/pallas_call | solution.py:329
  22.4 0.0 collective-permute-done.8.refs_16_
  22.4 0.1 collective-permute-start.9
  22.6 1.4 %collective-permute-done.9.refs_17_ = bf16[2,96,512]{2,1,0:T(8,128)(2,1)S(1)} collective-permute-done((bf16[2,96,512]{2,1,0:T(8,128)(2,1)S(1)}, bf16[2,96,512]{2,1,0:T(8,128)(2,1)S(1)}, u32[]{:S(2)}, u32[]{:S(2)}) %collective-permute-start.9) | collective-permute-done | bytes 196640 | tf_op jit(solution)/shard_map/ppermute | solution.py:363
  24.0 0.0 collective-permute-done.4.off_ref
  24.0 0.4 collective-permute-done.5.corner_ref
  24.3 0.8 %shard_map.87 = (bf16[128,128]{1,0:T(8,128)(2,1)S(1)}, bf16[168,512]{1,0:T(8,128)(2,1)S(1)}, bf16[168,512]{1,0:T(8,128)(2,1)S(1)}) custom-call(bf16[128,512]{1,0:T(8,128)(2,1)S(1)} %bitcast.69, bf16[128,512]{1,0:T(8,128)(2,1)S(1)} %bitcast.64, bf16[2,96,512]{2,1,0:T(8,128)(2,1)S(1)} %collective-permute-done.4.off_ref, ...), custom_call_target="tpu_custom_call" | custom-call | flops 1024 | bytes 1024 | tf_op jit(solution)/shard_map/pallas_call | solution.py:329
  25.2 0.1 collective-permute-start.10
  25.4 1.1 %collective-permute-done.10 = bf16[8,16,128]{2,1,0:T(8,128)(2,1)S(1)} collective-permute-done((bf16[8,16,128]{2,1,0:T(8,128)(2,1)S(1)}, bf16[8,16,128]{2,1,0:T(8,128)(2,1)S(1)}, u32[]{:S(2)}, u32[]{:S(2)}) %collective-permute-start.10) | collective-permute-done | bytes 32800 | tf_op jit(solution)/shard_map/ppermute | solution.py:363
  26.5 0.1 collective-permute-start.11
  26.6 2.8 %collective-permute-start.13 = (bf16[2,168,512]{2,1,0:T(8,128)(2,1)S(1)}, bf16[2,168,512]{2,1,0:T(8,128)(2,1)S(1)}, u32[]{:S(2)}, u32[]{:S(2)}) collective-permute-start(bf16[2,168,512]{2,1,0:T(8,128)(2,1)S(1)} %maximum_maximum_fusion), channel_id=1, source_target_pairs={{0,2},{1,3},{2,0},{3,1},{4,8},{5,9},{6,10},{7,11},{8,4},{9,5},{10,... | collective-permute-start | bytes 1032200 | tf_op jit(solution)/shard_map/ppermute | solution.py:363
  29.4 2.4 %shard_map.88.refs_9_ = bf16[128,384]{1,0:T(8,128)(2,1)S(1)} custom-call(bf16[128,512]{1,0:T(8,128)(2,1)S(1)} %bitcast.70, bf16[128,512]{1,0:T(8,128)(2,1)S(1)} %bitcast.65, bf16[448,512]{1,0:T(8,128)(2,1)S(1)} %get-tuple-element.33.k_near.refs_2_, bf16[448,512]{1,0:T(8,128)(2,1)S(1)} %get-tuple-element.34.v_near.refs_3_, ...), custom_call_target="tpu_custom_call" | custom-call | flops 1024 | bytes 1024 | tf_op jit(solution)/shard_map/pallas_call | solution.py:329
  31.8 0.4 %collective-permute-done.11.refs_20_ = bf16[96,128]{1,0:T(8,128)(2,1)S(1)} collective-permute-done((bf16[96,128]{1,0:T(8,128)(2,1)S(1)}, bf16[96,128]{1,0:T(8,128)(2,1)S(1)}, u32[]{:S(2)}, u32[]{:S(2)}) %collective-permute-start.11) | collective-permute-done | bytes 24608 | tf_op jit(solution)/shard_map/ppermute | solution.py:363
  32.3 0.0 collective-permute-start.12
  32.3 1.2 %collective-permute-done.12.refs_21_ = bf16[96,128]{1,0:T(8,128)(2,1)S(1)} collective-permute-done((bf16[96,128]{1,0:T(8,128)(2,1)S(1)}, bf16[96,128]{1,0:T(8,128)(2,1)S(1)}, u32[]{:S(2)}, u32[]{:S(2)}) %collective-permute-start.12) | collective-permute-done | bytes 24608 | tf_op jit(solution)/shard_map/ppermute | solution.py:363
  33.5 0.9 %collective-permute-start.14 = (bf16[168,128]{1,0:T(8,128)(2,1)S(1)}, bf16[168,128]{1,0:T(8,128)(2,1)S(1)}, u32[]{:S(2)}, u32[]{:S(2)}) collective-permute-start(bf16[168,128]{1,0:T(8,128)(2,1)S(1)} %pad_maximum_fusion.5), channel_id=1, source_target_pairs={{0,2},{1,3},{2,0},{3,1},{4,8},{5,9},{6,10},{7,11},{8,4},{9,5},{10,... | collective-permute-start | bytes 129032 | tf_op jit(solution)/shard_map/ppermute | solution.py:363
  34.4 4.0 %shard_map.89 = (bf16[128,512]{1,0:T(8,128)(2,1)}, f32[128,512]{1,0:T(8,128)S(1)}, f32[128,512]{1,0:T(8,128)S(1)}) custom-call(bf16[128,512]{1,0:T(8,128)(2,1)S(1)} %bitcast.71, bf16[128,512]{1,0:T(8,128)(2,1)S(1)} %bitcast.66, bf16[448,512]{1,0:T(8,128)(2,1)S(1)} %get-tuple-element.33.k_near.refs_2_, bf16[448,512]{1,0:T(8,128)(2,1)S(1)} %get-tuple-element.34.v_near.refs_3_, ...), custom_call_target="tpu_custom_call" | custom-call | flops 1024 | bytes 1024 | tf_op jit(solution)/shard_map/pallas_call | solution.py:329
  38.3 1.3 %collective-permute-done.14.st_off = bf16[168,128]{1,0:T(8,128)(2,1)S(1)} collective-permute-done((bf16[168,128]{1,0:T(8,128)(2,1)S(1)}, bf16[168,128]{1,0:T(8,128)(2,1)S(1)}, u32[]{:S(2)}, u32[]{:S(2)}) %collective-permute-start.14) | collective-permute-done | bytes 43040 | tf_op jit(solution)/shard_map/ppermute | solution.py:363
  39.7 0.0 collective-permute-done.13.off_ref
  39.7 2.0 %shard_map.90 = (bf16[128,512]{1,0:T(8,128)(2,1)}, bf16[128,512]{1,0:T(8,128)(2,1)}) custom-call(bf16[128,512]{1,0:T(8,128)(2,1)S(1)} %bitcast.78, bf16[128,512]{1,0:T(8,128)(2,1)S(1)} %bitcast.75, bf16[2,168,512]{2,1,0:T(8,128)(2,1)S(1)} %collective-permute-done.13.off_ref, bf16[168,128]{1,0:T(8,128)(2,1)S(1)} %collective-permute-done.14.st_off, ...), custom_call_target="tpu_custom_call" | custom-call | flops 1024 | bytes 1024 | tf_op jit(solution)/shard_map/pallas_call | solution.py:329
  (42 shorter events, 0.8 us)
Async XLA Ops:
  0.6 2.6 %collective-permute-start = (bf16[8,16,512]{2,1,0:T(8,128)(2,1)}, bf16[8,16,512]{2,1,0:T(8,128)(2,1)S(1)}, u32[]{:S(2)}, u32[]{:S(2)}) collective-permute-start(bf16[8,16,512]{2,1,0:T(8,128)(2,1)} %param.7), channel_id=1, source_target_pairs={{0,4},{1,5},{2,6},{3,7},{4,0},{5,1},{6,2},{7,3},{8,12},{9,13},{10,... | collective-permute-start | bytes 393224 | tf_op jit(solution)/shard_map/ppermute | solution.py:363
  1.1 2.1 %collective-permute-start.1 = (bf16[8,16,512]{2,1,0:T(8,128)(2,1)}, bf16[8,16,512]{2,1,0:T(8,128)(2,1)S(1)}, u32[]{:S(2)}, u32[]{:S(2)}) collective-permute-start(bf16[8,16,512]{2,1,0:T(8,128)(2,1)} %param.8), channel_id=1, source_target_pairs={{0,4},{1,5},{2,6},{3,7},{4,0},{5,1},{6,2},{7,3},{8,12},{9,13},{10,... | collective-permute-start | bytes 393224 | tf_op jit(solution)/shard_map/ppermute | solution.py:363
  1.2 8.0 %collective-permute-start.7 = (bf16[8,16,512]{2,1,0:T(8,128)(2,1)}, bf16[8,16,512]{2,1,0:T(8,128)(2,1)S(1)}, u32[]{:S(2)}, u32[]{:S(2)}) collective-permute-start(bf16[8,16,512]{2,1,0:T(8,128)(2,1)} %param.9), channel_id=1, source_target_pairs={{0,4},{1,5},{2,6},{3,7},{4,0},{5,1},{6,2},{7,3},{8,12},{9,13},{10,... | collective-permute-start | bytes 393224 | tf_op jit(solution)/shard_map/ppermute | solution.py:363
  1.7 7.5 %collective-permute-start.6 = (bf16[8,16,512]{2,1,0:T(8,128)(2,1)}, bf16[8,16,512]{2,1,0:T(8,128)(2,1)S(1)}, u32[]{:S(2)}, u32[]{:S(2)}) collective-permute-start(bf16[8,16,512]{2,1,0:T(8,128)(2,1)} %param.6), channel_id=1, source_target_pairs={{0,4},{1,5},{2,6},{3,7},{4,0},{5,1},{6,2},{7,3},{8,12},{9,13},{10,... | collective-permute-start | bytes 393224 | tf_op jit(solution)/shard_map/ppermute | solution.py:363
  3.4 10.8 %collective-permute-start.2 = (bf16[2,96,512]{2,1,0:T(8,128)(2,1)S(1)}, bf16[2,96,512]{2,1,0:T(8,128)(2,1)S(1)}, u32[]{:S(2)}, u32[]{:S(2)}) collective-permute-start(bf16[2,96,512]{2,1,0:T(8,128)(2,1)S(1)} %pad_maximum_fusion.1), channel_id=1, source_target_pairs={{0,1},{1,2},{2,3},{3,0},{4,7},{5,4},{6,5},{7,6},{8,9},{9,10},{10,1... | collective-permute-start | bytes 589832 | tf_op jit(solution)/shard_map/ppermute | solution.py:363
  6.5 17.5 %collective-permute-start.4 = (bf16[2,96,512]{2,1,0:T(8,128)(2,1)S(1)}, bf16[2,96,512]{2,1,0:T(8,128)(2,1)S(1)}, u32[]{:S(2)}, u32[]{:S(2)}) collective-permute-start(bf16[2,96,512]{2,1,0:T(8,128)(2,1)S(1)} %pad_maximum_fusion.2), channel_id=1, source_target_pairs={{0,2},{1,3},{2,0},{3,1},{4,8},{5,9},{6,10},{7,11},{8,4},{9,5},{10,... | collective-permute-start | bytes 589832 | tf_op jit(solution)/shard_map/ppermute | solution.py:363
  9.5 4.7 %copy-start = (s32[8,616]{1,0:T(8,128)S(1)}, s32[8,616]{1,0:T(8,128)}, u32[]{:S(2)}) copy-start(s32[8,616]{1,0:T(8,128)} %constant.17.clone.table_hbm) | copy-start | bytes 59140
  9.5 4.7 %copy-start.1 = (s32[2,64]{1,0:T(2,128)S(1)}, s32[2,64]{1,0:T(2,128)}, u32[]{:S(2)}) copy-start(s32[2,64]{1,0:T(2,128)} %reach_hbm) | copy-start | bytes 1540
  9.5 12.9 %collective-permute-start.8 = (bf16[2,96,512]{2,1,0:T(8,128)(2,1)S(1)}, bf16[2,96,512]{2,1,0:T(8,128)(2,1)S(1)}, u32[]{:S(2)}, u32[]{:S(2)}) collective-permute-start(bf16[2,96,512]{2,1,0:T(8,128)(2,1)S(1)} %pad_maximum_fusion.3), channel_id=1, source_target_pairs={{0,1},{1,2},{2,3},{3,0},{4,7},{5,4},{6,5},{7,6},{8,9},{9,10},{10,1... | collective-permute-start | bytes 589832 | tf_op jit(solution)/shard_map/ppermute | solution.py:363
  15.1 1.5 %collective-permute-start.3 = (bf16[2,96,512]{2,1,0:T(8,128)(2,1)S(1)}, bf16[2,96,512]{2,1,0:T(8,128)(2,1)S(1)}, u32[]{:S(2)}, u32[]{:S(2)}) collective-permute-start(bf16[2,96,512]{2,1,0:T(8,128)(2,1)S(1)} %collective-permute-done.2.lc_ref), channel_id=1, source_target_pairs={{0,4},{1,5},{2,6},{3,7},{4,0},{5,1},{6,2},{7,3},{8,12},{9,13},{10,... | collective-permute-start | bytes 589832 | tf_op jit(solution)/shard_map/ppermute | solution.py:363
  16.7 7.6 %collective-permute-start.5 = (bf16[2,72,512]{2,1,0:T(8,128)(2,1)S(1)}, bf16[2,72,512]{2,1,0:T(8,128)(2,1)S(1)}, u32[]{:S(2)}, u32[]{:S(2)}) collective-permute-start(bf16[2,72,512]{2,1,0:T(8,128)(2,1)S(1)} %pad_maximum_fusion.4), channel_id=1, source_target_pairs={{0,2},{1,3},{2,0},{3,1},{4,8},{5,9},{6,10},{7,11},{8,4},{9,5},{10,... | collective-permute-start | bytes 442376 | tf_op jit(solution)/shard_map/ppermute | solution.py:363
  22.4 1.5 %collective-permute-start.9 = (bf16[2,96,512]{2,1,0:T(8,128)(2,1)S(1)}, bf16[2,96,512]{2,1,0:T(8,128)(2,1)S(1)}, u32[]{:S(2)}, u32[]{:S(2)}) collective-permute-start(bf16[2,96,512]{2,1,0:T(8,128)(2,1)S(1)} %collective-permute-done.8.refs_16_), channel_id=1, source_target_pairs={{0,4},{1,5},{2,6},{3,7},{4,0},{5,1},{6,2},{7,3},{8,12},{9,13},{10,... | collective-permute-start | bytes 589832 | tf_op jit(solution)/shard_map/ppermute | solution.py:363
  25.2 1.3 %collective-permute-start.10 = (bf16[8,16,128]{2,1,0:T(8,128)(2,1)S(1)}, bf16[8,16,128]{2,1,0:T(8,128)(2,1)S(1)}, u32[]{:S(2)}, u32[]{:S(2)}) collective-permute-start(bf16[8,16,128]{2,1,0:T(8,128)(2,1)S(1)} %bitcast.79), channel_id=1, source_target_pairs={{0,4},{1,5},{2,6},{3,7},{4,0},{5,1},{6,2},{7,3},{8,12},{9,13},{10,... | collective-permute-start | bytes 98312 | tf_op jit(solution)/shard_map/ppermute | solution.py:363
  26.5 5.8 %collective-permute-start.11 = (bf16[96,128]{1,0:T(8,128)(2,1)S(1)}, bf16[96,128]{1,0:T(8,128)(2,1)S(1)}, u32[]{:S(2)}, u32[]{:S(2)}) collective-permute-start(bf16[96,128]{1,0:T(8,128)(2,1)S(1)} %pad_maximum_fusion.6), channel_id=1, source_target_pairs={{0,1},{1,2},{2,3},{3,0},{4,7},{5,4},{6,5},{7,6},{8,9},{9,10},{10,1... | collective-permute-start | bytes 73736 | tf_op jit(solution)/shard_map/ppermute | solution.py:363
  26.6 13.1 %collective-permute-start.13 = (bf16[2,168,512]{2,1,0:T(8,128)(2,1)S(1)}, bf16[2,168,512]{2,1,0:T(8,128)(2,1)S(1)}, u32[]{:S(2)}, u32[]{:S(2)}) collective-permute-start(bf16[2,168,512]{2,1,0:T(8,128)(2,1)S(1)} %maximum_maximum_fusion), channel_id=1, source_target_pairs={{0,2},{1,3},{2,0},{3,1},{4,8},{5,9},{6,10},{7,11},{8,4},{9,5},{10,... | collective-permute-start | bytes 1032200 | tf_op jit(solution)/shard_map/ppermute | solution.py:363
  32.3 1.2 %collective-permute-start.12 = (bf16[96,128]{1,0:T(8,128)(2,1)S(1)}, bf16[96,128]{1,0:T(8,128)(2,1)S(1)}, u32[]{:S(2)}, u32[]{:S(2)}) collective-permute-start(bf16[96,128]{1,0:T(8,128)(2,1)S(1)} %collective-permute-done.11.refs_20_), channel_id=1, source_target_pairs={{0,4},{1,5},{2,6},{3,7},{4,0},{5,1},{6,2},{7,3},{8,12},{9,13},{10,... | collective-permute-start | bytes 73736 | tf_op jit(solution)/shard_map/ppermute | solution.py:363
  33.5 6.2 %collective-permute-start.14 = (bf16[168,128]{1,0:T(8,128)(2,1)S(1)}, bf16[168,128]{1,0:T(8,128)(2,1)S(1)}, u32[]{:S(2)}, u32[]{:S(2)}) collective-permute-start(bf16[168,128]{1,0:T(8,128)(2,1)S(1)} %pad_maximum_fusion.5), channel_id=1, source_target_pairs={{0,2},{1,3},{2,0},{3,1},{4,8},{5,9},{6,10},{7,11},{8,4},{9,5},{10,... | collective-permute-start | bytes 129032 | tf_op jit(solution)/shard_map/ppermute | solution.py:363

commit v9 on v8

--- a/solution.py
+++ b/solution.py
@@ -334,7 +334,7 @@
             out_specs=jax.tree.map(lambda _: vmem, outs),
             scratch_shapes=scratch,
             compiler_params=pltpu.CompilerParams(vmem_limit_bytes=16 << 20),
-            cost_estimate=pl.CostEstimate(flops=flops, bytes_accessed=1 << 10, transcendentals=0),
+            cost_estimate=pl.CostEstimate(flops=flops, bytes_accessed=1 << 20, transcendentals=0),
         )(*operands)
 
     def array(*shape, dtype=jnp.bfloat16):

time: 41.8 us -> 41.8 us (level)
  no operation moved by 1% of the time
where the time goes in v9:
time: 41.8 us; the launch traced here: 41.7 us
  starting transfers between devices  15.1 us (36%)
  waiting for transfers between devices  11.8 us (28%)
  Pallas kernels  11.6 us (28%)
  other arithmetic  1.82 us (4%)
  between operations  1.05 us (3%)
    ppermute x15, starting transfers between devices, send(): return lax.ppermute(block, axes, route)  15.1 us
    ppermute x15, waiting for transfers between devices, send(): return lax.ppermute(block, axes, route)  11.8 us
    pallas_call x6, Pallas kernels, call(): pl.pallas_call(body, out_shape=outs, in_specs=[smem] * scalars + [pl.Bloc...  11.6 us
    another operation x1, other arithmetic, shards(): mine = lax.optimization_barrier(jnp.stack([key, value, query, grad]))  1.16 us
  transfers between devices with their start and end apart: 15, of which 8 were waited for; matrix products, arithmetic and copies ran while one was open for 5% of the time, Pallas kernels for 21%

profile of v9, /device:TPU:0, one launch (start us, length us, event | category | flops | bytes accessed | tf_op | source)
XLA Modules:
  0.0 41.7 jit_solution(8316360934005970817)
XLA Ops:
  0.6 0.5 %collective-permute-start = (bf16[8,16,512]{2,1,0:T(8,128)(2,1)}, bf16[8,16,512]{2,1,0:T(8,128)(2,1)S(1)}, u32[]{:S(2)}, u32[]{:S(2)}) collective-permute-start(bf16[8,16,512]{2,1,0:T(8,128)(2,1)} %param.7), channel_id=1, source_target_pairs={{0,4},{1,5},{2,6},{3,7},{4,0},{5,1},{6,2},{7,3},{8,12},{9,13},{10,... | collective-permute-start | bytes 393224 | tf_op jit(solution)/shard_map/ppermute | solution.py:363
  1.1 0.1 collective-permute-start.1
  1.2 0.4 %collective-permute-start.7 = (bf16[8,16,512]{2,1,0:T(8,128)(2,1)}, bf16[8,16,512]{2,1,0:T(8,128)(2,1)S(1)}, u32[]{:S(2)}, u32[]{:S(2)}) collective-permute-start(bf16[8,16,512]{2,1,0:T(8,128)(2,1)} %param.9), channel_id=1, source_target_pairs={{0,4},{1,5},{2,6},{3,7},{4,0},{5,1},{6,2},{7,3},{8,12},{9,13},{10,... | collective-permute-start | bytes 393224 | tf_op jit(solution)/shard_map/ppermute | solution.py:363
  1.7 0.1 collective-permute-start.6
  1.7 1.2 %pad_maximum_fusion = bf16[4,8,16,512]{3,2,1,0:T(8,128)(2,1)S(1)} fusion(bf16[1,8,16,512]{3,2,1,0:T(8,128)(2,1)} %bitcast.92, bf16[1,8,16,512]{3,2,1,0:T(8,128)(2,1)} %bitcast.93, bf16[1,8,16,512]{3,2,1,0:T(8,128)(2,1)} %bitcast.91, bf16[1,8,16,512]{3,2,1,0:T(8,128)(2,1)} %bitcast.90), kind=kLoop, calls=%fused_computation | loop fusion | flops 786432 | bytes 1048576 | tf_op jit(solution)/shard_map/stack | solution.py:379
  2.9 0.1 slice_bitcast_fusion.3
  3.1 0.1 pad_add_fusion.sc_ref
  3.2 0.0 collective-permute-done
  3.2 0.0 collective-permute-done.1
  3.4 3.1 %collective-permute-start.2 = (bf16[2,96,512]{2,1,0:T(8,128)(2,1)S(1)}, bf16[2,96,512]{2,1,0:T(8,128)(2,1)S(1)}, u32[]{:S(2)}, u32[]{:S(2)}) collective-permute-start(bf16[2,96,512]{2,1,0:T(8,128)(2,1)S(1)} %pad_maximum_fusion.1), channel_id=1, source_target_pairs={{0,1},{1,2},{2,3},{3,0},{4,7},{5,4},{6,5},{7,6},{8,9},{9,10},{10,1... | collective-permute-start | bytes 589832 | tf_op jit(solution)/shard_map/ppermute | solution.py:363
  6.5 2.7 %collective-permute-start.4 = (bf16[2,96,512]{2,1,0:T(8,128)(2,1)S(1)}, bf16[2,96,512]{2,1,0:T(8,128)(2,1)S(1)}, u32[]{:S(2)}, u32[]{:S(2)}) collective-permute-start(bf16[2,96,512]{2,1,0:T(8,128)(2,1)S(1)} %pad_maximum_fusion.2), channel_id=1, source_target_pairs={{0,2},{1,3},{2,0},{3,1},{4,8},{5,9},{6,10},{7,11},{8,4},{9,5},{10,... | collective-permute-start | bytes 589832 | tf_op jit(solution)/shard_map/ppermute | solution.py:363
  9.2 0.0 collective-permute-done.7
  9.2 0.0 collective-permute-done.6
  9.5 0.0 copy-start
  9.5 0.0 copy-start.1
  9.5 0.1 collective-permute-start.8
  9.6 4.5 %collective-permute-done.2.lc_ref = bf16[2,96,512]{2,1,0:T(8,128)(2,1)S(1)} collective-permute-done((bf16[2,96,512]{2,1,0:T(8,128)(2,1)S(1)}, bf16[2,96,512]{2,1,0:T(8,128)(2,1)S(1)}, u32[]{:S(2)}, u32[]{:S(2)}) %collective-permute-start.2) | collective-permute-done | bytes 196640 | tf_op jit(solution)/shard_map/ppermute | solution.py:363
  14.1 0.0 copy-done
  14.1 0.0 copy-done.1
  14.1 1.0 %shard_map.85 = (f32[128,448]{1,0:T(8,128)S(1)}, f32[128,168]{1,0:T(8,128)S(1)}, f32[616,128]{1,0:T(8,128)S(1)}) custom-call(s32[2]{0:T(128)S(1)} %pad_add_fusion.sc_ref, s32[2,64]{1,0:T(2,128)S(1)} %copy-done.1, s32[8,616]{1,0:T(8,128)S(1)} %copy-done), custom_call_target="tpu_custom_call" | custom-call | flops 1024 | bytes 1048576 | tf_op jit(solution)/shard_map/pallas_call | solution.py:329
  15.1 0.1 collective-permute-start.3
  15.3 1.4 %collective-permute-done.3.s2_ref = bf16[2,96,512]{2,1,0:T(8,128)(2,1)S(1)} collective-permute-done((bf16[2,96,512]{2,1,0:T(8,128)(2,1)S(1)}, bf16[2,96,512]{2,1,0:T(8,128)(2,1)S(1)}, u32[]{:S(2)}, u32[]{:S(2)}) %collective-permute-start.3) | collective-permute-done | bytes 196640 | tf_op jit(solution)/shard_map/ppermute | solution.py:363
  16.7 4.3 %collective-permute-start.5 = (bf16[2,72,512]{2,1,0:T(8,128)(2,1)S(1)}, bf16[2,72,512]{2,1,0:T(8,128)(2,1)S(1)}, u32[]{:S(2)}, u32[]{:S(2)}) collective-permute-start(bf16[2,72,512]{2,1,0:T(8,128)(2,1)S(1)} %pad_maximum_fusion.4), channel_id=1, source_target_pairs={{0,2},{1,3},{2,0},{3,1},{4,8},{5,9},{6,10},{7,11},{8,4},{9,5},{10,... | collective-permute-start | bytes 442376 | tf_op jit(solution)/shard_map/ppermute | solution.py:363
  21.0 1.4 %shard_map.86 = (bf16[448,512]{1,0:T(8,128)(2,1)S(1)}, bf16[448,512]{1,0:T(8,128)(2,1)S(1)}, f32[16,128]{1,0:T(8,128)S(1)}, f32[16,128]{1,0:T(8,128)S(1)}, f32[16,128]{1,0:T(8,128)S(1)}) custom-call(bf16[128,512]{1,0:T(8,128)(2,1)S(1)} %bitcast.68, bf16[128,512]{1,0:T(8,128)(2,1)S(1)} %bitcast.63, bf16[128,512]{1,0:T(8,128)(2,1)S(1)} %bitcast.76, ...), custom_call_target="tpu_custom_call" | custom-call | flops 1024 | bytes 1048576 | tf_op jit(solution)/shard_map/pallas_call | solution.py:329
  22.4 0.0 collective-permute-done.8.refs_16_
  22.4 0.1 collective-permute-start.9
  22.6 1.4 %collective-permute-done.9.refs_17_ = bf16[2,96,512]{2,1,0:T(8,128)(2,1)S(1)} collective-permute-done((bf16[2,96,512]{2,1,0:T(8,128)(2,1)S(1)}, bf16[2,96,512]{2,1,0:T(8,128)(2,1)S(1)}, u32[]{:S(2)}, u32[]{:S(2)}) %collective-permute-start.9) | collective-permute-done | bytes 196640 | tf_op jit(solution)/shard_map/ppermute | solution.py:363
  24.0 0.0 collective-permute-done.4.off_ref
  24.0 0.4 collective-permute-done.5.corner_ref
  24.3 0.8 %shard_map.87 = (bf16[128,128]{1,0:T(8,128)(2,1)S(1)}, bf16[168,512]{1,0:T(8,128)(2,1)S(1)}, bf16[168,512]{1,0:T(8,128)(2,1)S(1)}) custom-call(bf16[128,512]{1,0:T(8,128)(2,1)S(1)} %bitcast.69, bf16[128,512]{1,0:T(8,128)(2,1)S(1)} %bitcast.64, bf16[2,96,512]{2,1,0:T(8,128)(2,1)S(1)} %collective-permute-done.4.off_ref, ...), custom_call_target="tpu_custom_call" | custom-call | flops 1024 | bytes 1048576 | tf_op jit(solution)/shard_map/pallas_call | solution.py:329
  25.2 0.1 collective-permute-start.10
  25.4 1.1 %collective-permute-done.10 = bf16[8,16,128]{2,1,0:T(8,128)(2,1)S(1)} collective-permute-done((bf16[8,16,128]{2,1,0:T(8,128)(2,1)S(1)}, bf16[8,16,128]{2,1,0:T(8,128)(2,1)S(1)}, u32[]{:S(2)}, u32[]{:S(2)}) %collective-permute-start.10) | collective-permute-done | bytes 32800 | tf_op jit(solution)/shard_map/ppermute | solution.py:363
  26.5 0.1 collective-permute-start.11
  26.6 2.8 %collective-permute-start.13 = (bf16[2,168,512]{2,1,0:T(8,128)(2,1)S(1)}, bf16[2,168,512]{2,1,0:T(8,128)(2,1)S(1)}, u32[]{:S(2)}, u32[]{:S(2)}) collective-permute-start(bf16[2,168,512]{2,1,0:T(8,128)(2,1)S(1)} %maximum_maximum_fusion), channel_id=1, source_target_pairs={{0,2},{1,3},{2,0},{3,1},{4,8},{5,9},{6,10},{7,11},{8,4},{9,5},{10,... | collective-permute-start | bytes 1032200 | tf_op jit(solution)/shard_map/ppermute | solution.py:363
  29.4 2.4 %shard_map.88.refs_9_ = bf16[128,384]{1,0:T(8,128)(2,1)S(1)} custom-call(bf16[128,512]{1,0:T(8,128)(2,1)S(1)} %bitcast.70, bf16[128,512]{1,0:T(8,128)(2,1)S(1)} %bitcast.65, bf16[448,512]{1,0:T(8,128)(2,1)S(1)} %get-tuple-element.33.k_near.refs_2_, bf16[448,512]{1,0:T(8,128)(2,1)S(1)} %get-tuple-element.34.v_near.refs_3_, ...), custom_call_target="tpu_custom_call" | custom-call | flops 1024 | bytes 1048576 | tf_op jit(solution)/shard_map/pallas_call | solution.py:329
  31.8 0.4 %collective-permute-done.11.refs_20_ = bf16[96,128]{1,0:T(8,128)(2,1)S(1)} collective-permute-done((bf16[96,128]{1,0:T(8,128)(2,1)S(1)}, bf16[96,128]{1,0:T(8,128)(2,1)S(1)}, u32[]{:S(2)}, u32[]{:S(2)}) %collective-permute-start.11) | collective-permute-done | bytes 24608 | tf_op jit(solution)/shard_map/ppermute | solution.py:363
  32.3 0.0 collective-permute-start.12
  32.3 1.2 %collective-permute-done.12.refs_21_ = bf16[96,128]{1,0:T(8,128)(2,1)S(1)} collective-permute-done((bf16[96,128]{1,0:T(8,128)(2,1)S(1)}, bf16[96,128]{1,0:T(8,128)(2,1)S(1)}, u32[]{:S(2)}, u32[]{:S(2)}) %collective-permute-start.12) | collective-permute-done | bytes 24608 | tf_op jit(solution)/shard_map/ppermute | solution.py:363
  33.5 0.9 %collective-permute-start.14 = (bf16[168,128]{1,0:T(8,128)(2,1)S(1)}, bf16[168,128]{1,0:T(8,128)(2,1)S(1)}, u32[]{:S(2)}, u32[]{:S(2)}) collective-permute-start(bf16[168,128]{1,0:T(8,128)(2,1)S(1)} %pad_maximum_fusion.5), channel_id=1, source_target_pairs={{0,2},{1,3},{2,0},{3,1},{4,8},{5,9},{6,10},{7,11},{8,4},{9,5},{10,... | collective-permute-start | bytes 129032 | tf_op jit(solution)/shard_map/ppermute | solution.py:363
  34.4 4.0 %shard_map.89 = (bf16[128,512]{1,0:T(8,128)(2,1)}, f32[128,512]{1,0:T(8,128)S(1)}, f32[128,512]{1,0:T(8,128)S(1)}) custom-call(bf16[128,512]{1,0:T(8,128)(2,1)S(1)} %bitcast.71, bf16[128,512]{1,0:T(8,128)(2,1)S(1)} %bitcast.66, bf16[448,512]{1,0:T(8,128)(2,1)S(1)} %get-tuple-element.33.k_near.refs_2_, bf16[448,512]{1,0:T(8,128)(2,1)S(1)} %get-tuple-element.34.v_near.refs_3_, ...), custom_call_target="tpu_custom_call" | custom-call | flops 1024 | bytes 1048576 | tf_op jit(solution)/shard_map/pallas_call | solution.py:329
  38.3 1.3 %collective-permute-done.14.st_off = bf16[168,128]{1,0:T(8,128)(2,1)S(1)} collective-permute-done((bf16[168,128]{1,0:T(8,128)(2,1)S(1)}, bf16[168,128]{1,0:T(8,128)(2,1)S(1)}, u32[]{:S(2)}, u32[]{:S(2)}) %collective-permute-start.14) | collective-permute-done | bytes 43040 | tf_op jit(solution)/shard_map/ppermute | solution.py:363
  39.7 0.0 collective-permute-done.13.off_ref
  39.7 2.0 %shard_map.90 = (bf16[128,512]{1,0:T(8,128)(2,1)}, bf16[128,512]{1,0:T(8,128)(2,1)}) custom-call(bf16[128,512]{1,0:T(8,128)(2,1)S(1)} %bitcast.78, bf16[128,512]{1,0:T(8,128)(2,1)S(1)} %bitcast.75, bf16[2,168,512]{2,1,0:T(8,128)(2,1)S(1)} %collective-permute-done.13.off_ref, bf16[168,128]{1,0:T(8,128)(2,1)S(1)} %collective-permute-done.14.st_off, ...), custom_call_target="tpu_custom_call" | custom-call | flops 1024 | bytes 1048576 | tf_op jit(solution)/shard_map/pallas_call | solution.py:329
  (42 shorter events, 0.8 us)
Async XLA Ops:
  0.6 2.6 %collective-permute-start = (bf16[8,16,512]{2,1,0:T(8,128)(2,1)}, bf16[8,16,512]{2,1,0:T(8,128)(2,1)S(1)}, u32[]{:S(2)}, u32[]{:S(2)}) collective-permute-start(bf16[8,16,512]{2,1,0:T(8,128)(2,1)} %param.7), channel_id=1, source_target_pairs={{0,4},{1,5},{2,6},{3,7},{4,0},{5,1},{6,2},{7,3},{8,12},{9,13},{10,... | collective-permute-start | bytes 393224 | tf_op jit(solution)/shard_map/ppermute | solution.py:363
  1.1 2.1 %collective-permute-start.1 = (bf16[8,16,512]{2,1,0:T(8,128)(2,1)}, bf16[8,16,512]{2,1,0:T(8,128)(2,1)S(1)}, u32[]{:S(2)}, u32[]{:S(2)}) collective-permute-start(bf16[8,16,512]{2,1,0:T(8,128)(2,1)} %param.8), channel_id=1, source_target_pairs={{0,4},{1,5},{2,6},{3,7},{4,0},{5,1},{6,2},{7,3},{8,12},{9,13},{10,... | collective-permute-start | bytes 393224 | tf_op jit(solution)/shard_map/ppermute | solution.py:363
  1.2 8.0 %collective-permute-start.7 = (bf16[8,16,512]{2,1,0:T(8,128)(2,1)}, bf16[8,16,512]{2,1,0:T(8,128)(2,1)S(1)}, u32[]{:S(2)}, u32[]{:S(2)}) collective-permute-start(bf16[8,16,512]{2,1,0:T(8,128)(2,1)} %param.9), channel_id=1, source_target_pairs={{0,4},{1,5},{2,6},{3,7},{4,0},{5,1},{6,2},{7,3},{8,12},{9,13},{10,... | collective-permute-start | bytes 393224 | tf_op jit(solution)/shard_map/ppermute | solution.py:363
  1.7 7.5 %collective-permute-start.6 = (bf16[8,16,512]{2,1,0:T(8,128)(2,1)}, bf16[8,16,512]{2,1,0:T(8,128)(2,1)S(1)}, u32[]{:S(2)}, u32[]{:S(2)}) collective-permute-start(bf16[8,16,512]{2,1,0:T(8,128)(2,1)} %param.6), channel_id=1, source_target_pairs={{0,4},{1,5},{2,6},{3,7},{4,0},{5,1},{6,2},{7,3},{8,12},{9,13},{10,... | collective-permute-start | bytes 393224 | tf_op jit(solution)/shard_map/ppermute | solution.py:363
  3.4 10.8 %collective-permute-start.2 = (bf16[2,96,512]{2,1,0:T(8,128)(2,1)S(1)}, bf16[2,96,512]{2,1,0:T(8,128)(2,1)S(1)}, u32[]{:S(2)}, u32[]{:S(2)}) collective-permute-start(bf16[2,96,512]{2,1,0:T(8,128)(2,1)S(1)} %pad_maximum_fusion.1), channel_id=1, source_target_pairs={{0,1},{1,2},{2,3},{3,0},{4,7},{5,4},{6,5},{7,6},{8,9},{9,10},{10,1... | collective-permute-start | bytes 589832 | tf_op jit(solution)/shard_map/ppermute | solution.py:363
  6.5 17.5 %collective-permute-start.4 = (bf16[2,96,512]{2,1,0:T(8,128)(2,1)S(1)}, bf16[2,96,512]{2,1,0:T(8,128)(2,1)S(1)}, u32[]{:S(2)}, u32[]{:S(2)}) collective-permute-start(bf16[2,96,512]{2,1,0:T(8,128)(2,1)S(1)} %pad_maximum_fusion.2), channel_id=1, source_target_pairs={{0,2},{1,3},{2,0},{3,1},{4,8},{5,9},{6,10},{7,11},{8,4},{9,5},{10,... | collective-permute-start | bytes 589832 | tf_op jit(solution)/shard_map/ppermute | solution.py:363
  9.5 4.7 %copy-start = (s32[8,616]{1,0:T(8,128)S(1)}, s32[8,616]{1,0:T(8,128)}, u32[]{:S(2)}) copy-start(s32[8,616]{1,0:T(8,128)} %constant.17.clone.table_hbm) | copy-start | bytes 59140
  9.5 4.7 %copy-start.1 = (s32[2,64]{1,0:T(2,128)S(1)}, s32[2,64]{1,0:T(2,128)}, u32[]{:S(2)}) copy-start(s32[2,64]{1,0:T(2,128)} %reach_hbm) | copy-start | bytes 1540
  9.5 12.9 %collective-permute-start.8 = (bf16[2,96,512]{2,1,0:T(8,128)(2,1)S(1)}, bf16[2,96,512]{2,1,0:T(8,128)(2,1)S(1)}, u32[]{:S(2)}, u32[]{:S(2)}) collective-permute-start(bf16[2,96,512]{2,1,0:T(8,128)(2,1)S(1)} %pad_maximum_fusion.3), channel_id=1, source_target_pairs={{0,1},{1,2},{2,3},{3,0},{4,7},{5,4},{6,5},{7,6},{8,9},{9,10},{10,1... | collective-permute-start | bytes 589832 | tf_op jit(solution)/shard_map/ppermute | solution.py:363
  15.1 1.5 %collective-permute-start.3 = (bf16[2,96,512]{2,1,0:T(8,128)(2,1)S(1)}, bf16[2,96,512]{2,1,0:T(8,128)(2,1)S(1)}, u32[]{:S(2)}, u32[]{:S(2)}) collective-permute-start(bf16[2,96,512]{2,1,0:T(8,128)(2,1)S(1)} %collective-permute-done.2.lc_ref), channel_id=1, source_target_pairs={{0,4},{1,5},{2,6},{3,7},{4,0},{5,1},{6,2},{7,3},{8,12},{9,13},{10,... | collective-permute-start | bytes 589832 | tf_op jit(solution)/shard_map/ppermute | solution.py:363
  16.7 7.6 %collective-permute-start.5 = (bf16[2,72,512]{2,1,0:T(8,128)(2,1)S(1)}, bf16[2,72,512]{2,1,0:T(8,128)(2,1)S(1)}, u32[]{:S(2)}, u32[]{:S(2)}) collective-permute-start(bf16[2,72,512]{2,1,0:T(8,128)(2,1)S(1)} %pad_maximum_fusion.4), channel_id=1, source_target_pairs={{0,2},{1,3},{2,0},{3,1},{4,8},{5,9},{6,10},{7,11},{8,4},{9,5},{10,... | collective-permute-start | bytes 442376 | tf_op jit(solution)/shard_map/ppermute | solution.py:363
  22.4 1.5 %collective-permute-start.9 = (bf16[2,96,512]{2,1,0:T(8,128)(2,1)S(1)}, bf16[2,96,512]{2,1,0:T(8,128)(2,1)S(1)}, u32[]{:S(2)}, u32[]{:S(2)}) collective-permute-start(bf16[2,96,512]{2,1,0:T(8,128)(2,1)S(1)} %collective-permute-done.8.refs_16_), channel_id=1, source_target_pairs={{0,4},{1,5},{2,6},{3,7},{4,0},{5,1},{6,2},{7,3},{8,12},{9,13},{10,... | collective-permute-start | bytes 589832 | tf_op jit(solution)/shard_map/ppermute | solution.py:363
  25.2 1.3 %collective-permute-start.10 = (bf16[8,16,128]{2,1,0:T(8,128)(2,1)S(1)}, bf16[8,16,128]{2,1,0:T(8,128)(2,1)S(1)}, u32[]{:S(2)}, u32[]{:S(2)}) collective-permute-start(bf16[8,16,128]{2,1,0:T(8,128)(2,1)S(1)} %bitcast.79), channel_id=1, source_target_pairs={{0,4},{1,5},{2,6},{3,7},{4,0},{5,1},{6,2},{7,3},{8,12},{9,13},{10,... | collective-permute-start | bytes 98312 | tf_op jit(solution)/shard_map/ppermute | solution.py:363
  26.5 5.8 %collective-permute-start.11 = (bf16[96,128]{1,0:T(8,128)(2,1)S(1)}, bf16[96,128]{1,0:T(8,128)(2,1)S(1)}, u32[]{:S(2)}, u32[]{:S(2)}) collective-permute-start(bf16[96,128]{1,0:T(8,128)(2,1)S(1)} %pad_maximum_fusion.6), channel_id=1, source_target_pairs={{0,1},{1,2},{2,3},{3,0},{4,7},{5,4},{6,5},{7,6},{8,9},{9,10},{10,1... | collective-permute-start | bytes 73736 | tf_op jit(solution)/shard_map/ppermute | solution.py:363
  26.6 13.1 %collective-permute-start.13 = (bf16[2,168,512]{2,1,0:T(8,128)(2,1)S(1)}, bf16[2,168,512]{2,1,0:T(8,128)(2,1)S(1)}, u32[]{:S(2)}, u32[]{:S(2)}) collective-permute-start(bf16[2,168,512]{2,1,0:T(8,128)(2,1)S(1)} %maximum_maximum_fusion), channel_id=1, source_target_pairs={{0,2},{1,3},{2,0},{3,1},{4,8},{5,9},{6,10},{7,11},{8,4},{9,5},{10,... | collective-permute-start | bytes 1032200 | tf_op jit(solution)/shard_map/ppermute | solution.py:363
  32.3 1.2 %collective-permute-start.12 = (bf16[96,128]{1,0:T(8,128)(2,1)S(1)}, bf16[96,128]{1,0:T(8,128)(2,1)S(1)}, u32[]{:S(2)}, u32[]{:S(2)}) collective-permute-start(bf16[96,128]{1,0:T(8,128)(2,1)S(1)} %collective-permute-done.11.refs_20_), channel_id=1, source_target_pairs={{0,4},{1,5},{2,6},{3,7},{4,0},{5,1},{6,2},{7,3},{8,12},{9,13},{10,... | collective-permute-start | bytes 73736 | tf_op jit(solution)/shard_map/ppermute | solution.py:363
  33.5 6.2 %collective-permute-start.14 = (bf16[168,128]{1,0:T(8,128)(2,1)S(1)}, bf16[168,128]{1,0:T(8,128)(2,1)S(1)}, u32[]{:S(2)}, u32[]{:S(2)}) collective-permute-start(bf16[168,128]{1,0:T(8,128)(2,1)S(1)} %pad_maximum_fusion.5), channel_id=1, source_target_pairs={{0,2},{1,3},{2,0},{3,1},{4,8},{5,9},{6,10},{7,11},{8,4},{9,5},{10,... | collective-permute-start | bytes 129032 | tf_op jit(solution)/shard_map/ppermute | solution.py:363
